TPU v7x, 512 devices: a whole 4x4x16 slice. The times are simulated.
512 devices in a mesh: seq: 32 (over z, core), head: 16 (over y, x).
Axes of the slice: x: 4, y: 4, z: 16, core: 2. Of those that a mesh axis runs over, the one named last changes fastest.
Arguments:
- queries: bfloat16 [8192, 32, 128], P('seq', 'head'), may hold values from -6 to 6
- raw_keys: bfloat16 [8192, 128], P('seq'), may hold values from -24 to 24
- values: bfloat16 [8192, 32, 128], P('seq', 'head'), may hold values from -6 to 6
- cotangent: bfloat16 [8192, 32, 128], P('seq', 'head'), may hold values from -6 to 6
Outputs:
- output: bfloat16 [8192, 32, 128], P('seq', 'head')
- grad_queries: bfloat16 [8192, 32, 128], P('seq', 'head')
- grad_keys: bfloat16 [8192, 128], P('seq')
- grad_values: bfloat16 [8192, 32, 128], P('seq', 'head')
All inputs are finite; a program needn't handle non-finite values.
Results may differ from a plain program's by a relative error of at most 0.0038.
Values sent between devices are 32-bit elements; how exact they have to be, the bound alone decides.
No kernel may reach another device: no remote copies, remote signals or barrier semaphores. Data moves between devices by JAX's collectives and lax.ppermute only.
A program may use at most 64 MiB of HBM per device.

v0:
```python
import jax
import jax.numpy as jnp
from jax import lax
from jax.sharding import PartitionSpec as P

BLOCK = 128


HIGHEST = lax.Precision.HIGHEST


def prefix(array, axis, combine, identity, reverse):
    peers, place = (lax.axis_size(axis), lax.axis_index(axis))
    everything = jax.tree.map(lambda part: lax.all_gather(part, axis), array)
    start = jax.tree.map(
        lambda part, zero: jnp.broadcast_to(jnp.asarray(zero, part.dtype), part.shape),
        array,
        identity,
    )

    def hop(k, before):
        at = peers - 1 - k if reverse else k
        reached = at > place if reverse else at < place
        new = combine(before, jax.tree.map(lambda part: part[at], everything))
        return jax.tree.map(lambda a, b: jnp.where(reached, a, b), new, before)

    return lax.fori_loop(0, peers, hop, start)


def advance_block(carried, transition, block_query, block_key, block_value, places):
    block_len, head_count, key_width = block_query.shape
    value_width = block_value.shape[1] // head_count
    key_gram = jnp.dot(block_key, block_key.T, precision=HIGHEST)
    lower_mat = jnp.eye(block_len, dtype=jnp.float32) + 2.0 * jnp.tril(key_gram, -1)
    stacked = jnp.concatenate([block_key, 0.5 * block_value], axis=1)
    solved = lax.linalg.triangular_solve(
        lower_mat, stacked, left_side=True, lower=True, unit_diagonal=True
    )
    w_rows = solved[:, :key_width]
    u_rows = solved[:, key_width:] - jnp.dot(w_rows, carried, precision=HIGHEST)
    scores = jnp.tril(jnp.einsum("chk,tk->hct", block_query, block_key, precision=HIGHEST))
    result = jnp.einsum(
        "chk,khv->chv",
        block_query,
        carried.reshape(key_width, head_count, value_width),
        precision=HIGHEST,
    )
    result = result + 2.0 * jnp.einsum(
        "hct,thv->chv",
        scores,
        u_rows.reshape(block_len, head_count, value_width),
        precision=HIGHEST,
    )
    result = result / jnp.sqrt(places)[:, None, None]
    carried = carried + 2.0 * jnp.dot(block_key.T, u_rows, precision=HIGHEST)
    transition = transition - 2.0 * jnp.dot(
        block_key.T, jnp.dot(w_rows, transition, precision=HIGHEST), precision=HIGHEST
    )
    return (result, carried, transition)


def local_pass(query_in, unit_keys, value_in, places, start):
    tokens, head_count, key_width = query_in.shape
    value_width = value_in.shape[2]
    num_blocks = tokens // BLOCK
    inputs = (
        query_in.reshape(num_blocks, BLOCK, head_count, key_width),
        unit_keys.reshape(num_blocks, BLOCK, key_width),
        value_in.reshape(num_blocks, BLOCK, head_count * value_width),
        places.reshape(num_blocks, BLOCK),
    )

    def advance(carried_pair, block_in):
        result, carried, transition = advance_block(
            carried_pair[0], carried_pair[1], block_in[0], block_in[1], block_in[2], block_in[3]
        )
        return ((carried, transition), result)

    identity = jnp.eye(key_width, dtype=jnp.float32)
    (final_state, transition), results = lax.scan(advance, (start, identity), inputs)
    return (results.reshape(tokens, head_count, value_width), final_state, transition)


def compose(earlier, later):
    return (
        jnp.dot(later[0], earlier[0], precision=HIGHEST),
        jnp.dot(later[0], earlier[1], precision=HIGHEST) + later[1],
    )


def shards(queries, raw_keys, values, cotangent):
    tokens = raw_keys.shape[0]
    key_width = raw_keys.shape[1]
    head_count = queries.shape[1]
    value_width = values.shape[2]
    seq_index = lax.axis_index("seq")
    places = (seq_index * tokens + jnp.arange(tokens, dtype=jnp.int32) + 1).astype(jnp.float32)
    query_full = queries.astype(jnp.float32)
    key_full = raw_keys.astype(jnp.float32)
    key_norm = jnp.sqrt(jnp.sum(key_full * key_full, axis=-1, keepdims=True) + 1e-06)
    unit_keys = key_full / key_norm
    value_full = values.astype(jnp.float32)
    upstream = cotangent.astype(jnp.float32)
    empty_state = jnp.zeros((key_width, head_count * value_width), jnp.float32)

    def from_start(start):
        return local_pass(query_full, unit_keys, value_full, places, start)

    (first_result, block_end, transition), pull_first = jax.vjp(from_start, empty_state)
    (adjoint,) = pull_first((upstream, jnp.zeros_like(block_end), jnp.zeros_like(transition)))
    identity = (jnp.eye(key_width, dtype=jnp.float32), jnp.zeros_like(empty_state))
    start_state = prefix((transition, block_end), "seq", compose, identity, False)[1]
    incoming = prefix((transition.T, adjoint), "seq", compose, identity, True)[1]

    def with_start(query_in, key_in, value_in, start):
        result = local_pass(query_in, key_in, value_in, places, start)
        return (result[0], result[1])

    (output, final_state), pull_full = jax.vjp(
        with_start, query_full, unit_keys, value_full, start_state
    )
    grad_query, grad_unit, grad_value, start_grad = pull_full((upstream, incoming))
    unit_total = lax.psum(grad_unit, "head")
    along = jnp.sum(unit_total * unit_keys, axis=-1, keepdims=True)
    key_total = (unit_total - unit_keys * along) / key_norm
    return (
        output.astype(jnp.bfloat16),
        grad_query.astype(jnp.bfloat16),
        key_total.astype(jnp.bfloat16),
        grad_value.astype(jnp.bfloat16),
    )


def solution(mesh):
    placed = (
        P("seq", "head", None),
        P("seq", None),
        P("seq", "head", None),
        P("seq", "head", None),
    )
    return jax.shard_map(
        shards,
        mesh=mesh,
        in_specs=placed,
        out_specs=(
            P("seq", "head", None),
            P("seq", "head", None),
            P("seq", None),
            P("seq", "head", None),
        ),
        check_vma=False,
    )
```

profile of v0, /device:TPU:2, one launch (start us, length us, event | category | flops | bytes accessed | tf_op | source)
XLA Modules:
  0.0 539.3 jit_solution(12815148292353430432)
XLA Ops:
  11.8 25.3 %while.135 = (s32[]{:T(128)}, f32[128,256]{1,0:T(8,128)S(1)}, f32[128,128]{1,0:T(8,128)S(1)}, f32[2,128,128]{2,1,0:T(8,128)S(1)}, f32[2,2,128,128]{2,3,1,0:T(8,1...) while((s32[]{:T(128)}, f32[128,256]{1,0:T(8,128)S(1)}, ...), condition=%wide.region_2.4_spmd.clone.clone, body=%wide.region_1.3_spmd.clone.sunk.clone | while | flops 302481536 | bytes 2969764 | solution.py:80
  12.7 9.8 %custom-call.37 = f32[1,128,128]{1,2,0:T(8,128)S(1)} custom-call(f32[1,128,128]{2,1,0:T(8,128)S(1)} %fusion.459), custom_call_target="InvertDiagBlocksLowerTriangular" | custom-call | tf_op jit(solution)/shard_map/jvp()/while/body/eval_jaxpr/triangular_solve/custom-call.1 | solution.py:36
  25.4 9.8 %custom-call.37 = f32[1,128,128]{1,2,0:T(8,128)S(1)} custom-call(f32[1,128,128]{2,1,0:T(8,128)S(1)} %fusion.459), custom_call_target="InvertDiagBlocksLowerTriangular" | custom-call | tf_op jit(solution)/shard_map/jvp()/while/body/eval_jaxpr/triangular_solve/custom-call.1 | solution.py:36
  39.3 3.5 while.137
  45.2 70.8 %all-gather.13.cloned.1.call-done = f32[4096,128]{0,1:T(8,128)} async-done(((f32[128,128]{0,1:T(8,128)}), f32[4096,128]{0,1:T(8,128)}) %all-gather.13.cloned.1.call-update) | async-done | bytes 2097168 | tf_op jit(solution)/shard_map/all_gather | solution.py:14
  115.9 2.9 copy.51
  118.9 67.4 %all-gather.9.cloned.1.call-done = f32[4096,128]{1,0:T(8,128)} async-done(((f32[128,128]{1,0:T(8,128)}), f32[4096,128]{1,0:T(8,128)}) %all-gather.9.cloned.1.call-update) | async-done | bytes 2097168 | tf_op jit(solution)/shard_map/all_gather | solution.py:14
  186.3 73.7 %all-gather.11.cloned.1.call-done = f32[4096,256]{1,0:T(8,128)} async-done(((f32[128,256]{1,0:T(8,128)}), f32[4096,256]{1,0:T(8,128)}) %all-gather.11.cloned.1.call-update) | async-done | bytes 4194320 | tf_op jit(solution)/shard_map/all_gather | solution.py:14
  260.0 40.4 %while.136 = (s32[]{:T(128)}, f32[128,256]{1,0:T(8,128)S(1)}, s32[]{:T(128)}, f32[32,128,128]{2,1,0:T(8,128)}, f32[32,128,256]{2,1,0:T(8,128)}) while((s32[]{:T(128)}, f32[128,256]{1,0:T(8,128)S(1)}, s32[]{:T(128)}, f32[32,128,128]{2,1,0:T(8,128)}, f32[32,128,256]{2,1,0:T(8,128)}) %tuple.288), condition=%wide.region_4.6_spmd.clone.clone, body=%wide.region_3.5_spmd.clone.sunk.clone | while | flops 50462724 | bytes 854615 | solution.py:27
  275.2 1.2 fusion.467
  281.5 1.2 fusion.467
  282.8 1.2 fusion.467
  285.3 1.2 fusion.467
  286.6 1.2 fusion.467
  289.1 1.2 fusion.467
  291.6 1.2 fusion.467
  292.9 1.2 fusion.467
  294.1 1.2 fusion.467
  296.7 1.2 fusion.467
  303.1 32.8 %while.133 = (s32[]{:T(128)}, f32[128,256]{1,0:T(8,128)S(1)}, bf16[2,128,2,128]{3,1,2,0:T(8,128)(2,1)}, f32[2,128,128]{1,2,0:T(8,128)S(1)}, f32[2,128,128]{2,1,0...) while((s32[]{:T(128)}, f32[128,256]{1,0:T(8,128)S(1)}, ...), condition=%wide.region_6.8_spmd.clone.clone, body=%wide.region_5.7_spmd.clone.sunk.clone | while | flops 352813184 | bytes 5737269 | solution.py:80
  303.3 1.5 bitcast_dynamic-update-slice_fusion.27
  304.9 9.8 %custom-call.35 = f32[1,128,128]{1,2,0:T(8,128)S(1)} custom-call(f32[1,128,128]{2,1,0:T(8,128)S(1)} %add_bitcast_fusion.3), custom_call_target="InvertDiagBlocksLowerTriangular" | custom-call | tf_op jit(solution)/shard_map/jvp()/while/body/eval_jaxpr/triangular_solve/custom-call.1 | solution.py:36
  319.7 1.5 bitcast_dynamic-update-slice_fusion.27
  321.3 9.8 %custom-call.35 = f32[1,128,128]{1,2,0:T(8,128)S(1)} custom-call(f32[1,128,128]{2,1,0:T(8,128)S(1)} %add_bitcast_fusion.3), custom_call_target="InvertDiagBlocksLowerTriangular" | custom-call | tf_op jit(solution)/shard_map/jvp()/while/body/eval_jaxpr/triangular_solve/custom-call.1 | solution.py:36
  335.9 40.5 %while.138 = (s32[]{:T(128)}, f32[128,256]{1,0:T(8,128)S(1)}, s32[]{:T(128)}, f32[32,128,128]{2,1,0:T(8,128)}, f32[32,128,256]{2,1,0:T(8,128)}) while((s32[]{:T(128)}, f32[128,256]{1,0:T(8,128)S(1)}, s32[]{:T(128)}, f32[32,128,128]{2,1,0:T(8,128)}, f32[32,128,256]{2,1,0:T(8,128)}) %tuple.286), condition=%wide.region_10.12_spmd.clone.clone, body=%wide.region_9.11_spmd.clone.sunk.clone | while | flops 50462728 | bytes 854661 | solution.py:27
  337.2 1.2 fusion.482
  339.8 1.2 fusion.482
  342.3 1.2 fusion.482
  344.8 1.2 fusion.482
  347.4 1.2 fusion.482
  349.9 1.2 fusion.482
  352.4 1.2 fusion.482
  362.6 1.2 fusion.482
  365.1 1.2 fusion.482
  367.6 1.2 fusion.482
  370.2 1.2 fusion.482
  377.8 42.5 %while.134 = (s32[]{:T(128)}, f32[128,256]{1,0:T(8,128)S(1)}, bf16[2,128,2,128]{3,1,2,0:T(8,128)(2,1)}, f32[2,128,128]{2,1,0:T(8,128)}, bf16[2,128,256]{2,1,0:T(...) while((s32[]{:T(128)}, f32[128,256]{1,0:T(8,128)S(1)}, ...), condition=%wide.region_12.14_spmd.clone.clone.clone, body=%wide.region_11.13_spmd.clone.clone.sunk.clone | while | flops 730660992 | bytes 10445733 | solution.py:80
  379.4 1.4 fusion.435
  382.4 9.8 %custom-call.36 = f32[1,128,128]{1,2,0:T(8,128)S(1)} custom-call(f32[1,128,128]{2,1,0:T(8,128)S(1)} %convert_add_fusion.3), custom_call_target="InvertDiagBlocksLowerTriangular" | custom-call | tf_op jit(solution)/shard_map/transpose(jvp())/while/body/eval_jaxpr/triangular_solve | solution.py:36
  393.5 1.3 convolution_add_fusion.19
  400.7 1.4 fusion.435
  403.7 9.8 %custom-call.36 = f32[1,128,128]{1,2,0:T(8,128)S(1)} custom-call(f32[1,128,128]{2,1,0:T(8,128)S(1)} %convert_add_fusion.3), custom_call_target="InvertDiagBlocksLowerTriangular" | custom-call | tf_op jit(solution)/shard_map/transpose(jvp())/while/body/eval_jaxpr/triangular_solve | solution.py:36
  414.7 1.3 convolution_add_fusion.19
  420.4 1.7 copy.50
  422.1 1.7 copy.64
  423.8 1.6 convert_element_type.49
  425.4 104.6 %all-reduce.4.cloned.1.call-done = f32[256,128]{1,0:T(8,128)} async-done(((f32[256,128]{1,0:T(8,128)}), f32[256,128]{1,0:T(8,128)}) %all-reduce.4.cloned.1.call-update) | async-done | bytes 131088 | tf_op jit(solution)/shard_map/psum | solution.py:123
  531.1 1.7 divide_convert_fusion
  (328 shorter events, 102.7 us)
Async XLA Ops:
  7.2 108.8 %all-gather.13.cloned.1.call-start = ((), (), s32[]{:S(2)}) async-start(), calls=%async_computation.3 | async-start | bytes 2162688 | tf_op jit(solution)/shard_map/all_gather | solution.py:14
  8.7 3.0 copy-start.11
  11.7 27.5 %copy-start.10 = (bf16[256,2,128]{2,1,0:T(2,128)(2,1)S(1)}, bf16[256,2,128]{2,1,0:T(2,128)(2,1)}, u32[]{:S(2)}) copy-start(bf16[256,2,128]{2,1,0:T(2,128)(2,1)} %param.21) | copy-start | bytes 393220
  37.1 0.6 copy-start.2
  37.1 1.4 copy-start
  37.1 2.2 copy-start.13
  37.7 148.5 %all-gather.9.cloned.1.call-start = ((), (), s32[]{:S(2)}) async-start(), calls=%async_computation.1 | async-start | bytes 2162688 | tf_op jit(solution)/shard_map/all_gather | solution.py:14
  38.5 221.5 %all-gather.11.cloned.1.call-start = ((), (), s32[]{:S(2)}) async-start(), calls=%async_computation.2 | async-start | bytes 4325376 | tf_op jit(solution)/shard_map/all_gather | solution.py:14
  39.2 296.7 %all-gather.15.cloned.1.call-start = ((), (), s32[]{:S(2)}) async-start(), calls=%async_computation.4 | async-start | bytes 4325376 | tf_op jit(solution)/shard_map/all_gather | solution.py:14
  42.8 0.7 copy-start.1
  43.5 486.5 %all-reduce.4.cloned.1.call-start = ((), (), s32[]{:S(2)}) async-start(), calls=%async_computation | async-start | bytes 262144 | tf_op jit(solution)/shard_map/psum | solution.py:123
  316.8 2.1 copy-start.14
  316.8 2.1 copy-start.15
  318.9 0.6 copy-start.16
  333.2 2.1 copy-start.14
  333.2 2.1 copy-start.15
  335.4 0.6 copy-start.16
  335.9 41.9 %copy-start.17 = (f32[2,128,1,1]{1,3,2,0:T(1,128)S(1)}, f32[2,128,1,1]{1,3,2,0:T(1,128)}, u32[]{:S(2)}) copy-start(f32[2,128,1,1]{1,3,2,0:T(1,128)} %get-tuple-element.2555) | copy-start | bytes 3076
  377.8 152.2 %copy-start.5 = (bf16[256,128]{1,0:T(8,128)(2,1)S(1)}, bf16[256,128]{1,0:T(8,128)(2,1)}, u32[]{:S(2)}) copy-start(bf16[256,128]{1,0:T(8,128)(2,1)} %param.19) | copy-start | bytes 196612
  377.8 152.2 %copy-start.12 = (f32[256]{0:T(256)S(1)}, f32[256]{0:T(256)}, u32[]{:S(2)}) copy-start(f32[256]{0:T(256)} %copy-done.11) | copy-start | bytes 3076
  377.8 14.7 %copy-start.3 = (f32[2,128,128]{2,1,0:T(8,128)}, f32[2,128,128]{2,1,0:T(8,128)S(1)}, u32[]{:S(2)}) copy-start(f32[2,128,128]{2,1,0:T(8,128)S(1)} %get-tuple-element.2597) | copy-start | bytes 393220 | tf_op jit(solution)/shard_map/transpose(jvp())/while
  393.4 4.0 copy-start.8
  393.4 4.4 copy-start.6
  393.5 5.6 %copy-start.4 = (f32[2,128,128]{2,1,0:T(8,128)S(1)}, f32[2,128,128]{2,1,0:T(8,128)}, u32[]{:S(2)}) copy-start(f32[2,128,128]{2,1,0:T(8,128)} %copy-done.3) | copy-start | bytes 393220 | tf_op jit(solution)/shard_map/transpose(jvp())/while
  397.8 0.7 copy-start.9
  398.4 0.7 copy-start.7
  399.1 14.7 %copy-start.3 = (f32[2,128,128]{2,1,0:T(8,128)}, f32[2,128,128]{2,1,0:T(8,128)S(1)}, u32[]{:S(2)}) copy-start(f32[2,128,128]{2,1,0:T(8,128)S(1)} %get-tuple-element.2597) | copy-start | bytes 393220 | tf_op jit(solution)/shard_map/transpose(jvp())/while
  414.7 4.1 copy-start.8
  414.7 4.4 copy-start.6
  414.7 5.6 %copy-start.4 = (f32[2,128,128]{2,1,0:T(8,128)S(1)}, f32[2,128,128]{2,1,0:T(8,128)}, u32[]{:S(2)}) copy-start(f32[2,128,128]{2,1,0:T(8,128)} %copy-done.3) | copy-start | bytes 393220 | tf_op jit(solution)/shard_map/transpose(jvp())/while
  419.1 0.7 copy-start.9
  419.7 0.7 copy-start.7
Sparse Core Ops, SparseCore 0:
  37.9 78.0 all-gather.12
  118.6 67.6 all-gather.8
  189.0 70.9 all-gather.10
  262.6 71.2 all-gather.14
  420.5 109.4 all-reduce.3
where the time goes:
time: 541 us; the launch traced here: 539 us
  waiting for transfers between devices  318 us (59%)
  matrix products  113 us (21%)
  other arithmetic  66.9 us (12%)
  local copies, waits for them, and re-layouts  23.3 us (4%)
  between operations  14.1 us (3%)
    all_gather x4, waiting for transfers between devices, prefix(): everything = jax.tree.map(lambda part: lax.all_gather(part, axis), array)  212 us
    psum x1, waiting for transfers between devices, shards(): unit_total = lax.psum(grad_unit, 'head')  105 us
    dot_general x64, matrix products, compose(): jnp.dot(later[0], earlier[1], precision=HIGHEST) + later[1]  77.6 us
    another operation x16, other arithmetic, advance_block(): lax.linalg.triangular_solve(lower_mat, stacked, left_side=True, lower=Tru...  60.9 us
  transfers between devices with their start and end apart: 5, of which 4 were waited for; matrix products, arithmetic and copies ran while one was open for 16% of the time, Pallas kernels for 0%

commit v1 on v0

v1 whole, which is shorter than its diff:
```python
import functools

import jax
import jax.numpy as jnp
from jax import lax
from jax.experimental import pallas as pl
from jax.experimental.pallas import tpu as pltpu
from jax.sharding import PartitionSpec as P

T = 256
D = 128
F32 = jnp.float32
BF16 = jnp.bfloat16
VMEM_LIMIT = 48 * 1024 * 1024


def split(x):
    high = x.astype(BF16)
    return high, (x - high.astype(F32)).astype(BF16)


def exact(x):
    return x, None


def mm(a, b, over=(1, 0)):
    ca, cb = over
    terms = [(a[0], b[0])]
    if b[1] is not None:
        terms.append((a[0], b[1]))
    if a[1] is not None:
        terms.append((a[1], b[0]))
    left = jnp.concatenate([t[0] for t in terms], axis=ca)
    right = jnp.concatenate([t[1] for t in terms], axis=cb)
    return lax.dot_general(left, right, (((ca,), (cb,)), ((), ())), preferred_element_type=F32)


def iota(shape, dim):
    return lax.broadcasted_iota(jnp.int32, shape, dim)


def inverse(lower, size):
    row, col = iota((size, size), 0), iota((size, size), 1)
    level = row ^ col
    inv = jnp.where(row == col, 1.0, jnp.where((level == 1), -lower, 0.0))
    step = 2
    while step < size:
        part = jnp.where((level >= step) & (level < 2 * step), lower, 0.0)
        inv_pair = split(inv)
        inv = inv - mm(inv_pair, split(mm(split(part), inv_pair)))
        step *= 2
    return inv


def places_root(index):
    places = (index * T + iota((T, 1), 0) + 1).astype(F32)
    return 1.0 / jnp.sqrt(places)


def before_kernel(index_ref, raw_ref, q_ref, v_ref, d_ref, send_ref, k_ref, norm_ref, w_ref, m_ref, x_ref, z_ref,
                  qhat_ref, local_ref, qs_ref, vs_ref, ds_ref):
    qs_ref[...] = q_ref[...].astype(F32)
    vs_ref[...] = v_ref[...].astype(F32)
    ds_ref[...] = d_ref[...].astype(F32)
    rows = [pl.ds(head, T, stride=2) for head in range(2)]
    raw = raw_ref[...].astype(F32)
    norm = 1.0 / jnp.sqrt(jnp.sum(raw * raw, axis=1, keepdims=True) + 1e-06)
    key = raw * norm
    k_ref[...] = key
    norm_ref[...] = jnp.broadcast_to(norm, (T, D))
    root = places_root(index_ref[0])
    keys = split(key)
    gram = mm(keys, keys, (1, 1))
    row, col = iota((T, T), 0), iota((T, T), 1)
    lower = jnp.where(row > col, 2.0 * gram, 0.0)
    half = T // 2
    first = inverse(lower[:half, :half], half)
    second = inverse(lower[half:, half:], half)
    corner = -mm(split(second), split(mm(split(lower[half:, :half]), split(first))))
    inv = jnp.concatenate(
        [
            jnp.concatenate([first, jnp.zeros((half, half), F32)], axis=1),
            jnp.concatenate([corner, second], axis=1),
        ],
        axis=0,
    )
    invs = split(inv)
    w = 2.0 * mm(invs, keys)
    w_ref[...] = w
    ws = split(w)
    keys_t = split(key.T)
    eye = jnp.where(iota((D, D), 0) == iota((D, D), 1), 1.0, 0.0)
    send_ref[:, :D] = eye - mm(keys_t, ws)
    value = jnp.concatenate([vs_ref[r, :] for r in rows], axis=1).astype(BF16)
    x0 = mm(invs, exact(value))
    x_ref[...] = x0
    x0s = split(x0)
    send_ref[:, D : 3 * D] = mm(keys_t, x0s)
    inv_t = split(inv.T)
    m_ref[...] = mm(inv_t, keys)
    back = []
    for head in range(2):
        query = qs_ref[rows[head], :]
        grad = exact(ds_ref[rows[head], :].astype(BF16))
        score = jnp.where(row >= col, mm(exact(query.astype(BF16)), keys, (1, 1)), 0.0) * root
        scores = split(score)
        qhat = query * root - mm(scores, ws)
        qhat_ref[head] = qhat
        send_ref[:, (3 + head) * D : (4 + head) * D] = mm(split(qhat.T), grad)
        local_ref[head] = mm(scores, tuple(x[:, head * D : (head + 1) * D] for x in x0s))
        back.append(mm(split(score.T), grad))
    z_ref[...] = mm(inv_t, split(jnp.concatenate(back, axis=1)))


def pair_kernel(index_ref, got_ref, send_ref):
    core = index_ref[0] % 2
    at_b = pl.ds(pl.multiple_of(D + core * D, D), D)
    at_g = pl.ds(pl.multiple_of(3 * D + core * D, D), D)
    low, up = got_ref[0, :, :D], got_ref[1, :, :D]
    ahead = mm(split(up), split(jnp.concatenate([low, got_ref[0, :, at_b]], axis=1)))
    send_ref[:, :D] = ahead[:, :D]
    send_ref[:, D : 2 * D] = ahead[:, D:] + got_ref[1, :, at_b]
    send_ref[:, 2 * D :] = got_ref[0, :, at_g] + mm(split(low.T), split(got_ref[1, :, at_g]))


def level_kernel(first, last, bit, index_ref, got_ref, *refs):
    if first:
        send_ref, track_ref = refs
    else:
        old_ref, send_ref, track_ref = refs
    upper = (index_ref[0] // bit) % 2 == 1
    low, up = got_ref[0, :, :D], got_ref[1, :, :D]
    b_low, b_up = got_ref[0, :, D : 2 * D], got_ref[1, :, D : 2 * D]
    g_low, g_up = got_ref[0, :, 2 * D :], got_ref[1, :, 2 * D :]
    if last:
        top = (index_ref[0] // (2 * bit)) % 2 == 1
        step = mm(split(jnp.where(top, low.T, up)), split(jnp.where(top, g_up, b_low)))
        send_ref[...] = jnp.where(top, g_low, b_up) + step
    else:
        ahead = mm(split(up), split(jnp.concatenate([low, b_low], axis=1)))
        send_ref[:, :D] = ahead[:, :D]
        send_ref[:, D : 2 * D] = ahead[:, D:] + b_up
        send_ref[:, 2 * D :] = g_low + mm(split(low.T), split(g_up))
    other = jnp.where(upper, jnp.concatenate([low, b_low], axis=1), jnp.concatenate([up.T, g_up], axis=1))
    if first:
        eye = jnp.where(iota((D, D), 0) == iota((D, D), 1), 1.0, 0.0)
        blank = jnp.concatenate([eye, jnp.zeros((D, D), F32)], axis=1)
        track_ref[0] = jnp.where(upper, other, blank)
        track_ref[1] = jnp.where(upper, blank, other)
    else:
        mine = jnp.where(upper, old_ref[0], old_ref[1])
        new = mm(split(mine[:, :D]), split(other))
        new = jnp.concatenate([new[:, :D], new[:, D:] + mine[:, D:]], axis=1)
        track_ref[0] = jnp.where(upper, new, old_ref[0])
        track_ref[1] = jnp.where(upper, old_ref[1], new)


def top_kernel(bit, index_ref, got_ref, track_ref, send_ref):
    upper = (index_ref[0] // bit) % 2 == 1
    lead = jnp.where(upper, track_ref[0, :, :D], track_ref[1, :, :D])
    step = mm(split(lead), split(jnp.where(upper, got_ref[0], got_ref[1])))
    send_ref[:, :D] = track_ref[0, :, D:] + jnp.where(upper, step, 0.0)
    send_ref[:, D:] = track_ref[1, :, D:] + jnp.where(upper, 0.0, step)


def after_kernel(index_ref, pair_ref, got_ref, q_ref, d_ref, k_ref, w_ref, m_ref, x_ref, z_ref, qhat_ref, local_ref,
                 out_ref, gq_ref, gv_ref, gk_ref, qs_ref, ds_ref, os_ref, gs_ref, zs_ref):
    qs_ref[...] = q_ref[...].astype(F32)
    ds_ref[...] = d_ref[...].astype(F32)
    rows = [pl.ds(head, T, stride=2) for head in range(2)]
    upper = index_ref[0] % 2 == 1
    state = jnp.concatenate([got_ref[0, :, :D], got_ref[1, :, :D]], axis=1)
    adjoint = jnp.concatenate([got_ref[0, :, D:], got_ref[1, :, D:]], axis=1)
    step = mm(
        split(jnp.where(upper, pair_ref[0, :, :D], pair_ref[1, :, :D].T)),
        split(jnp.where(upper, state, adjoint)),
    )
    state = jnp.where(upper, step + pair_ref[0, :, D : 3 * D], state)
    adjoint = jnp.where(upper, adjoint, step + pair_ref[1, :, 3 * D :])
    states, adjoints = split(state), split(adjoint)
    root = places_root(index_ref[0])
    keys = split(k_ref[...])
    row, col = iota((T, T), 0), iota((T, T), 1)
    x = x_ref[...] - mm(split(w_ref[...]), states)
    xs = split(x)
    z = z_ref[...] + mm(split(m_ref[...]), adjoints)
    zs = split(z)
    edge = jnp.where(row > col, mm(zs, xs, (1, 1)), 0.0)
    gk = mm(xs, adjoints, (1, 1)) - 2.0 * mm(zs, states, (1, 1)) - 2.0 * mm(split(edge + edge.T), keys)
    for head in range(2):
        part = slice(head * D, (head + 1) * D)
        head_states = tuple(s[:, part] for s in states)
        query = exact(qs_ref[rows[head], :].astype(BF16))
        grad = exact(ds_ref[rows[head], :].astype(BF16))
        os_ref[rows[head], :] = local_ref[head] + mm(split(qhat_ref[head]), head_states)
        mix = jnp.where(row >= col, mm(grad, tuple(s[:, part] for s in xs), (1, 1)), 0.0) * root
        gs_ref[rows[head], :] = root * mm(grad, head_states, (1, 1)) + mm(split(mix), keys)
        gk = gk + mm(split(mix.T), query)
        zs_ref[rows[head], :] = z[:, part]
    gk_ref[...] = gk
    out_ref[...] = os_ref[...].astype(BF16)
    gq_ref[...] = gs_ref[...].astype(BF16)
    gv_ref[...] = zs_ref[...].astype(BF16)


def sum_kernel(got_ref, out_ref):
    out_ref[...] = jnp.broadcast_to(jnp.sum(got_ref[...], axis=0, keepdims=True), out_ref.shape)


def key_kernel(got_ref, k_ref, norm_ref, out_ref):
    total, key = got_ref[...], k_ref[...]
    along = jnp.sum(total * key, axis=1, keepdims=True)
    out_ref[...] = ((total - key * along) * norm_ref[...]).astype(BF16)


def call(kernel, outs, *operands, scratch=(), scalars=1):
    memory = [pl.BlockSpec(memory_space=pltpu.SMEM)] * scalars
    memory += [pl.BlockSpec(memory_space=pltpu.VMEM)] * (len(operands) - scalars)
    single = not isinstance(outs, list)
    shapes = [outs] if single else outs
    result = pl.pallas_call(
        kernel,
        out_shape=[jax.ShapeDtypeStruct(*s) for s in shapes],
        in_specs=memory,
        out_specs=[pl.BlockSpec(memory_space=pltpu.VMEM)] * len(shapes),
        scratch_shapes=list(scratch),
        compiler_params=pltpu.CompilerParams(vmem_limit_bytes=VMEM_LIMIT),
    )(*operands)
    return result[0] if single else result


def exchange(x, bit):
    size = lax.axis_size("seq")
    groups = [[i, i + bit] for i in range(size) if (i // bit) % 2 == 0]
    return lax.all_gather(x, "seq", axis_index_groups=groups)


def shards(queries, raw_keys, values, cotangent):
    index = lax.axis_index("seq").astype(jnp.int32).reshape(1)
    q = queries.reshape(2 * T, D)
    v = values.reshape(2 * T, D)
    d = cotangent.reshape(2 * T, D)
    wide = pltpu.VMEM((2 * T, D), F32)
    send, key, norm, w, m, x0, z0, qhat, local = call(
        before_kernel,
        [
            ((D, 5 * D), F32),
            ((T, D), F32),
            ((T, D), F32),
            ((T, D), F32),
            ((T, D), F32),
            ((T, 2 * D), F32),
            ((T, 2 * D), F32),
            ((2, T, D), F32),
            ((2, T, D), F32),
        ],
        index, raw_keys, q, v, d,
        scratch=[wide] * 3,
    )
    pair = exchange(send, 1)
    send = call(pair_kernel, ((D, 3 * D), F32), index, pair)
    size = lax.axis_size("seq")
    bit = 2
    track = None
    while bit < size // 2:
        got = exchange(send, bit)
        last = bit == size // 4
        send, track = call(
            functools.partial(level_kernel, track is None, last, bit),
            [((D, D if last else 3 * D), F32), ((2, D, 2 * D), F32)],
            index, got, *([] if track is None else [track]),
        )
        bit *= 2
    send = call(functools.partial(top_kernel, bit), ((D, 2 * D), F32), index, exchange(send, bit), track)
    got = exchange(send, 1)
    out, gq, gv, gk = call(
        after_kernel,
        [((2 * T, D), BF16), ((2 * T, D), BF16), ((2 * T, D), BF16), ((T, D), F32)],
        index, pair, got, q, d, key, w, m, x0, z0, qhat, local,
        scratch=[wide] * 5,
    )
    peers = lax.axis_size("head")
    pieces = lax.all_to_all(gk.reshape(peers, T // peers, D), "head", 0, 0)
    totals = call(sum_kernel, ((peers, T // peers, D), F32), pieces, scalars=0)
    total = lax.all_to_all(totals, "head", 0, 0).reshape(T, D)
    gkey = call(key_kernel, ((T, D), BF16), total, key, norm, scalars=0)
    shape = queries.shape
    return out.reshape(shape), gq.reshape(shape), gkey, gv.reshape(shape)


def solution(mesh):
    split_both = P("seq", "head", None)
    keys_only = P("seq", None)
    return jax.shard_map(
        shards,
        mesh=mesh,
        in_specs=(split_both, keys_only, split_both, split_both),
        out_specs=(split_both, split_both, keys_only, split_both),
        check_vma=False,
    )
```

time: 541 us -> 106 us (0.20)
  waiting for transfers between devices: 318 us -> 0 us
  matrix products: 113 us -> 0 us
  blocking collectives: 0 us -> 90.3 us
  other arithmetic: 66.9 us -> 0 us
  local copies, waits for them, and re-layouts: 23.3 us -> 3.56 us
  between operations: 14.1 us -> 0.72 us
  Pallas kernels: 0 us -> 11.4 us
    all_gather x4 -> x0, waiting for transfers between devices: 212 us -> none  [prefix(): everything = jax.tree.map(lambda part: lax.all_gather(part, axis), array)]
    dot_general x122 -> x0, matrix products: 109 us -> none  [the longest x64 77.6 us: compose(): jnp.dot(later[0], earlier[1], precision=HIGHEST) + later[1]]
    psum x1 -> x0, waiting for transfers between devices: 105 us -> none  [shards(): unit_total = lax.psum(grad_unit, 'head')]
    all_gather x0 -> x6, blocking collectives: none -> 65.4 us  [exchange(): return lax.all_gather(x, 'seq', axis_index_groups=groups)]
    another operation x19 -> x0, other arithmetic: 60.9 us -> none  [the longest x16 60.9 us: advance_block(): lax.linalg.triangular_solve(lower_mat, stacked, left_side=True, lower=Tru...]
    all_to_all x0 -> x2, blocking collectives: none -> 24.9 us  [the longest x1 13.9 us: shards(): pieces = lax.all_to_all(gk.reshape(peers, T // peers, D), 'head', 0, 0)]
    pallas_call x0 -> x9, Pallas kernels: none -> 11.4 us  [call(): pl.pallas_call(kernel, out_shape=[jax.ShapeDtypeStruct(*s) for s in shape...]
  transfers between devices with their start and end apart: 5 -> 0, of which waited for: 4 -> 0; matrix products, arithmetic and copies ran while one was open for 16% -> 0% of each run, Pallas kernels for 0% -> 0%
where the time goes in v1:
time: 106 us
  blocking collectives  90.3 us (85%)
  Pallas kernels  11.4 us (11%)
  local copies, waits for them, and re-layouts  3.56 us (3%)
    all_gather x6, blocking collectives, exchange(): return lax.all_gather(x, 'seq', axis_index_groups=groups)  65.4 us
    all_to_all x1, blocking collectives, shards(): pieces = lax.all_to_all(gk.reshape(peers, T // peers, D), 'head', 0, 0)  13.9 us
    pallas_call x9, Pallas kernels, call(): pl.pallas_call(kernel, out_shape=[jax.ShapeDtypeStruct(*s) for s in shape...  11.4 us
    all_to_all x1, blocking collectives, shards(): total = lax.all_to_all(totals, 'head', 0, 0).reshape(T, D)  11.1 us
    unnamed x12, local copies, waits for them, and re-layouts  3.56 us

profile of v1, /device:TPU:2, one launch (start us, length us, event | category | flops | bytes accessed | tf_op | source)
XLA Modules:
  0.0 106.0 jit_solution(6957897253560132258)
XLA Ops:
  0.6 0.0 copy-start
  0.6 0.9 copy-done
  1.5 0.0 copy-start.2
  1.5 0.9 copy-done.2
  2.4 0.0 copy-start.4
  2.5 0.9 copy-done.4
  3.4 0.0 copy-start.5
  3.4 0.8 copy-done.5
  4.2 6.7 %shard_map.75 = (f32[128,640]{1,0:T(8,128)S(1)}, f32[256,128]{1,0:T(8,128)S(1)}, f32[256,128]{1,0:T(8,128)S(1)}, f32[256,128]{1,0:T(8,128)S(1)}, f32[256,128]{1,...) custom-call(s32[1]{0:T(128)} %bitcast.index_ref, ...), custom_call_target="tpu_custom_call" | custom-call | tf_op jit(solution)/shard_map/pallas_call | solution.py:221
  10.9 2.3 %all-gather = f32[256,640]{1,0:T(8,128)S(1)} all-gather(f32[128,640]{1,0:T(8,128)S(1)} %get-tuple-element.23), channel_id=2, replica_groups={{0,16},{32,48},{64,80},{96,112},{128,144},{160,176},{192,208},{224,240}..., dimensions={0}, use_global_device_ids=true | all-gather | bytes 983040 | tf_op jit(solution)/shard_map/all_gather | solution.py:235
  13.2 0.2 shard_map.76
  13.4 7.8 %all-gather.1 = f32[256,384]{1,0:T(8,128)S(1)} all-gather(f32[128,384]{1,0:T(8,128)S(1)} %shard_map.76), channel_id=3, replica_groups={{0,32},{16,48},{64,96},{80,112},{128,160},{144,176},{192,224},{208,240}..., dimensions={0}, use_global_device_ids=true | all-gather | bytes 589824 | tf_op jit(solution)/shard_map/all_gather | solution.py:235
  21.2 0.2 shard_map.77
  21.5 12.7 %all-gather.2 = f32[256,384]{1,0:T(8,128)S(1)} all-gather(f32[128,384]{1,0:T(8,128)S(1)} %get-tuple-element.24), channel_id=4, replica_groups={{0,64},{16,80},{32,96},{48,112},{128,192},{144,208},{160,224},{176,240}..., dimensions={0}, use_global_device_ids=true | all-gather | bytes 589824 | tf_op jit(solution)/shard_map/all_gather | solution.py:235
  34.2 0.3 shard_map.78
  34.5 23.5 %all-gather.3 = f32[256,384]{1,0:T(8,128)S(1)} all-gather(f32[128,384]{1,0:T(8,128)S(1)} %get-tuple-element.26), channel_id=5, replica_groups={{0,128},{16,144},{32,160},{48,176},{64,192},{80,208},{96,224},{112,240}..., dimensions={0}, use_global_device_ids=true | all-gather | bytes 589824 | tf_op jit(solution)/shard_map/all_gather | solution.py:235
  58.0 0.3 shard_map.79
  58.3 17.0 %all-gather.4 = f32[256,128]{1,0:T(8,128)S(1)} all-gather(f32[128,128]{1,0:T(8,128)S(1)} %get-tuple-element.28), channel_id=6, replica_groups={{0,256},{16,272},{32,288},{48,304},{64,320},{80,336},{96,352},{112,368}..., dimensions={0}, use_global_device_ids=true | all-gather | bytes 196608 | tf_op jit(solution)/shard_map/all_gather | solution.py:235
  75.3 0.2 shard_map.80
  75.4 0.0 copy-start.1
  75.5 0.0 copy-start.3
  75.5 2.1 %all-gather.5 = f32[256,256]{1,0:T(8,128)S(1)} all-gather(f32[128,256]{1,0:T(8,128)S(1)} %shard_map.80), channel_id=7, replica_groups={{0,16},{32,48},{64,80},{96,112},{128,144},{160,176},{192,208},{224,240}..., dimensions={0}, use_global_device_ids=true | all-gather | bytes 393216 | tf_op jit(solution)/shard_map/all_gather | solution.py:235
  77.6 0.0 copy-done.1
  77.6 0.0 copy-done.3
  77.6 2.6 %shard_map.81 = (bf16[512,128]{1,0:T(8,128)(2,1)}, bf16[512,128]{1,0:T(8,128)(2,1)}, bf16[512,128]{1,0:T(8,128)(2,1)}, f32[256,128]{1,0:T(8,128)S(1)}) custom-call(s32[1]{0:T(128)} %bitcast.index_ref, f32[2,128,640]{2,1,0:T(8,128)S(1)} %bitcast.16, f32[2,128,256]{2,1,0:T(8,128)S(1)} %bitcast.20, bf16[512,128]{1,0:T(8,128)(2,1)S(1)} %bitcast.24, ...), custom_call_target="tpu_custom_call" | custom-call | tf_op jit(solution)/shard_map/pallas_call | solution.py:221
  80.2 13.9 %all_to_all.10.got_ref = f32[16,16,128]{2,1,0:T(8,128)S(1)} all-to-all(f32[16,16,128]{2,1,0:T(8,128)S(1)} %bitcast.27), channel_id=1, replica_groups=mesh['seq'=32,'head'=16] {'head'}, dimensions={0} | all-to-all | bytes 262144 | tf_op jit(solution)/shard_map/all_to_all | solution.py:283
  94.2 11.1 %all_to_all.11 = f32[16,16,128]{2,1,0:T(8,128)S(1)} all-to-all(f32[16,16,128]{2,1,0:T(8,128)S(1)} %shard_map.82), channel_id=1, replica_groups=mesh['seq'=32,'head'=16] {'head'}, dimensions={0} | all-to-all | bytes 262144 | tf_op jit(solution)/shard_map/all_to_all | solution.py:285
  105.2 0.7 shard_map.83
  (1 shorter events, 0.0 us)
Async XLA Ops:
  0.6 0.9 copy-start
  1.5 0.9 copy-start.2
  2.4 0.9 copy-start.4
  3.4 0.8 copy-start.5
  75.4 2.2 %copy-start.1 = (bf16[256,2,128]{2,1,0:T(2,128)(2,1)S(1)}, bf16[256,2,128]{2,1,0:T(2,128)(2,1)}, u32[]{:S(2)}) copy-start(bf16[256,2,128]{2,1,0:T(2,128)(2,1)} %param.4) | copy-start | bytes 393220
  75.5 2.1 %copy-start.3 = (bf16[256,2,128]{2,1,0:T(2,128)(2,1)S(1)}, bf16[256,2,128]{2,1,0:T(2,128)(2,1)}, u32[]{:S(2)}) copy-start(bf16[256,2,128]{2,1,0:T(2,128)(2,1)} %param.7) | copy-start | bytes 393220

commit v2 on v1

v2 whole, which is shorter than its diff:
```python
import functools

import jax
import jax.numpy as jnp
from jax import lax
from jax.experimental import pallas as pl
from jax.experimental.pallas import tpu as pltpu
from jax.sharding import PartitionSpec as P

T = 256
D = 128
C = D // 2
F32 = jnp.float32
BF16 = jnp.bfloat16
VMEM_LIMIT = 48 * 1024 * 1024
LONG = pl.CostEstimate(flops=4000000000, bytes_accessed=4000000, transcendentals=0)


def split(x):
    high = x.astype(BF16)
    return high, (x - high.astype(F32)).astype(BF16)


def exact(x):
    return x, None


def mm(a, b, over=(1, 0)):
    ca, cb = over
    terms = [(a[0], b[0])]
    if b[1] is not None:
        terms.append((a[0], b[1]))
    if a[1] is not None:
        terms.append((a[1], b[0]))
    left = jnp.concatenate([t[0] for t in terms], axis=ca)
    right = jnp.concatenate([t[1] for t in terms], axis=cb)
    return lax.dot_general(left, right, (((ca,), (cb,)), ((), ())), preferred_element_type=F32)


def iota(shape, dim):
    return lax.broadcasted_iota(jnp.int32, shape, dim)


def inverse(lower, size):
    row, col = iota((size, size), 0), iota((size, size), 1)
    level = row ^ col
    inv = jnp.where(row == col, 1.0, jnp.where((level == 1), -lower, 0.0))
    step = 2
    while step < size:
        part = jnp.where((level >= step) & (level < 2 * step), lower, 0.0)
        inv_pair = split(inv)
        inv = inv - mm(inv_pair, split(mm(split(part), inv_pair)))
        step *= 2
    return inv


def places_root(index):
    places = (index * T + iota((T, 1), 0) + 1).astype(F32)
    return 1.0 / jnp.sqrt(places)


def keys_kernel(raw_ref, k_ref, norm_ref, inv_ref):
    raw = raw_ref[...].astype(F32)
    norm = 1.0 / jnp.sqrt(jnp.sum(raw * raw, axis=1, keepdims=True) + 1e-06)
    key = raw * norm
    k_ref[...] = key
    norm_ref[...] = jnp.broadcast_to(norm, (T, D))
    keys = split(key)
    gram = mm(keys, keys, (1, 1))
    row, col = iota((T, T), 0), iota((T, T), 1)
    lower = jnp.where(row > col, 2.0 * gram, 0.0)
    half = T // 2
    first = inverse(lower[:half, :half], half)
    second = inverse(lower[half:, half:], half)
    corner = -mm(split(second), split(mm(split(lower[half:, :half]), split(first))))
    inv_ref[:half, :half] = first
    inv_ref[:half, half:] = jnp.zeros((half, half), F32)
    inv_ref[half:, :half] = corner
    inv_ref[half:, half:] = second


def before_kernel(index_ref, k_ref, inv_ref, q_ref, v_ref, d_ref, send_ref, w_ref, m_ref, x_ref, z_ref,
                  qs_ref, vs_ref, ds_ref):
    qs_ref[...] = q_ref[...].astype(F32)
    vs_ref[...] = v_ref[...].astype(F32)
    ds_ref[...] = d_ref[...].astype(F32)
    rows = [pl.ds(head, T, stride=2) for head in range(2)]
    root = places_root(index_ref[0])
    row, col = iota((T, T), 0), iota((T, T), 1)
    key, inv = k_ref[...], inv_ref[...]
    keys, invs = split(key), split(inv)
    w = 2.0 * mm(invs, keys)
    w_ref[...] = w
    ws = split(w)
    keys_t = split(key.T)
    eye = jnp.where(iota((D, D), 0) == iota((D, D), 1), 1.0, 0.0)
    send_ref[:, :D] = eye - mm(keys_t, ws)
    value = jnp.concatenate([vs_ref[r, :] for r in rows], axis=1).astype(BF16)
    x0 = mm(invs, exact(value))
    x_ref[...] = x0
    send_ref[:, D : 3 * D] = mm(keys_t, split(x0))
    inv_t = split(inv.T)
    m_ref[...] = mm(inv_t, keys)
    back = []
    for head in range(2):
        query = qs_ref[rows[head], :]
        grad = exact(ds_ref[rows[head], :].astype(BF16))
        score = jnp.where(row >= col, mm(exact(query.astype(BF16)), keys, (1, 1)), 0.0) * root
        qhat = query * root - mm(split(score), ws)
        send_ref[:, (3 + head) * D : (4 + head) * D] = mm(split(qhat.T), grad)
        back.append(mm(split(score.T), grad))
    z_ref[...] = mm(inv_t, split(jnp.concatenate(back, axis=1)))


def pair_kernel(index_ref, got_ref, send_ref):
    core = index_ref[0] % 2
    at_b = pl.ds(pl.multiple_of(D + core * D, D), D)
    at_g = pl.ds(pl.multiple_of(3 * D + core * D, D), D)
    low, up = got_ref[0, :, :D], got_ref[1, :, :D]
    ahead = mm(split(up), split(jnp.concatenate([low, got_ref[0, :, at_b]], axis=1)))
    send_ref[:, :D] = ahead[:, :D]
    send_ref[:, D : 2 * D] = ahead[:, D:] + got_ref[1, :, at_b]
    send_ref[:, 2 * D :] = got_ref[0, :, at_g] + mm(split(low.T), split(got_ref[1, :, at_g]))


def chip_kernel(index_ref, got_ref, send_ref):
    right = (index_ref[0] // 2) % 2 == 1
    low, up = got_ref[0, :, :D], got_ref[1, :, :D]
    b_low, b_up, g_low, g_up = pick(got_ref, right)
    ahead = mm(split(up), split(jnp.concatenate([low, b_low], axis=1)))
    send_ref[:, :D] = ahead[:, :D]
    send_ref[:, D:] = jnp.concatenate(
        [ahead[:, D:] + b_up, g_low + mm(split(low.T), split(g_up))], axis=1
    )


def pick(got_ref, right):
    return [
        jnp.where(right, half[:, C:], half[:, :C])
        for half in (
            got_ref[0, :, D : 2 * D], got_ref[1, :, D : 2 * D], got_ref[0, :, 2 * D :], got_ref[1, :, 2 * D :]
        )
    ]


def level_kernel(first, last, bit, index_ref, got_ref, *refs):
    if first:
        send_ref, track_ref = refs
    else:
        old_ref, send_ref, track_ref = refs
    upper = (index_ref[0] // bit) % 2 == 1
    low, up = got_ref[0, :, :D], got_ref[1, :, :D]
    b_low, b_up = got_ref[0, :, D : D + C], got_ref[1, :, D : D + C]
    g_low, g_up = got_ref[0, :, D + C :], got_ref[1, :, D + C :]
    if last:
        top = (index_ref[0] // (2 * bit)) % 2 == 1
        step = mm(split(jnp.where(top, low.T, up)), split(jnp.where(top, g_up, b_low)))
        half = jnp.where(top, g_low, b_up) + step
        send_ref[...] = jnp.concatenate([half[:C], half[C:]], axis=1)
    else:
        ahead = mm(split(up), split(jnp.concatenate([low, b_low], axis=1)))
        send_ref[:, :D] = ahead[:, :D]
        send_ref[:, D:] = jnp.concatenate(
            [ahead[:, D:] + b_up, g_low + mm(split(low.T), split(g_up))], axis=1
        )
    other = jnp.where(upper, jnp.concatenate([low, b_low], axis=1), jnp.concatenate([up.T, g_up], axis=1))
    if first:
        eye = jnp.where(iota((D, D), 0) == iota((D, D), 1), 1.0, 0.0)
        blank = jnp.concatenate([eye, jnp.zeros((D, C), F32)], axis=1)
        track_ref[0] = jnp.where(upper, other, blank)
        track_ref[1] = jnp.where(upper, blank, other)
    else:
        mine = jnp.where(upper, old_ref[0], old_ref[1])
        new = mm(split(mine[:, :D]), split(other))
        new = jnp.concatenate([new[:, :D], new[:, D:] + mine[:, D:]], axis=1)
        track_ref[0] = jnp.where(upper, new, old_ref[0])
        track_ref[1] = jnp.where(upper, old_ref[1], new)


def top_kernel(bit, index_ref, got_ref, track_ref, chips_ref, send_ref):
    upper = (index_ref[0] // bit) % 2 == 1
    lead = jnp.where(upper, track_ref[0, :, :D], track_ref[1, :, :D])
    got = jnp.where(upper, got_ref[0], got_ref[1])
    step = mm(split(lead), split(jnp.concatenate([got[:, :C], got[:, C:]], axis=0)))
    state = track_ref[0, :, D:] + jnp.where(upper, step, 0.0)
    adjoint = track_ref[1, :, D:] + jnp.where(upper, 0.0, step)
    b_low, _, _, g_up = pick(chips_ref, (index_ref[0] // 2) % 2 == 1)
    later = b_low + mm(split(chips_ref[0, :, :D]), split(state))
    sooner = g_up + mm(split(chips_ref[1, :, :D].T), split(adjoint))
    send_ref[:, :D] = jnp.concatenate([state, later], axis=1)
    send_ref[:, D:] = jnp.concatenate([sooner, adjoint], axis=1)


def after_kernel(index_ref, pair_ref, got_ref, q_ref, d_ref, k_ref, w_ref, m_ref, x0_ref, z0_ref,
                 gk_ref, s_ref, x_ref, z_ref, qs_ref, ds_ref):
    qs_ref[...] = q_ref[...].astype(F32)
    ds_ref[...] = d_ref[...].astype(F32)
    rows = [pl.ds(head, T, stride=2) for head in range(2)]
    upper = index_ref[0] % 2 == 1
    chip = (index_ref[0] // 2) % 2 == 1
    order = (0, 2, 1, 3)
    both = [jnp.concatenate([got_ref[j, :, half * D : (half + 1) * D] for j in order], axis=1) for half in range(2)]
    both = [
        [jnp.concatenate([b[:, (2 * i + w) * C : (2 * i + w + 1) * C] for i in range(4)], axis=1) for w in range(2)]
        for b in both
    ]
    state, adjoint = (jnp.where(chip, b[1], b[0]) for b in both)
    step = mm(
        split(jnp.where(upper, pair_ref[0, :, :D], pair_ref[1, :, :D].T)),
        split(jnp.where(upper, state, adjoint)),
    )
    state = jnp.where(upper, step + pair_ref[0, :, D : 3 * D], state)
    adjoint = jnp.where(upper, adjoint, step + pair_ref[1, :, 3 * D :])
    s_ref[...] = state
    states, adjoints = split(state), split(adjoint)
    root = places_root(index_ref[0])
    keys = split(k_ref[...])
    row, col = iota((T, T), 0), iota((T, T), 1)
    x = x0_ref[...] - mm(split(w_ref[...]), states)
    x_ref[...] = x
    xs = split(x)
    z = z0_ref[...] + mm(split(m_ref[...]), adjoints)
    z_ref[...] = z
    zs = split(z)
    edge = jnp.where(row > col, mm(zs, xs, (1, 1)), 0.0)
    gk = mm(xs, adjoints, (1, 1)) - 2.0 * mm(zs, states, (1, 1)) - 2.0 * mm(split(edge + edge.T), keys)
    for head in range(2):
        part = slice(head * D, (head + 1) * D)
        query = exact(qs_ref[rows[head], :].astype(BF16))
        grad = exact(ds_ref[rows[head], :].astype(BF16))
        mix = jnp.where(row >= col, mm(grad, tuple(s[:, part] for s in xs), (1, 1)), 0.0) * root
        gk = gk + mm(split(mix.T), query)
    gk_ref[...] = gk


def rest_kernel(index_ref, q_ref, d_ref, k_ref, s_ref, x_ref, z_ref, out_ref, gq_ref, gv_ref, qs_ref, ds_ref,
                os_ref, gs_ref, zs_ref):
    qs_ref[...] = q_ref[...].astype(F32)
    ds_ref[...] = d_ref[...].astype(F32)
    rows = [pl.ds(head, T, stride=2) for head in range(2)]
    root = places_root(index_ref[0])
    keys = split(k_ref[...])
    row, col = iota((T, T), 0), iota((T, T), 1)
    states, xs = split(s_ref[...]), split(x_ref[...])
    for head in range(2):
        part = slice(head * D, (head + 1) * D)
        head_states, head_xs = tuple(s[:, part] for s in states), tuple(s[:, part] for s in xs)
        query = exact(qs_ref[rows[head], :].astype(BF16))
        grad = exact(ds_ref[rows[head], :].astype(BF16))
        score = jnp.where(row >= col, mm(query, keys, (1, 1)), 0.0)
        os_ref[rows[head], :] = root * (mm(query, head_states) + mm(split(score), head_xs))
        mix = jnp.where(row >= col, mm(grad, head_xs, (1, 1)), 0.0)
        gs_ref[rows[head], :] = root * (mm(grad, head_states, (1, 1)) + mm(split(mix), keys))
        zs_ref[rows[head], :] = z_ref[:, part]
    out_ref[...] = os_ref[...].astype(BF16)
    gq_ref[...] = gs_ref[...].astype(BF16)
    gv_ref[...] = zs_ref[...].astype(BF16)


def sum_kernel(got_ref, out_ref):
    out_ref[...] = jnp.broadcast_to(jnp.sum(got_ref[...], axis=0, keepdims=True), out_ref.shape)


def key_kernel(got_ref, k_ref, norm_ref, out_ref):
    total, key = got_ref[...], k_ref[...]
    along = jnp.sum(total * key, axis=1, keepdims=True)
    out_ref[...] = ((total - key * along) * norm_ref[...]).astype(BF16)


def call(kernel, outs, *operands, scratch=(), scalars=1, cost=None):
    spaces = [pltpu.SMEM] * scalars + [pltpu.VMEM] * (len(operands) - scalars)
    single = not isinstance(outs, list)
    shapes = [outs] if single else outs
    result = pl.pallas_call(
        kernel,
        out_shape=[jax.ShapeDtypeStruct(*s) for s in shapes],
        in_specs=[pl.BlockSpec(memory_space=space) for space in spaces],
        out_specs=[pl.BlockSpec(memory_space=pltpu.VMEM)] * len(shapes),
        scratch_shapes=list(scratch),
        compiler_params=pltpu.CompilerParams(vmem_limit_bytes=VMEM_LIMIT),
        cost_estimate=cost,
    )(*operands)
    return result[0] if single else result


def exchange(x, bits):
    size = lax.axis_size("seq")
    mask = sum(bits)
    offsets = [0]
    for bit in bits:
        offsets = offsets + [o + bit for o in offsets]
    groups = [[i + o for o in offsets] for i in range(size) if i & mask == 0]
    return lax.all_gather(x, "seq", axis_index_groups=groups)


def shards(queries, raw_keys, values, cotangent):
    index = lax.axis_index("seq").astype(jnp.int32).reshape(1)
    q = queries.reshape(2 * T, D)
    v = values.reshape(2 * T, D)
    d = cotangent.reshape(2 * T, D)
    wide = pltpu.VMEM((2 * T, D), F32)
    key, norm, inv = call(
        keys_kernel, [((T, D), F32), ((T, D), F32), ((T, T), F32)], raw_keys, scalars=0, cost=LONG
    )
    send, w, m, x0, z0 = call(
        before_kernel,
        [((D, 5 * D), F32), ((T, D), F32), ((T, D), F32), ((T, 2 * D), F32), ((T, 2 * D), F32)],
        index, key, inv, q, v, d,
        scratch=[wide] * 3,
    )
    pair = exchange(send, (1,))
    send = call(pair_kernel, ((D, 3 * D), F32), index, pair)
    chips = exchange(send, (2,))
    send = call(chip_kernel, ((D, 2 * D), F32), index, chips)
    size = lax.axis_size("seq")
    bit = 4
    track = None
    while bit < size // 2:
        got = exchange(send, (bit,))
        last = bit == size // 4
        send, track = call(
            functools.partial(level_kernel, track is None, last, bit),
            [((C, D) if last else (D, 2 * D), F32), ((2, D, D + C), F32)],
            index, got, *([] if track is None else [track]),
        )
        bit *= 2
    send = call(functools.partial(top_kernel, bit), ((D, 2 * D), F32), index, exchange(send, (bit,)), track, chips)
    got = exchange(send, (1, 2))
    gk, state, x, z = call(
        after_kernel,
        [((T, D), F32), ((D, 2 * D), F32), ((T, 2 * D), F32), ((T, 2 * D), F32)],
        index, pair, got, q, d, key, w, m, x0, z0,
        scratch=[wide] * 2,
    )
    peers = lax.axis_size("head")
    pieces = lax.all_to_all(gk.reshape(peers, T // peers, D), "head", 0, 0)
    out, gq, gv = call(
        rest_kernel,
        [((2 * T, D), BF16)] * 3,
        index, q, d, key, state, x, z,
        scratch=[wide] * 5,
        cost=LONG,
    )
    totals = call(sum_kernel, ((peers, T // peers, D), F32), pieces, scalars=0)
    total = lax.all_to_all(totals, "head", 0, 0).reshape(T, D)
    gkey = call(key_kernel, ((T, D), BF16), total, key, norm, scalars=0)
    shape = queries.shape
    return out.reshape(shape), gq.reshape(shape), gkey, gv.reshape(shape)


def solution(mesh):
    split_both = P("seq", "head", None)
    keys_only = P("seq", None)
    return jax.shard_map(
        shards,
        mesh=mesh,
        in_specs=(split_both, keys_only, split_both, split_both),
        out_specs=(split_both, split_both, keys_only, split_both),
        check_vma=False,
    )
```

time: 106 us -> 97.8 us (0.923)
  the two profiles are of different devices: /device:TPU:2 before, /device:TPU:32 now
where the time goes in v2:
time: 97.8 us; the launch traced here: 97.4 us
  blocking collectives  72.5 us (74%)
  Pallas kernels  14 us (14%)
  waiting for transfers between devices  5.83 us (6%)
  starting transfers between devices  3.51 us (4%)
    all_gather x6, blocking collectives, exchange(): return lax.all_gather(x, 'seq', axis_index_groups=groups)  59.5 us
    pallas_call x11, Pallas kernels, call(): pl.pallas_call(kernel, out_shape=[jax.ShapeDtypeStruct(*s) for s in shape...  14 us
    all_to_all x1, blocking collectives, shards(): pieces = lax.all_to_all(gk.reshape(peers, T // peers, D), 'head', 0, 0)  13 us
    all_to_all x1, waiting for transfers between devices, shards(): total = lax.all_to_all(totals, 'head', 0, 0).reshape(T, D)  5.83 us
    all_to_all x1, starting transfers between devices, shards(): total = lax.all_to_all(totals, 'head', 0, 0).reshape(T, D)  3.51 us
  transfers between devices with their start and end apart: 1, of which 1 were waited for; matrix products, arithmetic and copies ran while one was open for 0% of the time, Pallas kernels for 2%

profile of v2, /device:TPU:32, one launch (start us, length us, event | category | flops | bytes accessed | tf_op | source)
XLA Modules:
  0.0 97.4 jit_solution(11441797910829716635)
XLA Ops:
  0.6 0.0 copy-start.3
  0.6 0.8 copy-done.3
  1.5 0.0 copy-start
  1.5 0.0 copy-start.1
  1.5 0.0 copy-start.2
  1.5 4.4 %shard_map.75 = (f32[256,128]{1,0:T(8,128)S(1)}, f32[256,128]{1,0:T(8,128)S(1)}, f32[256,256]{1,0:T(8,128)S(1)}) custom-call(bf16[256,128]{1,0:T(8,128)(2,1)S(1)} %copy-done.3), custom_call_target="tpu_custom_call" | custom-call | flops 4000000000 | bytes 4000000 | tf_op jit(solution)/shard_map/pallas_call | solution.py:274
  5.9 0.0 copy-done
  5.9 0.0 copy-done.1
  5.9 0.0 copy-done.2
  5.9 2.2 %shard_map.76 = (f32[128,640]{1,0:T(8,128)S(1)}, f32[256,128]{1,0:T(8,128)S(1)}, f32[256,128]{1,0:T(8,128)S(1)}, f32[256,256]{1,0:T(8,128)S(1)}, f32[256,256]{1,0:T(8,128)S(1)}) custom-call(s32[1]{0:T(128)} %bitcast.index_ref, f32[256,128]{1,0:T(8,128)S(1)} %get-tuple-element.23.k_ref, f32[256,256]{1,0:T(8,128)S(1)} %get-tuple-element.24.inv_ref, ...), custom_call_target="tpu_custom_call" | custom-call | tf_op jit(solution)/shard_map/pallas_call | solution.py:274
  8.1 2.3 %all-gather = f32[256,640]{1,0:T(8,128)S(1)} all-gather(f32[128,640]{1,0:T(8,128)S(1)} %get-tuple-element.25), channel_id=2, replica_groups={{0,16},{32,48},{64,80},{96,112},{128,144},{160,176},{192,208},{224,240}..., dimensions={0}, use_global_device_ids=true | all-gather | bytes 983040 | tf_op jit(solution)/shard_map/all_gather | solution.py:293
  10.4 0.2 shard_map.77
  10.6 11.3 %all-gather.1 = f32[256,384]{1,0:T(8,128)S(1)} all-gather(f32[128,384]{1,0:T(8,128)S(1)} %shard_map.77), channel_id=3, replica_groups={{0,32},{16,48},{64,96},{80,112},{128,160},{144,176},{192,224},{208,240}..., dimensions={0}, use_global_device_ids=true | all-gather | bytes 589824 | tf_op jit(solution)/shard_map/all_gather | solution.py:293
  22.0 0.4 shard_map.78
  22.4 6.7 %all-gather.2 = f32[256,256]{1,0:T(8,128)S(1)} all-gather(f32[128,256]{1,0:T(8,128)S(1)} %shard_map.78), channel_id=4, replica_groups={{0,64},{16,80},{32,96},{48,112},{128,192},{144,208},{160,224},{176,240}..., dimensions={0}, use_global_device_ids=true | all-gather | bytes 393216 | tf_op jit(solution)/shard_map/all_gather | solution.py:293
  29.1 0.4 shard_map.79
  29.5 15.7 %all-gather.3 = f32[256,256]{1,0:T(8,128)S(1)} all-gather(f32[128,256]{1,0:T(8,128)S(1)} %get-tuple-element.26), channel_id=5, replica_groups={{0,128},{16,144},{32,160},{48,176},{64,192},{80,208},{96,224},{112,240}..., dimensions={0}, use_global_device_ids=true | all-gather | bytes 393216 | tf_op jit(solution)/shard_map/all_gather | solution.py:293
  45.2 0.5 shard_map.80
  45.7 13.3 %all-gather.4 = f32[128,128]{1,0:T(8,128)S(1)} all-gather(f32[64,128]{1,0:T(8,128)S(1)} %get-tuple-element.28), channel_id=6, replica_groups={{0,256},{16,272},{32,288},{48,304},{64,320},{80,336},{96,352},{112,368}..., dimensions={0}, use_global_device_ids=true | all-gather | bytes 98304 | tf_op jit(solution)/shard_map/all_gather | solution.py:293
  59.0 0.6 shard_map.81
  59.5 10.2 %all-gather.5 = f32[512,256]{1,0:T(8,128)S(1)} all-gather(f32[128,256]{1,0:T(8,128)S(1)} %shard_map.81), channel_id=7, replica_groups={{0,16,32,48},{64,80,96,112},{128,144,160,176},{192,208,224,240},{256,27..., dimensions={0}, use_global_device_ids=true | all-gather | bytes 655360 | tf_op jit(solution)/shard_map/all_gather | solution.py:293
  69.7 1.9 %shard_map.82 = (f32[256,128]{1,0:T(8,128)S(1)}, f32[128,256]{1,0:T(8,128)S(1)}, f32[256,256]{1,0:T(8,128)S(1)}, f32[256,256]{1,0:T(8,128)S(1)}) custom-call(s32[1]{0:T(128)} %bitcast.index_ref, f32[2,128,640]{2,1,0:T(8,128)S(1)} %bitcast.16, f32[4,128,256]{2,1,0:T(8,128)S(1)} %bitcast.19, bf16[512,128]{1,0:T(8,128)(2,1)S(1)} %bitcast.24, ...), custom_call_target="tpu_custom_call" | custom-call | tf_op jit(solution)/shard_map/pallas_call | solution.py:274
  71.6 13.0 %all_to_all.10.got_ref = f32[16,16,128]{2,1,0:T(8,128)S(1)} all-to-all(f32[16,16,128]{2,1,0:T(8,128)S(1)} %bitcast.30), channel_id=1, replica_groups=mesh['seq'=32,'head'=16] {'head'}, dimensions={0} | all-to-all | bytes 262144 | tf_op jit(solution)/shard_map/all_to_all | solution.py:336
  84.6 0.7 shard_map.84
  85.2 3.5 %all-to-all-start.1 = ((f32[16,16,128]{2,1,0:T(8,128)}), f32[16,16,128]{2,1,0:T(8,128)S(1)}, u32[]{:S(2)}, u32[]{:S(2)}) async-start(f32[16,16,128]{2,1,0:T(8,128)} %shard_map.84), calls=%async_computation.1 | async-start | bytes 262144 | tf_op jit(solution)/shard_map/all_to_all | solution.py:345
  88.8 2.1 %shard_map.83 = (bf16[512,128]{1,0:T(8,128)(2,1)}, bf16[512,128]{1,0:T(8,128)(2,1)}, bf16[512,128]{1,0:T(8,128)(2,1)}) custom-call(s32[1]{0:T(128)} %bitcast.index_ref, bf16[512,128]{1,0:T(8,128)(2,1)S(1)} %bitcast.25, bf16[512,128]{1,0:T(8,128)(2,1)S(1)} %bitcast.28, f32[256,128]{1,0:T(8,128)S(1)} %get-tuple-element.23.k_ref, ...), custom_call_target="tpu_custom_call" | custom-call | flops 4000000000 | bytes 4000000 | tf_op jit(solution)/shard_map/pallas_call | solution.py:274
  90.9 5.8 %all-to-all-done.1 = f32[16,16,128]{2,1,0:T(8,128)S(1)} async-done(((f32[16,16,128]{2,1,0:T(8,128)}), f32[16,16,128]{2,1,0:T(8,128)S(1)}, u32[]{:S(2)}, u32[]{:S(2)}) %all-to-all-start.1) | async-done | bytes 131104 | tf_op jit(solution)/shard_map/all_to_all | solution.py:345
  96.7 0.7 shard_map.85
Async XLA Ops:
  0.6 0.8 copy-start.3
  1.5 4.4 %copy-start = (bf16[256,2,128]{2,1,0:T(2,128)(2,1)S(1)}, bf16[256,2,128]{2,1,0:T(2,128)(2,1)}, u32[]{:S(2)}) copy-start(bf16[256,2,128]{2,1,0:T(2,128)(2,1)} %param.4) | copy-start | bytes 393220
  1.5 4.4 %copy-start.1 = (bf16[256,2,128]{2,1,0:T(2,128)(2,1)S(1)}, bf16[256,2,128]{2,1,0:T(2,128)(2,1)}, u32[]{:S(2)}) copy-start(bf16[256,2,128]{2,1,0:T(2,128)(2,1)} %param.7) | copy-start | bytes 393220
  1.5 4.4 %copy-start.2 = (bf16[256,2,128]{2,1,0:T(2,128)(2,1)S(1)}, bf16[256,2,128]{2,1,0:T(2,128)(2,1)}, u32[]{:S(2)}) copy-start(bf16[256,2,128]{2,1,0:T(2,128)(2,1)} %param.6) | copy-start | bytes 393220
  85.2 11.5 %all-to-all-start.1 = ((f32[16,16,128]{2,1,0:T(8,128)}), f32[16,16,128]{2,1,0:T(8,128)S(1)}, u32[]{:S(2)}, u32[]{:S(2)}) async-start(f32[16,16,128]{2,1,0:T(8,128)} %shard_map.84), calls=%async_computation.1 | async-start | bytes 262144 | tf_op jit(solution)/shard_map/all_to_all | solution.py:345

commit v3 on v2

--- a/solution.py
+++ b/solution.py
@@ -8,6 +8,7 @@
 from jax.sharding import PartitionSpec as P
 
 T = 256
+PARTS = 32
 D = 128
 C = D // 2
 F32 = jnp.float32
@@ -143,47 +144,50 @@
     ]
 
 
-def level_kernel(first, last, bit, index_ref, got_ref, *refs):
-    if first:
-        send_ref, track_ref = refs
-    else:
-        old_ref, send_ref, track_ref = refs
-    upper = (index_ref[0] // bit) % 2 == 1
+def pack(x):
+    return jnp.concatenate([x[:C], x[C:]], axis=1)
+
+
+def unpack(x):
+    return jnp.concatenate([x[:, :C], x[:, C:]], axis=0)
+
+
+def block_kernel(index_ref, got_ref, send_ref, block_ref, track_ref):
+    block = index_ref[0] // 8
+    upper = (index_ref[0] // 4) % 2 == 1
     low, up = got_ref[0, :, :D], got_ref[1, :, :D]
     b_low, b_up = got_ref[0, :, D : D + C], got_ref[1, :, D : D + C]
     g_low, g_up = got_ref[0, :, D + C :], got_ref[1, :, D + C :]
-    if last:
-        top = (index_ref[0] // (2 * bit)) % 2 == 1
-        step = mm(split(jnp.where(top, low.T, up)), split(jnp.where(top, g_up, b_low)))
-        half = jnp.where(top, g_low, b_up) + step
-        send_ref[...] = jnp.concatenate([half[:C], half[C:]], axis=1)
-    else:
-        ahead = mm(split(up), split(jnp.concatenate([low, b_low], axis=1)))
-        send_ref[:, :D] = ahead[:, :D]
-        send_ref[:, D:] = jnp.concatenate(
-            [ahead[:, D:] + b_up, g_low + mm(split(low.T), split(g_up))], axis=1
-        )
-    other = jnp.where(upper, jnp.concatenate([low, b_low], axis=1), jnp.concatenate([up.T, g_up], axis=1))
-    if first:
-        eye = jnp.where(iota((D, D), 0) == iota((D, D), 1), 1.0, 0.0)
-        blank = jnp.concatenate([eye, jnp.zeros((D, C), F32)], axis=1)
-        track_ref[0] = jnp.where(upper, other, blank)
-        track_ref[1] = jnp.where(upper, blank, other)
-    else:
-        mine = jnp.where(upper, old_ref[0], old_ref[1])
-        new = mm(split(mine[:, :D]), split(other))
-        new = jnp.concatenate([new[:, :D], new[:, D:] + mine[:, D:]], axis=1)
-        track_ref[0] = jnp.where(upper, new, old_ref[0])
-        track_ref[1] = jnp.where(upper, old_ref[1], new)
-
-
-def top_kernel(bit, index_ref, got_ref, track_ref, chips_ref, send_ref):
-    upper = (index_ref[0] // bit) % 2 == 1
-    lead = jnp.where(upper, track_ref[0, :, :D], track_ref[1, :, :D])
-    got = jnp.where(upper, got_ref[0], got_ref[1])
-    step = mm(split(lead), split(jnp.concatenate([got[:, :C], got[:, C:]], axis=0)))
-    state = track_ref[0, :, D:] + jnp.where(upper, step, 0.0)
-    adjoint = track_ref[1, :, D:] + jnp.where(upper, 0.0, step)
+    ahead = mm(split(up), split(jnp.concatenate([low, b_low], axis=1)))
+    b_all = ahead[:, D:] + b_up
+    g_all = g_low + mm(split(low.T), split(g_up))
+    send_ref[...] = pack(jnp.where(block == 3, g_all, b_all))
+    block_ref[:, :D] = ahead[:, :D]
+    block_ref[:, D:] = jnp.concatenate([b_all, g_all], axis=1)
+    eye = jnp.where(iota((D, D), 0) == iota((D, D), 1), 1.0, 0.0)
+    blank = jnp.concatenate([eye, jnp.zeros((D, C), F32)], axis=1)
+    track_ref[0] = jnp.where(upper, jnp.concatenate([low, b_low], axis=1), blank)
+    track_ref[1] = jnp.where(upper, blank, jnp.concatenate([up.T, g_up], axis=1))
+
+
+def hop_kernel(downward, index_ref, got_ref, block_ref, send_ref):
+    down = index_ref[0] // 8 == downward
+    whole = block_ref[:, :D]
+    got = unpack(jnp.where(down, got_ref[1], got_ref[0]))
+    own = jnp.where(down, block_ref[:, D + C :], block_ref[:, D : D + C])
+    send_ref[...] = pack(own + mm(split(jnp.where(down, whole.T, whole)), split(got)))
+
+
+def top_kernel(index_ref, first_ref, second_ref, third_ref, track_ref, chips_ref, send_ref):
+    block = index_ref[0] // 8
+    got = jnp.where(
+        block == 1, first_ref[0], jnp.where(block == 2, second_ref[0], jnp.where(block == 3, third_ref[0], 0.0))
+    )
+    state = track_ref[0, :, D:] + mm(split(track_ref[0, :, :D]), split(unpack(got)))
+    got = jnp.where(
+        block == 2, first_ref[1], jnp.where(block == 1, second_ref[1], jnp.where(block == 0, third_ref[1], 0.0))
+    )
+    adjoint = track_ref[1, :, D:] + mm(split(track_ref[1, :, :D]), split(unpack(got)))
     b_low, _, _, g_up = pick(chips_ref, (index_ref[0] // 2) % 2 == 1)
     later = b_low + mm(split(chips_ref[0, :, :D]), split(state))
     sooner = g_up + mm(split(chips_ref[1, :, :D].T), split(adjoint))
@@ -283,14 +287,20 @@
     return result[0] if single else result
 
 
-def exchange(x, bits):
-    size = lax.axis_size("seq")
-    mask = sum(bits)
-    offsets = [0]
-    for bit in bits:
-        offsets = offsets + [o + bit for o in offsets]
-    groups = [[i + o for o in offsets] for i in range(size) if i & mask == 0]
+def exchange(x, groups):
     return lax.all_gather(x, "seq", axis_index_groups=groups)
+
+
+def near(*offsets):
+    groups, taken = [], set()
+    for i in range(PARTS):
+        if i not in taken:
+            groups.append([i + offset for offset in offsets])
+            taken.update(groups[-1])
+    return groups
+
+
+CROSS = [[i, i + 24] for i in range(8)] + [[i, i + 8] for i in range(8, 16)]
 
 
 def shards(queries, raw_keys, values, cotangent):
@@ -308,24 +318,22 @@
         index, key, inv, q, v, d,
         scratch=[wide] * 3,
     )
-    pair = exchange(send, (1,))
+    pair = exchange(send, near(0, 1))
     send = call(pair_kernel, ((D, 3 * D), F32), index, pair)
-    chips = exchange(send, (2,))
+    chips = exchange(send, near(0, 2))
     send = call(chip_kernel, ((D, 2 * D), F32), index, chips)
-    size = lax.axis_size("seq")
-    bit = 4
-    track = None
-    while bit < size // 2:
-        got = exchange(send, (bit,))
-        last = bit == size // 4
-        send, track = call(
-            functools.partial(level_kernel, track is None, last, bit),
-            [((C, D) if last else (D, 2 * D), F32), ((2, D, D + C), F32)],
-            index, got, *([] if track is None else [track]),
-        )
-        bit *= 2
-    send = call(functools.partial(top_kernel, bit), ((D, 2 * D), F32), index, exchange(send, (bit,)), track, chips)
-    got = exchange(send, (1, 2))
+    send, block, track = call(
+        block_kernel,
+        [((C, D), F32), ((D, 2 * D), F32), ((2, D, D + C), F32)],
+        index, exchange(send, near(0, 4)),
+    )
+    first = exchange(send, near(0, 8))
+    send = call(functools.partial(hop_kernel, 2), ((C, D), F32), index, first, block)
+    second = exchange(send, CROSS)
+    send = call(functools.partial(hop_kernel, 1), ((C, D), F32), index, second, block)
+    third = exchange(send, near(0, 8))
+    send = call(top_kernel, ((D, 2 * D), F32), index, first, second, third, track, chips)
+    got = exchange(send, near(0, 1, 2, 3))
     gk, state, x, z = call(
         after_kernel,
         [((T, D), F32), ((D, 2 * D), F32), ((T, 2 * D), F32), ((T, 2 * D), F32)],

time: 97.8 us -> 95.7 us (0.979)
  blocking collectives: 72.5 us -> 70 us
    all_gather x6 -> x7, blocking collectives: 59.5 us -> 56 us  [exchange(): return lax.all_gather(x, 'seq', axis_index_groups=groups)]
    pallas_call x11 -> x12, Pallas kernels: 14 us -> 14.4 us  [call(): pl.pallas_call(kernel, out_shape=[jax.ShapeDtypeStruct(*s) for s in shape...]
where the time goes in v3:
time: 95.7 us; the launch traced here: 95.3 us
  blocking collectives  70 us (73%)
  Pallas kernels  14.4 us (15%)
  waiting for transfers between devices  5.83 us (6%)
  starting transfers between devices  3.51 us (4%)
    all_gather x7, blocking collectives, exchange(): return lax.all_gather(x, 'seq', axis_index_groups=groups)  56 us
    pallas_call x12, Pallas kernels, call(): pl.pallas_call(kernel, out_shape=[jax.ShapeDtypeStruct(*s) for s in shape...  14.4 us
    all_to_all x1, blocking collectives, shards(): pieces = lax.all_to_all(gk.reshape(peers, T // peers, D), 'head', 0, 0)  13.9 us
    all_to_all x1, waiting for transfers between devices, shards(): total = lax.all_to_all(totals, 'head', 0, 0).reshape(T, D)  5.83 us
    all_to_all x1, starting transfers between devices, shards(): total = lax.all_to_all(totals, 'head', 0, 0).reshape(T, D)  3.51 us
  transfers between devices with their start and end apart: 1, of which 1 were waited for; matrix products, arithmetic and copies ran while one was open for 0% of the time, Pallas kernels for 2%

profile of v3, /device:TPU:32, one launch (start us, length us, event | category | flops | bytes accessed | tf_op | source)
XLA Modules:
  0.0 95.3 jit_solution(16364276666485306981)
XLA Ops:
  0.6 0.0 copy-start.3
  0.6 0.8 copy-done.3
  1.5 0.0 copy-start
  1.5 0.0 copy-start.1
  1.5 0.0 copy-start.2
  1.5 4.4 %shard_map.75 = (f32[256,128]{1,0:T(8,128)S(1)}, f32[256,128]{1,0:T(8,128)S(1)}, f32[256,256]{1,0:T(8,128)S(1)}) custom-call(bf16[256,128]{1,0:T(8,128)(2,1)S(1)} %copy-done.3), custom_call_target="tpu_custom_call" | custom-call | flops 4000000000 | bytes 4000000 | tf_op jit(solution)/shard_map/pallas_call | solution.py:278
  5.9 0.0 copy-done
  5.9 0.0 copy-done.1
  5.9 0.0 copy-done.2
  5.9 2.2 %shard_map.76 = (f32[128,640]{1,0:T(8,128)S(1)}, f32[256,128]{1,0:T(8,128)S(1)}, f32[256,128]{1,0:T(8,128)S(1)}, f32[256,256]{1,0:T(8,128)S(1)}, f32[256,256]{1,0:T(8,128)S(1)}) custom-call(s32[1]{0:T(128)} %bitcast.index_ref, f32[256,128]{1,0:T(8,128)S(1)} %get-tuple-element.22.k_ref, f32[256,256]{1,0:T(8,128)S(1)} %get-tuple-element.23.inv_ref, ...), custom_call_target="tpu_custom_call" | custom-call | tf_op jit(solution)/shard_map/pallas_call | solution.py:278
  8.1 2.3 %all-gather = f32[256,640]{1,0:T(8,128)S(1)} all-gather(f32[128,640]{1,0:T(8,128)S(1)} %get-tuple-element.24), channel_id=2, replica_groups={{0,16},{32,48},{64,80},{96,112},{128,144},{160,176},{192,208},{224,240}..., dimensions={0}, use_global_device_ids=true | all-gather | bytes 983040 | tf_op jit(solution)/shard_map/all_gather | solution.py:291
  10.4 0.2 shard_map.77
  10.6 11.3 %all-gather.1 = f32[256,384]{1,0:T(8,128)S(1)} all-gather(f32[128,384]{1,0:T(8,128)S(1)} %shard_map.77), channel_id=3, replica_groups={{0,32},{16,48},{64,96},{80,112},{128,160},{144,176},{192,224},{208,240}..., dimensions={0}, use_global_device_ids=true | all-gather | bytes 589824 | tf_op jit(solution)/shard_map/all_gather | solution.py:291
  22.0 0.4 shard_map.78
  22.4 6.7 %all-gather.2 = f32[256,256]{1,0:T(8,128)S(1)} all-gather(f32[128,256]{1,0:T(8,128)S(1)} %shard_map.78), channel_id=4, replica_groups={{0,64},{16,80},{32,96},{48,112},{128,192},{144,208},{160,224},{176,240}..., dimensions={0}, use_global_device_ids=true | all-gather | bytes 393216 | tf_op jit(solution)/shard_map/all_gather | solution.py:291
  29.1 0.4 shard_map.79
  29.6 8.5 %all-gather.3 = f32[128,128]{1,0:T(8,128)S(1)} all-gather(f32[64,128]{1,0:T(8,128)S(1)} %get-tuple-element.25), channel_id=5, replica_groups={{0,128},{16,144},{32,160},{48,176},{64,192},{80,208},{96,224},{112,240}..., dimensions={0}, use_global_device_ids=true | all-gather | bytes 98304 | tf_op jit(solution)/shard_map/all_gather | solution.py:291
  38.1 0.4 shard_map.80
  38.5 9.2 %all-gather.4 = f32[128,128]{1,0:T(8,128)S(1)} all-gather(f32[64,128]{1,0:T(8,128)S(1)} %shard_map.80), channel_id=6, replica_groups={{0,384},{16,400},{32,416},{48,432},{64,448},{80,464},{96,480},{112,496}..., dimensions={0}, use_global_device_ids=true | all-gather | bytes 98304 | tf_op jit(solution)/shard_map/all_gather | solution.py:291
  47.7 0.4 shard_map.81
  48.1 8.9 %all-gather.5 = f32[128,128]{1,0:T(8,128)S(1)} all-gather(f32[64,128]{1,0:T(8,128)S(1)} %shard_map.81), channel_id=7, replica_groups={{0,128},{16,144},{32,160},{48,176},{64,192},{80,208},{96,224},{112,240}..., dimensions={0}, use_global_device_ids=true | all-gather | bytes 98304 | tf_op jit(solution)/shard_map/all_gather | solution.py:291
  57.0 0.6 shard_map.82
  57.6 9.1 %all-gather.6 = f32[512,256]{1,0:T(8,128)S(1)} all-gather(f32[128,256]{1,0:T(8,128)S(1)} %shard_map.82), channel_id=8, replica_groups={{0,16,32,48},{64,80,96,112},{128,144,160,176},{192,208,224,240},{256,27..., dimensions={0}, use_global_device_ids=true | all-gather | bytes 655360 | tf_op jit(solution)/shard_map/all_gather | solution.py:291
  66.6 1.9 %shard_map.83 = (f32[256,128]{1,0:T(8,128)S(1)}, f32[128,256]{1,0:T(8,128)S(1)}, f32[256,256]{1,0:T(8,128)S(1)}, f32[256,256]{1,0:T(8,128)S(1)}) custom-call(s32[1]{0:T(128)} %bitcast.index_ref, f32[2,128,640]{2,1,0:T(8,128)S(1)} %bitcast.17, f32[4,128,256]{2,1,0:T(8,128)S(1)} %bitcast.20, bf16[512,128]{1,0:T(8,128)(2,1)S(1)} %bitcast.28, ...), custom_call_target="tpu_custom_call" | custom-call | tf_op jit(solution)/shard_map/pallas_call | solution.py:278
  68.5 13.9 %all_to_all.10.got_ref = f32[16,16,128]{2,1,0:T(8,128)S(1)} all-to-all(f32[16,16,128]{2,1,0:T(8,128)S(1)} %bitcast.34), channel_id=1, replica_groups=mesh['seq'=32,'head'=16] {'head'}, dimensions={0} | all-to-all | bytes 262144 | tf_op jit(solution)/shard_map/all_to_all | solution.py:344
  82.5 0.7 shard_map.85
  83.1 3.5 %all-to-all-start.1 = ((f32[16,16,128]{2,1,0:T(8,128)}), f32[16,16,128]{2,1,0:T(8,128)S(1)}, u32[]{:S(2)}, u32[]{:S(2)}) async-start(f32[16,16,128]{2,1,0:T(8,128)} %shard_map.85), calls=%async_computation.1 | async-start | bytes 262144 | tf_op jit(solution)/shard_map/all_to_all | solution.py:353
  86.6 2.1 %shard_map.84 = (bf16[512,128]{1,0:T(8,128)(2,1)}, bf16[512,128]{1,0:T(8,128)(2,1)}, bf16[512,128]{1,0:T(8,128)(2,1)}) custom-call(s32[1]{0:T(128)} %bitcast.index_ref, bf16[512,128]{1,0:T(8,128)(2,1)S(1)} %bitcast.29, bf16[512,128]{1,0:T(8,128)(2,1)S(1)} %bitcast.32, f32[256,128]{1,0:T(8,128)S(1)} %get-tuple-element.22.k_ref, ...), custom_call_target="tpu_custom_call" | custom-call | flops 4000000000 | bytes 4000000 | tf_op jit(solution)/shard_map/pallas_call | solution.py:278
  88.8 5.8 %all-to-all-done.1 = f32[16,16,128]{2,1,0:T(8,128)S(1)} async-done(((f32[16,16,128]{2,1,0:T(8,128)}), f32[16,16,128]{2,1,0:T(8,128)S(1)}, u32[]{:S(2)}, u32[]{:S(2)}) %all-to-all-start.1) | async-done | bytes 131104 | tf_op jit(solution)/shard_map/all_to_all | solution.py:353
  94.6 0.7 shard_map.86
Async XLA Ops:
  0.6 0.8 copy-start.3
  1.5 4.4 %copy-start = (bf16[256,2,128]{2,1,0:T(2,128)(2,1)S(1)}, bf16[256,2,128]{2,1,0:T(2,128)(2,1)}, u32[]{:S(2)}) copy-start(bf16[256,2,128]{2,1,0:T(2,128)(2,1)} %param.4) | copy-start | bytes 393220
  1.5 4.4 %copy-start.1 = (bf16[256,2,128]{2,1,0:T(2,128)(2,1)S(1)}, bf16[256,2,128]{2,1,0:T(2,128)(2,1)}, u32[]{:S(2)}) copy-start(bf16[256,2,128]{2,1,0:T(2,128)(2,1)} %param.7) | copy-start | bytes 393220
  1.5 4.4 %copy-start.2 = (bf16[256,2,128]{2,1,0:T(2,128)(2,1)S(1)}, bf16[256,2,128]{2,1,0:T(2,128)(2,1)}, u32[]{:S(2)}) copy-start(bf16[256,2,128]{2,1,0:T(2,128)(2,1)} %param.6) | copy-start | bytes 393220
  83.1 11.5 %all-to-all-start.1 = ((f32[16,16,128]{2,1,0:T(8,128)}), f32[16,16,128]{2,1,0:T(8,128)S(1)}, u32[]{:S(2)}, u32[]{:S(2)}) async-start(f32[16,16,128]{2,1,0:T(8,128)} %shard_map.85), calls=%async_computation.1 | async-start | bytes 262144 | tf_op jit(solution)/shard_map/all_to_all | solution.py:353

commit v4 on v3

--- a/solution.py
+++ b/solution.py
@@ -10,10 +10,10 @@
 T = 256
 PARTS = 32
 D = 128
-C = D // 2
 F32 = jnp.float32
 BF16 = jnp.bfloat16
 VMEM_LIMIT = 48 * 1024 * 1024
+SHORT = pl.CostEstimate(flops=500000000, bytes_accessed=1000000, transcendentals=0)
 LONG = pl.CostEstimate(flops=4000000000, bytes_accessed=4000000, transcendentals=0)
 
 
@@ -80,36 +80,48 @@
     inv_ref[half:, half:] = second
 
 
-def before_kernel(index_ref, k_ref, inv_ref, q_ref, v_ref, d_ref, send_ref, w_ref, m_ref, x_ref, z_ref,
-                  qs_ref, vs_ref, ds_ref):
-    qs_ref[...] = q_ref[...].astype(F32)
-    vs_ref[...] = v_ref[...].astype(F32)
-    ds_ref[...] = d_ref[...].astype(F32)
-    rows = [pl.ds(head, T, stride=2) for head in range(2)]
+def load_heads(pairs):
+    for source, room in pairs:
+        room[...] = source[...].astype(F32)
+    return [pl.ds(head, T, stride=2) for head in range(2)]
+
+
+def causal_scores(query, keys, root):
+    row, col = iota((T, T), 0), iota((T, T), 1)
+    return jnp.where(row >= col, mm(exact(query.astype(BF16)), keys, (1, 1)), 0.0) * root
+
+
+def before_kernel(index_ref, k_ref, inv_ref, q_ref, v_ref, d_ref, send_ref, w_ref, x_ref, qs_ref, vs_ref, ds_ref):
+    rows = load_heads([(q_ref, qs_ref), (v_ref, vs_ref), (d_ref, ds_ref)])
     root = places_root(index_ref[0])
-    row, col = iota((T, T), 0), iota((T, T), 1)
-    key, inv = k_ref[...], inv_ref[...]
-    keys, invs = split(key), split(inv)
+    key = k_ref[...]
+    keys, invs, keys_t = split(key), split(inv_ref[...]), split(key.T)
     w = 2.0 * mm(invs, keys)
     w_ref[...] = w
     ws = split(w)
-    keys_t = split(key.T)
     eye = jnp.where(iota((D, D), 0) == iota((D, D), 1), 1.0, 0.0)
     send_ref[:, :D] = eye - mm(keys_t, ws)
     value = jnp.concatenate([vs_ref[r, :] for r in rows], axis=1).astype(BF16)
     x0 = mm(invs, exact(value))
     x_ref[...] = x0
     send_ref[:, D : 3 * D] = mm(keys_t, split(x0))
-    inv_t = split(inv.T)
+    for head in range(2):
+        query = qs_ref[rows[head], :]
+        grad = exact(ds_ref[rows[head], :].astype(BF16))
+        qhat = query * root - mm(split(causal_scores(query, keys, root)), ws)
+        send_ref[:, (3 + head) * D : (4 + head) * D] = mm(split(qhat.T), grad)
+
+
+def side_kernel(index_ref, sent_ref, k_ref, inv_ref, q_ref, d_ref, m_ref, z_ref, qs_ref, ds_ref):
+    del sent_ref
+    rows = load_heads([(q_ref, qs_ref), (d_ref, ds_ref)])
+    root = places_root(index_ref[0])
+    keys, inv_t = split(k_ref[...]), split(inv_ref[...].T)
     m_ref[...] = mm(inv_t, keys)
     back = []
     for head in range(2):
-        query = qs_ref[rows[head], :]
-        grad = exact(ds_ref[rows[head], :].astype(BF16))
-        score = jnp.where(row >= col, mm(exact(query.astype(BF16)), keys, (1, 1)), 0.0) * root
-        qhat = query * root - mm(split(score), ws)
-        send_ref[:, (3 + head) * D : (4 + head) * D] = mm(split(qhat.T), grad)
-        back.append(mm(split(score.T), grad))
+        score = causal_scores(qs_ref[rows[head], :], keys, root)
+        back.append(mm(split(score.T), exact(ds_ref[rows[head], :].astype(BF16))))
     z_ref[...] = mm(inv_t, split(jnp.concatenate(back, axis=1)))
 
 
@@ -124,75 +136,58 @@
     send_ref[:, 2 * D :] = got_ref[0, :, at_g] + mm(split(low.T), split(got_ref[1, :, at_g]))
 
 
-def chip_kernel(index_ref, got_ref, send_ref):
-    right = (index_ref[0] // 2) % 2 == 1
-    low, up = got_ref[0, :, :D], got_ref[1, :, :D]
-    b_low, b_up, g_low, g_up = pick(got_ref, right)
-    ahead = mm(split(up), split(jnp.concatenate([low, b_low], axis=1)))
-    send_ref[:, :D] = ahead[:, :D]
-    send_ref[:, D:] = jnp.concatenate(
-        [ahead[:, D:] + b_up, g_low + mm(split(low.T), split(g_up))], axis=1
-    )
-
-
-def pick(got_ref, right):
-    return [
-        jnp.where(right, half[:, C:], half[:, :C])
-        for half in (
-            got_ref[0, :, D : 2 * D], got_ref[1, :, D : 2 * D], got_ref[0, :, 2 * D :], got_ref[1, :, 2 * D :]
-        )
-    ]
-
-
-def pack(x):
-    return jnp.concatenate([x[:C], x[C:]], axis=1)
-
-
-def unpack(x):
-    return jnp.concatenate([x[:, :C], x[:, C:]], axis=0)
-
-
-def block_kernel(index_ref, got_ref, send_ref, block_ref, track_ref):
+def joined(low, up):
+    ahead = mm(split(up[:, :D]), split(low[:, : 2 * D]))
+    state = ahead[:, D:] + up[:, D : 2 * D]
+    gradient = low[:, 2 * D :] + mm(split(low[:, :D].T), split(up[:, 2 * D :]))
+    return jnp.concatenate([ahead[:, :D], state, gradient], axis=1)
+
+
+def block_kernel(index_ref, got_ref, send_ref, block_ref, halves_ref):
     block = index_ref[0] // 8
-    upper = (index_ref[0] // 4) % 2 == 1
-    low, up = got_ref[0, :, :D], got_ref[1, :, :D]
-    b_low, b_up = got_ref[0, :, D : D + C], got_ref[1, :, D : D + C]
-    g_low, g_up = got_ref[0, :, D + C :], got_ref[1, :, D + C :]
-    ahead = mm(split(up), split(jnp.concatenate([low, b_low], axis=1)))
-    b_all = ahead[:, D:] + b_up
-    g_all = g_low + mm(split(low.T), split(g_up))
-    send_ref[...] = pack(jnp.where(block == 3, g_all, b_all))
-    block_ref[:, :D] = ahead[:, :D]
-    block_ref[:, D:] = jnp.concatenate([b_all, g_all], axis=1)
+    low = joined(got_ref[0], got_ref[1])
+    up = joined(got_ref[2], got_ref[3])
+    halves_ref[0] = low
+    halves_ref[1] = up
+    whole = joined(low, up)
+    block_ref[...] = whole
+    send_ref[...] = jnp.where(block == 3, whole[:, 2 * D :], whole[:, D : 2 * D])
+
+
+def place_kernel(index_ref, sent_ref, got_ref, halves_ref, track_ref):
+    del sent_ref
+    chip = (index_ref[0] // 2) % 4
     eye = jnp.where(iota((D, D), 0) == iota((D, D), 1), 1.0, 0.0)
-    blank = jnp.concatenate([eye, jnp.zeros((D, C), F32)], axis=1)
-    track_ref[0] = jnp.where(upper, jnp.concatenate([low, b_low], axis=1), blank)
-    track_ref[1] = jnp.where(upper, blank, jnp.concatenate([up.T, g_up], axis=1))
+    blank = jnp.concatenate([eye, jnp.zeros((D, D), F32)], axis=1)
+    below = halves_ref[0, :, : 2 * D]
+    above = jnp.concatenate([halves_ref[1, :, :D].T, halves_ref[1, :, 2 * D :]], axis=1)
+    outer = chip == 3
+    step = mm(
+        split(jnp.where(outer, got_ref[2, :, :D], got_ref[1, :, :D].T)), split(jnp.where(outer, below, above))
+    )
+    add = jnp.where(outer, got_ref[2, :, D : 2 * D], got_ref[1, :, 2 * D :])
+    step = jnp.concatenate([step[:, :D], step[:, D:] + add], axis=1)
+    track_ref[0] = jnp.where(
+        chip == 0, blank, jnp.where(chip == 1, got_ref[0, :, : 2 * D], jnp.where(chip == 2, below, step))
+    )
+    last = jnp.concatenate([got_ref[3, :, :D].T, got_ref[3, :, 2 * D :]], axis=1)
+    track_ref[1] = jnp.where(chip == 3, blank, jnp.where(chip == 2, last, jnp.where(chip == 1, above, step)))
 
 
 def hop_kernel(downward, index_ref, got_ref, block_ref, send_ref):
     down = index_ref[0] // 8 == downward
     whole = block_ref[:, :D]
-    got = unpack(jnp.where(down, got_ref[1], got_ref[0]))
-    own = jnp.where(down, block_ref[:, D + C :], block_ref[:, D : D + C])
-    send_ref[...] = pack(own + mm(split(jnp.where(down, whole.T, whole)), split(got)))
-
-
-def top_kernel(index_ref, first_ref, second_ref, third_ref, track_ref, chips_ref, send_ref):
+    own = jnp.where(down, block_ref[:, 2 * D :], block_ref[:, D : 2 * D])
+    send_ref[...] = own + mm(split(jnp.where(down, whole.T, whole)), split(got_ref[...]))
+
+
+def top_kernel(index_ref, first_ref, second_ref, third_ref, track_ref, send_ref):
     block = index_ref[0] // 8
-    got = jnp.where(
-        block == 1, first_ref[0], jnp.where(block == 2, second_ref[0], jnp.where(block == 3, third_ref[0], 0.0))
-    )
-    state = track_ref[0, :, D:] + mm(split(track_ref[0, :, :D]), split(unpack(got)))
-    got = jnp.where(
-        block == 2, first_ref[1], jnp.where(block == 1, second_ref[1], jnp.where(block == 0, third_ref[1], 0.0))
-    )
-    adjoint = track_ref[1, :, D:] + mm(split(track_ref[1, :, :D]), split(unpack(got)))
-    b_low, _, _, g_up = pick(chips_ref, (index_ref[0] // 2) % 2 == 1)
-    later = b_low + mm(split(chips_ref[0, :, :D]), split(state))
-    sooner = g_up + mm(split(chips_ref[1, :, :D].T), split(adjoint))
-    send_ref[:, :D] = jnp.concatenate([state, later], axis=1)
-    send_ref[:, D:] = jnp.concatenate([sooner, adjoint], axis=1)
+    first, second, third = first_ref[...], second_ref[...], third_ref[...]
+    state = jnp.where(block == 1, first, jnp.where(block == 2, second, jnp.where(block == 3, third, 0.0)))
+    adjoint = jnp.where(block == 2, first, jnp.where(block == 1, second, jnp.where(block == 0, third, 0.0)))
+    send_ref[:, :D] = track_ref[0, :, D:] + mm(split(track_ref[0, :, :D]), split(state))
+    send_ref[:, D:] = track_ref[1, :, D:] + mm(split(track_ref[1, :, :D]), split(adjoint))
 
 
 def after_kernel(index_ref, pair_ref, got_ref, q_ref, d_ref, k_ref, w_ref, m_ref, x0_ref, z0_ref,
@@ -201,14 +196,8 @@
     ds_ref[...] = d_ref[...].astype(F32)
     rows = [pl.ds(head, T, stride=2) for head in range(2)]
     upper = index_ref[0] % 2 == 1
-    chip = (index_ref[0] // 2) % 2 == 1
-    order = (0, 2, 1, 3)
-    both = [jnp.concatenate([got_ref[j, :, half * D : (half + 1) * D] for j in order], axis=1) for half in range(2)]
-    both = [
-        [jnp.concatenate([b[:, (2 * i + w) * C : (2 * i + w + 1) * C] for i in range(4)], axis=1) for w in range(2)]
-        for b in both
-    ]
-    state, adjoint = (jnp.where(chip, b[1], b[0]) for b in both)
+    state = jnp.concatenate([got_ref[0, :, :D], got_ref[1, :, :D]], axis=1)
+    adjoint = jnp.concatenate([got_ref[0, :, D:], got_ref[1, :, D:]], axis=1)
     step = mm(
         split(jnp.where(upper, pair_ref[0, :, :D], pair_ref[1, :, :D].T)),
         split(jnp.where(upper, state, adjoint)),
@@ -300,7 +289,8 @@
     return groups
 
 
-CROSS = [[i, i + 24] for i in range(8)] + [[i, i + 8] for i in range(8, 16)]
+def hop(x, *moves):
+    return lax.ppermute(x, "seq", [(8 * a + i, 8 * b + i) for a, b in moves for i in range(8)])
 
 
 def shards(queries, raw_keys, values, cotangent):
@@ -312,28 +302,33 @@
     key, norm, inv = call(
         keys_kernel, [((T, D), F32), ((T, D), F32), ((T, T), F32)], raw_keys, scalars=0, cost=LONG
     )
-    send, w, m, x0, z0 = call(
+    send, w, x0 = call(
         before_kernel,
-        [((D, 5 * D), F32), ((T, D), F32), ((T, D), F32), ((T, 2 * D), F32), ((T, 2 * D), F32)],
+        [((D, 5 * D), F32), ((T, D), F32), ((T, 2 * D), F32)],
         index, key, inv, q, v, d,
         scratch=[wide] * 3,
     )
     pair = exchange(send, near(0, 1))
     send = call(pair_kernel, ((D, 3 * D), F32), index, pair)
-    chips = exchange(send, near(0, 2))
-    send = call(chip_kernel, ((D, 2 * D), F32), index, chips)
-    send, block, track = call(
-        block_kernel,
-        [((C, D), F32), ((D, 2 * D), F32), ((2, D, D + C), F32)],
-        index, exchange(send, near(0, 4)),
-    )
-    first = exchange(send, near(0, 8))
-    send = call(functools.partial(hop_kernel, 2), ((C, D), F32), index, first, block)
-    second = exchange(send, CROSS)
-    send = call(functools.partial(hop_kernel, 1), ((C, D), F32), index, second, block)
-    third = exchange(send, near(0, 8))
-    send = call(top_kernel, ((D, 2 * D), F32), index, first, second, third, track, chips)
-    got = exchange(send, near(0, 1, 2, 3))
+    chips = exchange(send, near(0, 2, 4, 6))
+    send, block, halves = call(
+        block_kernel, [((D, D), F32), ((D, 3 * D), F32), ((2, D, 3 * D), F32)], index, chips
+    )
+    first = hop(send, (0, 1), (3, 2))
+    track = call(place_kernel, ((2, D, 2 * D), F32), index, send, chips, halves, cost=SHORT)
+    m, z0 = call(
+        side_kernel,
+        [((T, D), F32), ((T, 2 * D), F32)],
+        index, send, key, inv, q, d,
+        scratch=[wide] * 2,
+        cost=SHORT,
+    )
+    send = call(functools.partial(hop_kernel, 2), ((D, D), F32), index, first, block)
+    second = hop(send, (1, 2), (2, 1))
+    send = call(functools.partial(hop_kernel, 1), ((D, D), F32), index, second, block)
+    third = hop(send, (2, 3), (1, 0))
+    send = call(top_kernel, ((D, 2 * D), F32), index, first, second, third, track)
+    got = exchange(send, near(0, 1))
     gk, state, x, z = call(
         after_kernel,
         [((T, D), F32), ((D, 2 * D), F32), ((T, 2 * D), F32), ((T, 2 * D), F32)],

time: 95.7 us -> 95.3 us (level)
  the two profiles are of different devices: /device:TPU:32 before, /device:TPU:2 now
where the time goes in v4:
time: 95.3 us; the launch traced here: 95 us
  blocking collectives  39 us (41%)
  waiting for transfers between devices  24.3 us (25%)
  starting transfers between devices  15.8 us (17%)
  Pallas kernels  14.3 us (15%)
    all_gather x3, blocking collectives, exchange(): return lax.all_gather(x, 'seq', axis_index_groups=groups)  25.1 us
    ppermute x3, waiting for transfers between devices, hop(): lax.ppermute(x, 'seq', [(8 * a + i, 8 * b + i) for a, b in moves for i in...  19.7 us
    pallas_call x13, Pallas kernels, call(): pl.pallas_call(kernel, out_shape=[jax.ShapeDtypeStruct(*s) for s in shape...  14.3 us
    all_to_all x1, blocking collectives, shards(): pieces = lax.all_to_all(gk.reshape(peers, T // peers, D), 'head', 0, 0)  13.9 us
    ppermute x3, starting transfers between devices, hop(): lax.ppermute(x, 'seq', [(8 * a + i, 8 * b + i) for a, b in moves for i in...  11.1 us
    all_to_all x1, starting transfers between devices, shards(): total = lax.all_to_all(totals, 'head', 0, 0).reshape(T, D)  4.76 us
    all_to_all x1, waiting for transfers between devices, shards(): total = lax.all_to_all(totals, 'head', 0, 0).reshape(T, D)  4.6 us
  transfers between devices with their start and end apart: 4, of which 3 were waited for; matrix products, arithmetic and copies ran while one was open for 0% of the time, Pallas kernels for 4%

profile of v4, /device:TPU:2, one launch (start us, length us, event | category | flops | bytes accessed | tf_op | source)
XLA Modules:
  0.0 95.0 jit_solution(14662368461941971309)
XLA Ops:
  0.6 0.0 copy-start.3
  0.6 0.8 copy-done.3
  1.5 0.0 copy-start
  1.5 0.0 copy-start.1
  1.5 0.0 copy-start.2
  1.5 4.4 %shard_map.75 = (f32[256,128]{1,0:T(8,128)S(1)}, f32[256,128]{1,0:T(8,128)S(1)}, f32[256,256]{1,0:T(8,128)S(1)}) custom-call(bf16[256,128]{1,0:T(8,128)(2,1)S(1)} %copy-done.3), custom_call_target="tpu_custom_call" | custom-call | flops 4000000000 | bytes 4000000 | tf_op jit(solution)/shard_map/pallas_call | solution.py:267
  5.9 0.0 copy-done
  5.9 0.0 copy-done.1
  5.9 0.0 copy-done.2
  5.9 1.7 %shard_map.76 = (f32[128,640]{1,0:T(8,128)S(1)}, f32[256,128]{1,0:T(8,128)S(1)}, f32[256,256]{1,0:T(8,128)S(1)}) custom-call(s32[1]{0:T(128)} %bitcast.index_ref, f32[256,128]{1,0:T(8,128)S(1)} %get-tuple-element.22.k_ref, f32[256,256]{1,0:T(8,128)S(1)} %get-tuple-element.23.inv_ref, bf16[512,128]{1,0:T(8,128)(2,1)S(1)} %bitcast.18, ...), custom_call_target="tpu_custom_call" | custom-call | tf_op jit(solution)/shard_map/pallas_call | solution.py:267
  7.6 2.3 %all-gather = f32[256,640]{1,0:T(8,128)S(1)} all-gather(f32[128,640]{1,0:T(8,128)S(1)} %get-tuple-element.24), channel_id=2, replica_groups={{0,16},{32,48},{64,80},{96,112},{128,144},{160,176},{192,208},{224,240}..., dimensions={0}, use_global_device_ids=true | all-gather | bytes 983040 | tf_op jit(solution)/shard_map/all_gather | solution.py:280
  9.9 0.2 shard_map.77
  10.1 20.8 %all-gather.1 = f32[512,384]{1,0:T(8,128)S(1)} all-gather(f32[128,384]{1,0:T(8,128)S(1)} %shard_map.77), channel_id=3, replica_groups={{0,32,64,96},{16,48,80,112},{128,160,192,224},{144,176,208,240},{256,28..., dimensions={0}, use_global_device_ids=true | all-gather | bytes 983040 | tf_op jit(solution)/shard_map/all_gather | solution.py:280
  31.0 0.5 shard_map.78
  31.5 9.1 %collective-permute-start = (f32[128,128]{1,0:T(8,128)S(1)}, f32[128,128]{1,0:T(8,128)S(1)}, u32[]{:S(2)}, u32[]{:S(2)}) collective-permute-start(f32[128,128]{1,0:T(8,128)S(1)} %get-tuple-element.25.sent_ref), channel_id=1, source_target_pairs={{0,128},{16,144},{32,160},{48,176},{64,192},{80,208},{96,224},{112... | collective-permute-start | bytes 196616 | tf_op jit(solution)/shard_map/ppermute | solution.py:293
  40.6 1.9 %collective-permute-done.got_ref.first_ref = f32[128,128]{1,0:T(8,128)S(1)} collective-permute-done((f32[128,128]{1,0:T(8,128)S(1)}, f32[128,128]{1,0:T(8,128)S(1)}, u32[]{:S(2)}, u32[]{:S(2)}) %collective-permute-start) | collective-permute-done | bytes 65568 | tf_op jit(solution)/shard_map/ppermute | solution.py:293
  42.5 0.2 shard_map.79
  42.7 0.7 collective-permute-start.1
  43.4 0.0 collective-permute-done.1.got_ref.second_ref
  43.4 0.2 shard_map.80
  43.6 1.3 %collective-permute-start.2 = (f32[128,128]{1,0:T(8,128)S(1)}, f32[128,128]{1,0:T(8,128)S(1)}, u32[]{:S(2)}, u32[]{:S(2)}) collective-permute-start(f32[128,128]{1,0:T(8,128)S(1)} %shard_map.80), channel_id=1, source_target_pairs={{256,384},{272,400},{288,416},{304,432},{320,448},{336,464},{352,4... | collective-permute-start | bytes 196616 | tf_op jit(solution)/shard_map/ppermute | solution.py:293
  44.9 1.3 %shard_map.83 = (f32[256,128]{1,0:T(8,128)S(1)}, f32[256,256]{1,0:T(8,128)S(1)}) custom-call(s32[1]{0:T(128)} %bitcast.index_ref, f32[128,128]{1,0:T(8,128)S(1)} %get-tuple-element.25.sent_ref, f32[256,128]{1,0:T(8,128)S(1)} %get-tuple-element.22.k_ref, f32[256,256]{1,0:T(8,128)S(1)} %get-tuple-element.23.inv_ref, bf16[512,128]{1,0:T(8,128)(2,1)S(1)} %bitcast.19, ...), custom_call_target="tpu_custom_call" | custom-call | flops 500000000 | bytes 1000000 | tf_op jit(solution)/shard_map/pallas_call | solution.py:267
  46.2 0.3 shard_map.81.track_ref
  46.5 17.8 %collective-permute-done.2.third_ref = f32[128,128]{1,0:T(8,128)S(1)} collective-permute-done((f32[128,128]{1,0:T(8,128)S(1)}, f32[128,128]{1,0:T(8,128)S(1)}, u32[]{:S(2)}, u32[]{:S(2)}) %collective-permute-start.2) | collective-permute-done | bytes 65568 | tf_op jit(solution)/shard_map/ppermute | solution.py:293
  64.3 0.2 shard_map.82
  64.5 2.0 %all-gather.2 = f32[256,256]{1,0:T(8,128)S(1)} all-gather(f32[128,256]{1,0:T(8,128)S(1)} %shard_map.82), channel_id=4, replica_groups={{0,16},{32,48},{64,80},{96,112},{128,144},{160,176},{192,208},{224,240}..., dimensions={0}, use_global_device_ids=true | all-gather | bytes 393216 | tf_op jit(solution)/shard_map/all_gather | solution.py:280
  66.5 1.7 %shard_map.84 = (f32[256,128]{1,0:T(8,128)S(1)}, f32[128,256]{1,0:T(8,128)S(1)}, f32[256,256]{1,0:T(8,128)S(1)}, f32[256,256]{1,0:T(8,128)S(1)}) custom-call(s32[1]{0:T(128)} %bitcast.index_ref, f32[2,128,640]{2,1,0:T(8,128)S(1)} %bitcast.13, f32[2,128,256]{2,1,0:T(8,128)S(1)} %bitcast.16, bf16[512,128]{1,0:T(8,128)(2,1)S(1)} %bitcast.20, ...), custom_call_target="tpu_custom_call" | custom-call | tf_op jit(solution)/shard_map/pallas_call | solution.py:267
  68.2 13.9 %all_to_all.10.got_ref = f32[16,16,128]{2,1,0:T(8,128)S(1)} all-to-all(f32[16,16,128]{2,1,0:T(8,128)S(1)} %bitcast.26), channel_id=1, replica_groups=mesh['seq'=32,'head'=16] {'head'}, dimensions={0} | all-to-all | bytes 262144 | tf_op jit(solution)/shard_map/all_to_all | solution.py:339
  82.1 0.7 shard_map.86
  82.8 4.8 %all-to-all-start.1 = ((f32[16,16,128]{2,1,0:T(8,128)}), f32[16,16,128]{2,1,0:T(8,128)S(1)}, u32[]{:S(2)}, u32[]{:S(2)}) async-start(f32[16,16,128]{2,1,0:T(8,128)} %shard_map.86), calls=%async_computation.1 | async-start | bytes 262144 | tf_op jit(solution)/shard_map/all_to_all | solution.py:348
  87.6 2.1 %shard_map.85 = (bf16[512,128]{1,0:T(8,128)(2,1)}, bf16[512,128]{1,0:T(8,128)(2,1)}, bf16[512,128]{1,0:T(8,128)(2,1)}) custom-call(s32[1]{0:T(128)} %bitcast.index_ref, bf16[512,128]{1,0:T(8,128)(2,1)S(1)} %bitcast.21, bf16[512,128]{1,0:T(8,128)(2,1)S(1)} %bitcast.25, f32[256,128]{1,0:T(8,128)S(1)} %get-tuple-element.22.k_ref, ...), custom_call_target="tpu_custom_call" | custom-call | flops 4000000000 | bytes 4000000 | tf_op jit(solution)/shard_map/pallas_call | solution.py:267
  89.7 4.6 %all-to-all-done.1 = f32[16,16,128]{2,1,0:T(8,128)S(1)} async-done(((f32[16,16,128]{2,1,0:T(8,128)}), f32[16,16,128]{2,1,0:T(8,128)S(1)}, u32[]{:S(2)}, u32[]{:S(2)}) %all-to-all-start.1) | async-done | bytes 131104 | tf_op jit(solution)/shard_map/all_to_all | solution.py:348
  94.3 0.7 shard_map.87
Async XLA Ops:
  0.6 0.8 copy-start.3
  1.5 4.4 %copy-start = (bf16[256,2,128]{2,1,0:T(2,128)(2,1)S(1)}, bf16[256,2,128]{2,1,0:T(2,128)(2,1)}, u32[]{:S(2)}) copy-start(bf16[256,2,128]{2,1,0:T(2,128)(2,1)} %param.4) | copy-start | bytes 393220
  1.5 4.4 %copy-start.1 = (bf16[256,2,128]{2,1,0:T(2,128)(2,1)S(1)}, bf16[256,2,128]{2,1,0:T(2,128)(2,1)}, u32[]{:S(2)}) copy-start(bf16[256,2,128]{2,1,0:T(2,128)(2,1)} %param.7) | copy-start | bytes 393220
  1.5 4.4 %copy-start.2 = (bf16[256,2,128]{2,1,0:T(2,128)(2,1)S(1)}, bf16[256,2,128]{2,1,0:T(2,128)(2,1)}, u32[]{:S(2)}) copy-start(bf16[256,2,128]{2,1,0:T(2,128)(2,1)} %param.6) | copy-start | bytes 393220
  31.5 11.0 %collective-permute-start = (f32[128,128]{1,0:T(8,128)S(1)}, f32[128,128]{1,0:T(8,128)S(1)}, u32[]{:S(2)}, u32[]{:S(2)}) collective-permute-start(f32[128,128]{1,0:T(8,128)S(1)} %get-tuple-element.25.sent_ref), channel_id=1, source_target_pairs={{0,128},{16,144},{32,160},{48,176},{64,192},{80,208},{96,224},{112... | collective-permute-start | bytes 196616 | tf_op jit(solution)/shard_map/ppermute | solution.py:293
  42.7 0.7 collective-permute-start.1
  43.6 20.7 %collective-permute-start.2 = (f32[128,128]{1,0:T(8,128)S(1)}, f32[128,128]{1,0:T(8,128)S(1)}, u32[]{:S(2)}, u32[]{:S(2)}) collective-permute-start(f32[128,128]{1,0:T(8,128)S(1)} %shard_map.80), channel_id=1, source_target_pairs={{256,384},{272,400},{288,416},{304,432},{320,448},{336,464},{352,4... | collective-permute-start | bytes 196616 | tf_op jit(solution)/shard_map/ppermute | solution.py:293
  82.8 11.5 %all-to-all-start.1 = ((f32[16,16,128]{2,1,0:T(8,128)}), f32[16,16,128]{2,1,0:T(8,128)S(1)}, u32[]{:S(2)}, u32[]{:S(2)}) async-start(f32[16,16,128]{2,1,0:T(8,128)} %shard_map.86), calls=%async_computation.1 | async-start | bytes 262144 | tf_op jit(solution)/shard_map/all_to_all | solution.py:348

commit v5 on v4

--- a/solution.py
+++ b/solution.py
@@ -1,5 +1,3 @@
-import functools
-
 import jax
 import jax.numpy as jnp
 from jax import lax
@@ -125,69 +123,65 @@
     z_ref[...] = mm(inv_t, split(jnp.concatenate(back, axis=1)))
 
 
+def then(first, second):
+    step = mm(split(second[:, :D]), split(first))
+    return jnp.concatenate([step[:, :D], step[:, D:] + second[:, D:]], axis=1)
+
+
+def along(index_ref, size, unit):
+    place = (index_ref[0] // unit) % size
+    return jnp.where(index_ref[0] % 2 == 1, size - 1 - place, place)
+
+
 def pair_kernel(index_ref, got_ref, send_ref):
-    core = index_ref[0] % 2
-    at_b = pl.ds(pl.multiple_of(D + core * D, D), D)
-    at_g = pl.ds(pl.multiple_of(3 * D + core * D, D), D)
-    low, up = got_ref[0, :, :D], got_ref[1, :, :D]
-    ahead = mm(split(up), split(jnp.concatenate([low, got_ref[0, :, at_b]], axis=1)))
-    send_ref[:, :D] = ahead[:, :D]
-    send_ref[:, D : 2 * D] = ahead[:, D:] + got_ref[1, :, at_b]
-    send_ref[:, 2 * D :] = got_ref[0, :, at_g] + mm(split(low.T), split(got_ref[1, :, at_g]))
-
-
-def joined(low, up):
-    ahead = mm(split(up[:, :D]), split(low[:, : 2 * D]))
-    state = ahead[:, D:] + up[:, D : 2 * D]
-    gradient = low[:, 2 * D :] + mm(split(low[:, :D].T), split(up[:, 2 * D :]))
-    return jnp.concatenate([ahead[:, :D], state, gradient], axis=1)
-
-
-def block_kernel(index_ref, got_ref, send_ref, block_ref, halves_ref):
-    block = index_ref[0] // 8
-    low = joined(got_ref[0], got_ref[1])
-    up = joined(got_ref[2], got_ref[3])
-    halves_ref[0] = low
-    halves_ref[1] = up
-    whole = joined(low, up)
+    down = index_ref[0] % 2 == 1
+
+    def ranges(i):
+        return jnp.concatenate(
+            [
+                jnp.where(down, got_ref[1 - i, :, :D].T, got_ref[i, :, :D]),
+                jnp.where(down, got_ref[1 - i, :, 3 * D :], got_ref[i, :, D : 3 * D]),
+            ],
+            axis=1,
+        )
+
+    send_ref[...] = then(ranges(0), ranges(1))
+
+
+def chip_kernel(index_ref, got_ref, send_ref):
+    down, right = index_ref[0] % 2 == 1, (index_ref[0] // 2) % 2 == 1
+    first, second = [halved(jnp.where(down, got_ref[1 - i], got_ref[i]), right) for i in range(2)]
+    send_ref[...] = then(first, second)
+
+
+def halved(x, right):
+    return jnp.concatenate([x[:, :D], jnp.where(right, x[:, 2 * D :], x[:, D : 2 * D])], axis=1)
+
+
+def block_kernel(index_ref, got_ref, send_ref, block_ref):
+    down = index_ref[0] % 2 == 1
+    first, second = [jnp.where(down, got_ref[1 - i], got_ref[i]) for i in range(2)]
+    whole = then(first, second)
     block_ref[...] = whole
-    send_ref[...] = jnp.where(block == 3, whole[:, 2 * D :], whole[:, D : 2 * D])
-
-
-def place_kernel(index_ref, sent_ref, got_ref, halves_ref, track_ref):
-    del sent_ref
-    chip = (index_ref[0] // 2) % 4
-    eye = jnp.where(iota((D, D), 0) == iota((D, D), 1), 1.0, 0.0)
-    blank = jnp.concatenate([eye, jnp.zeros((D, D), F32)], axis=1)
-    below = halves_ref[0, :, : 2 * D]
-    above = jnp.concatenate([halves_ref[1, :, :D].T, halves_ref[1, :, 2 * D :]], axis=1)
-    outer = chip == 3
-    step = mm(
-        split(jnp.where(outer, got_ref[2, :, :D], got_ref[1, :, :D].T)), split(jnp.where(outer, below, above))
-    )
-    add = jnp.where(outer, got_ref[2, :, D : 2 * D], got_ref[1, :, 2 * D :])
-    step = jnp.concatenate([step[:, :D], step[:, D:] + add], axis=1)
-    track_ref[0] = jnp.where(
-        chip == 0, blank, jnp.where(chip == 1, got_ref[0, :, : 2 * D], jnp.where(chip == 2, below, step))
-    )
-    last = jnp.concatenate([got_ref[3, :, :D].T, got_ref[3, :, 2 * D :]], axis=1)
-    track_ref[1] = jnp.where(chip == 3, blank, jnp.where(chip == 2, last, jnp.where(chip == 1, above, step)))
-
-
-def hop_kernel(downward, index_ref, got_ref, block_ref, send_ref):
-    down = index_ref[0] // 8 == downward
-    whole = block_ref[:, :D]
-    own = jnp.where(down, block_ref[:, 2 * D :], block_ref[:, D : 2 * D])
-    send_ref[...] = own + mm(split(jnp.where(down, whole.T, whole)), split(got_ref[...]))
-
-
-def top_kernel(index_ref, first_ref, second_ref, third_ref, track_ref, send_ref):
-    block = index_ref[0] // 8
-    first, second, third = first_ref[...], second_ref[...], third_ref[...]
-    state = jnp.where(block == 1, first, jnp.where(block == 2, second, jnp.where(block == 3, third, 0.0)))
-    adjoint = jnp.where(block == 2, first, jnp.where(block == 1, second, jnp.where(block == 0, third, 0.0)))
-    send_ref[:, :D] = track_ref[0, :, D:] + mm(split(track_ref[0, :, :D]), split(state))
-    send_ref[:, D:] = track_ref[1, :, D:] + mm(split(track_ref[1, :, :D]), split(adjoint))
+    send_ref[...] = whole[:, D:]
+
+
+def hop_kernel(got_ref, block_ref, send_ref):
+    send_ref[...] = block_ref[:, D:] + mm(split(block_ref[:, :D]), split(got_ref[...]))
+
+
+def top_kernel(index_ref, first_ref, second_ref, third_ref, units_ref, chips_ref, send_ref):
+    down, right = index_ref[0] % 2 == 1, (index_ref[0] // 2) % 2 == 1
+    place = along(index_ref, 4, 8)
+    got = jnp.where(
+        place == 1, first_ref[...], jnp.where(place == 2, second_ref[...], jnp.where(place == 3, third_ref[...], 0.0))
+    )
+    unit = jnp.where(down, units_ref[1], units_ref[0])
+    later = unit[:, D:] + mm(split(unit[:, :D]), split(got))
+    got = jnp.where(along(index_ref, 2, 4) == 1, later, got)
+    send_ref[:, :D] = got
+    chip = halved(jnp.where(down, chips_ref[1], chips_ref[0]), right)
+    send_ref[:, D:] = chip[:, D:] + mm(split(chip[:, :D]), split(got))
 
 
 def after_kernel(index_ref, pair_ref, got_ref, q_ref, d_ref, k_ref, w_ref, m_ref, x0_ref, z0_ref,
@@ -196,8 +190,13 @@
     ds_ref[...] = d_ref[...].astype(F32)
     rows = [pl.ds(head, T, stride=2) for head in range(2)]
     upper = index_ref[0] % 2 == 1
-    state = jnp.concatenate([got_ref[0, :, :D], got_ref[1, :, :D]], axis=1)
-    adjoint = jnp.concatenate([got_ref[0, :, D:], got_ref[1, :, D:]], axis=1)
+    right = (index_ref[0] // 2) % 2 == 1
+    state, adjoint = [
+        jnp.concatenate(
+            [jnp.where(right == flip, got_ref[i, :, :D], got_ref[i, :, D:]) for i in (core, core + 2)], axis=1
+        )
+        for core, flip in ((0, False), (1, True))
+    ]
     step = mm(
         split(jnp.where(upper, pair_ref[0, :, :D], pair_ref[1, :, :D].T)),
         split(jnp.where(upper, state, adjoint)),
@@ -289,8 +288,9 @@
     return groups
 
 
-def hop(x, *moves):
-    return lax.ppermute(x, "seq", [(8 * a + i, 8 * b + i) for a, b in moves for i in range(8)])
+def hop(x, place):
+    up = [(8 * place + i, 8 * place + i + 8) for i in range(0, 8, 2)]
+    return lax.ppermute(x, "seq", up + [(PARTS - 1 - a, PARTS - 1 - b) for a, b in up])
 
 
 def shards(queries, raw_keys, values, cotangent):
@@ -310,12 +310,11 @@
     )
     pair = exchange(send, near(0, 1))
     send = call(pair_kernel, ((D, 3 * D), F32), index, pair)
-    chips = exchange(send, near(0, 2, 4, 6))
-    send, block, halves = call(
-        block_kernel, [((D, D), F32), ((D, 3 * D), F32), ((2, D, 3 * D), F32)], index, chips
-    )
-    first = hop(send, (0, 1), (3, 2))
-    track = call(place_kernel, ((2, D, 2 * D), F32), index, send, chips, halves, cost=SHORT)
+    chips = exchange(send, near(0, 2))
+    send = call(chip_kernel, ((D, 2 * D), F32), index, chips)
+    units = exchange(send, near(0, 4))
+    send, block = call(block_kernel, [((D, D), F32), ((D, 2 * D), F32)], index, units)
+    first = hop(send, 0)
     m, z0 = call(
         side_kernel,
         [((T, D), F32), ((T, 2 * D), F32)],
@@ -323,12 +322,12 @@
         scratch=[wide] * 2,
         cost=SHORT,
     )
-    send = call(functools.partial(hop_kernel, 2), ((D, D), F32), index, first, block)
-    second = hop(send, (1, 2), (2, 1))
-    send = call(functools.partial(hop_kernel, 1), ((D, D), F32), index, second, block)
-    third = hop(send, (2, 3), (1, 0))
-    send = call(top_kernel, ((D, 2 * D), F32), index, first, second, third, track)
-    got = exchange(send, near(0, 1))
+    send = call(hop_kernel, ((D, D), F32), first, block, scalars=0)
+    second = hop(send, 1)
+    send = call(hop_kernel, ((D, D), F32), second, block, scalars=0)
+    third = hop(send, 2)
+    send = call(top_kernel, ((D, 2 * D), F32), index, first, second, third, units, chips)
+    got = exchange(send, near(0, 1, 2, 3))
     gk, state, x, z = call(
         after_kernel,
         [((T, D), F32), ((D, 2 * D), F32), ((T, 2 * D), F32), ((T, 2 * D), F32)],

time: 95.3 us -> 91.7 us (0.962)
  the two profiles are of different devices: /device:TPU:2 before, /device:TPU:32 now
where the time goes in v5:
time: 91.7 us; the launch traced here: 91.4 us
  blocking collectives  55.6 us (61%)
  Pallas kernels  14.1 us (15%)
  starting transfers between devices  12.4 us (14%)
  waiting for transfers between devices  7.71 us (8%)
    all_gather x4, blocking collectives, exchange(): return lax.all_gather(x, 'seq', axis_index_groups=groups)  40.8 us
    all_to_all x1, blocking collectives, shards(): pieces = lax.all_to_all(gk.reshape(peers, T // peers, D), 'head', 0, 0)  14.8 us
    pallas_call x13, Pallas kernels, call(): pl.pallas_call(kernel, out_shape=[jax.ShapeDtypeStruct(*s) for s in shape...  14.1 us
    ppermute x3, starting transfers between devices, hop(): lax.ppermute(x, 'seq', up + [(PARTS - 1 - a, PARTS - 1 - b) for a, b in up])  8.86 us
    all_to_all x1, waiting for transfers between devices, shards(): total = lax.all_to_all(totals, 'head', 0, 0).reshape(T, D)  5.82 us
    all_to_all x1, starting transfers between devices, shards(): total = lax.all_to_all(totals, 'head', 0, 0).reshape(T, D)  3.51 us
    ppermute x3, waiting for transfers between devices, hop(): lax.ppermute(x, 'seq', up + [(PARTS - 1 - a, PARTS - 1 - b) for a, b in up])  1.89 us
  transfers between devices with their start and end apart: 4, of which 2 were waited for; matrix products, arithmetic and copies ran while one was open for 0% of the time, Pallas kernels for 4%

profile of v5, /device:TPU:32, one launch (start us, length us, event | category | flops | bytes accessed | tf_op | source)
XLA Modules:
  0.0 91.4 jit_solution(17280985332924558955)
XLA Ops:
  0.6 0.0 copy-start.3
  0.6 0.8 copy-done.3
  1.5 0.0 copy-start
  1.5 0.0 copy-start.1
  1.5 0.0 copy-start.2
  1.5 4.4 %shard_map.75 = (f32[256,128]{1,0:T(8,128)S(1)}, f32[256,128]{1,0:T(8,128)S(1)}, f32[256,256]{1,0:T(8,128)S(1)}) custom-call(bf16[256,128]{1,0:T(8,128)(2,1)S(1)} %copy-done.3), custom_call_target="tpu_custom_call" | custom-call | flops 4000000000 | bytes 4000000 | tf_op jit(solution)/shard_map/pallas_call | solution.py:266
  5.9 0.0 copy-done
  5.9 0.0 copy-done.1
  5.9 0.0 copy-done.2
  5.9 1.7 %shard_map.76 = (f32[128,640]{1,0:T(8,128)S(1)}, f32[256,128]{1,0:T(8,128)S(1)}, f32[256,256]{1,0:T(8,128)S(1)}) custom-call(s32[1]{0:T(128)} %bitcast.index_ref, f32[256,128]{1,0:T(8,128)S(1)} %get-tuple-element.21.k_ref, f32[256,256]{1,0:T(8,128)S(1)} %get-tuple-element.22.inv_ref, bf16[512,128]{1,0:T(8,128)(2,1)S(1)} %bitcast.21, ...), custom_call_target="tpu_custom_call" | custom-call | tf_op jit(solution)/shard_map/pallas_call | solution.py:266
  7.6 2.3 %all-gather = f32[256,640]{1,0:T(8,128)S(1)} all-gather(f32[128,640]{1,0:T(8,128)S(1)} %get-tuple-element.23), channel_id=2, replica_groups={{0,16},{32,48},{64,80},{96,112},{128,144},{160,176},{192,208},{224,240}..., dimensions={0}, use_global_device_ids=true | all-gather | bytes 983040 | tf_op jit(solution)/shard_map/all_gather | solution.py:279
  9.9 0.3 shard_map.77
  10.2 11.3 %all-gather.1 = f32[256,384]{1,0:T(8,128)S(1)} all-gather(f32[128,384]{1,0:T(8,128)S(1)} %shard_map.77), channel_id=3, replica_groups={{0,32},{16,48},{64,96},{80,112},{128,160},{144,176},{192,224},{208,240}..., dimensions={0}, use_global_device_ids=true | all-gather | bytes 589824 | tf_op jit(solution)/shard_map/all_gather | solution.py:279
  21.5 0.2 shard_map.78
  21.7 6.7 %all-gather.2 = f32[256,256]{1,0:T(8,128)S(1)} all-gather(f32[128,256]{1,0:T(8,128)S(1)} %shard_map.78), channel_id=4, replica_groups={{0,64},{16,80},{32,96},{48,112},{128,192},{144,208},{160,224},{176,240}..., dimensions={0}, use_global_device_ids=true | all-gather | bytes 393216 | tf_op jit(solution)/shard_map/all_gather | solution.py:279
  28.4 0.2 shard_map.79
  28.6 7.5 %collective-permute-start = (f32[128,128]{1,0:T(8,128)S(1)}, f32[128,128]{1,0:T(8,128)S(1)}, u32[]{:S(2)}, u32[]{:S(2)}) collective-permute-start(f32[128,128]{1,0:T(8,128)S(1)} %get-tuple-element.24.sent_ref), channel_id=1, source_target_pairs={{0,128},{32,160},{64,192},{96,224},{496,368},{464,336},{432,304},{... | collective-permute-start | bytes 196616 | tf_op jit(solution)/shard_map/ppermute | solution.py:293
  36.2 1.9 %collective-permute-done.got_ref.first_ref = f32[128,128]{1,0:T(8,128)S(1)} collective-permute-done((f32[128,128]{1,0:T(8,128)S(1)}, f32[128,128]{1,0:T(8,128)S(1)}, u32[]{:S(2)}, u32[]{:S(2)}) %collective-permute-start) | collective-permute-done | bytes 65568 | tf_op jit(solution)/shard_map/ppermute | solution.py:293
  38.1 0.2 shard_map.80
  38.3 0.7 collective-permute-start.1
  38.9 0.0 collective-permute-done.1.got_ref.second_ref
  38.9 0.2 shard_map.81
  39.1 0.7 collective-permute-start.2
  39.8 1.3 %shard_map.83 = (f32[256,128]{1,0:T(8,128)S(1)}, f32[256,256]{1,0:T(8,128)S(1)}) custom-call(s32[1]{0:T(128)} %bitcast.index_ref, f32[128,128]{1,0:T(8,128)S(1)} %get-tuple-element.24.sent_ref, f32[256,128]{1,0:T(8,128)S(1)} %get-tuple-element.21.k_ref, f32[256,256]{1,0:T(8,128)S(1)} %get-tuple-element.22.inv_ref, bf16[512,128]{1,0:T(8,128)(2,1)S(1)} %bitcast.22, ...), custom_call_target="tpu_custom_call" | custom-call | flops 500000000 | bytes 1000000 | tf_op jit(solution)/shard_map/pallas_call | solution.py:266
  41.1 0.0 collective-permute-done.2.third_ref
  41.1 0.4 shard_map.82
  41.5 20.5 %all-gather.3 = f32[512,256]{1,0:T(8,128)S(1)} all-gather(f32[128,256]{1,0:T(8,128)S(1)} %shard_map.82), channel_id=5, replica_groups={{0,16,32,48},{64,80,96,112},{128,144,160,176},{192,208,224,240},{256,27..., dimensions={0}, use_global_device_ids=true | all-gather | bytes 655360 | tf_op jit(solution)/shard_map/all_gather | solution.py:279
  62.0 1.7 %shard_map.84 = (f32[256,128]{1,0:T(8,128)S(1)}, f32[128,256]{1,0:T(8,128)S(1)}, f32[256,256]{1,0:T(8,128)S(1)}, f32[256,256]{1,0:T(8,128)S(1)}) custom-call(s32[1]{0:T(128)} %bitcast.index_ref, f32[2,128,640]{2,1,0:T(8,128)S(1)} %bitcast.14, f32[4,128,256]{2,1,0:T(8,128)S(1)} %bitcast.19, bf16[512,128]{1,0:T(8,128)(2,1)S(1)} %bitcast.23, ...), custom_call_target="tpu_custom_call" | custom-call | tf_op jit(solution)/shard_map/pallas_call | solution.py:266
  63.7 14.8 %all_to_all.10.got_ref = f32[16,16,128]{2,1,0:T(8,128)S(1)} all-to-all(f32[16,16,128]{2,1,0:T(8,128)S(1)} %bitcast.29), channel_id=1, replica_groups=mesh['seq'=32,'head'=16] {'head'}, dimensions={0} | all-to-all | bytes 262144 | tf_op jit(solution)/shard_map/all_to_all | solution.py:338
  78.5 0.7 shard_map.86
  79.2 3.5 %all-to-all-start.1 = ((f32[16,16,128]{2,1,0:T(8,128)}), f32[16,16,128]{2,1,0:T(8,128)S(1)}, u32[]{:S(2)}, u32[]{:S(2)}) async-start(f32[16,16,128]{2,1,0:T(8,128)} %shard_map.86), calls=%async_computation.1 | async-start | bytes 262144 | tf_op jit(solution)/shard_map/all_to_all | solution.py:347
  82.7 2.1 %shard_map.85 = (bf16[512,128]{1,0:T(8,128)(2,1)}, bf16[512,128]{1,0:T(8,128)(2,1)}, bf16[512,128]{1,0:T(8,128)(2,1)}) custom-call(s32[1]{0:T(128)} %bitcast.index_ref, bf16[512,128]{1,0:T(8,128)(2,1)S(1)} %bitcast.24, bf16[512,128]{1,0:T(8,128)(2,1)S(1)} %bitcast.28, f32[256,128]{1,0:T(8,128)S(1)} %get-tuple-element.21.k_ref, ...), custom_call_target="tpu_custom_call" | custom-call | flops 4000000000 | bytes 4000000 | tf_op jit(solution)/shard_map/pallas_call | solution.py:266
  84.8 5.8 %all-to-all-done.1 = f32[16,16,128]{2,1,0:T(8,128)S(1)} async-done(((f32[16,16,128]{2,1,0:T(8,128)}), f32[16,16,128]{2,1,0:T(8,128)S(1)}, u32[]{:S(2)}, u32[]{:S(2)}) %all-to-all-start.1) | async-done | bytes 131104 | tf_op jit(solution)/shard_map/all_to_all | solution.py:347
  90.7 0.7 shard_map.87
Async XLA Ops:
  0.6 0.8 copy-start.3
  1.5 4.4 %copy-start = (bf16[256,2,128]{2,1,0:T(2,128)(2,1)S(1)}, bf16[256,2,128]{2,1,0:T(2,128)(2,1)}, u32[]{:S(2)}) copy-start(bf16[256,2,128]{2,1,0:T(2,128)(2,1)} %param.4) | copy-start | bytes 393220
  1.5 4.4 %copy-start.1 = (bf16[256,2,128]{2,1,0:T(2,128)(2,1)S(1)}, bf16[256,2,128]{2,1,0:T(2,128)(2,1)}, u32[]{:S(2)}) copy-start(bf16[256,2,128]{2,1,0:T(2,128)(2,1)} %param.7) | copy-start | bytes 393220
  1.5 4.4 %copy-start.2 = (bf16[256,2,128]{2,1,0:T(2,128)(2,1)S(1)}, bf16[256,2,128]{2,1,0:T(2,128)(2,1)}, u32[]{:S(2)}) copy-start(bf16[256,2,128]{2,1,0:T(2,128)(2,1)} %param.6) | copy-start | bytes 393220
  28.6 9.4 %collective-permute-start = (f32[128,128]{1,0:T(8,128)S(1)}, f32[128,128]{1,0:T(8,128)S(1)}, u32[]{:S(2)}, u32[]{:S(2)}) collective-permute-start(f32[128,128]{1,0:T(8,128)S(1)} %get-tuple-element.24.sent_ref), channel_id=1, source_target_pairs={{0,128},{32,160},{64,192},{96,224},{496,368},{464,336},{432,304},{... | collective-permute-start | bytes 196616 | tf_op jit(solution)/shard_map/ppermute | solution.py:293
  38.3 0.7 collective-permute-start.1
  39.1 2.0 %collective-permute-start.2 = (f32[128,128]{1,0:T(8,128)S(1)}, f32[128,128]{1,0:T(8,128)S(1)}, u32[]{:S(2)}, u32[]{:S(2)}) collective-permute-start(f32[128,128]{1,0:T(8,128)S(1)} %shard_map.81), channel_id=1, source_target_pairs={{256,384},{288,416},{320,448},{352,480},{240,112},{208,80},{176,48... | collective-permute-start | bytes 196616 | tf_op jit(solution)/shard_map/ppermute | solution.py:293
  79.2 11.5 %all-to-all-start.1 = ((f32[16,16,128]{2,1,0:T(8,128)}), f32[16,16,128]{2,1,0:T(8,128)S(1)}, u32[]{:S(2)}, u32[]{:S(2)}) async-start(f32[16,16,128]{2,1,0:T(8,128)} %shard_map.86), calls=%async_computation.1 | async-start | bytes 262144 | tf_op jit(solution)/shard_map/all_to_all | solution.py:347

commit v6 on v5

--- a/solution.py
+++ b/solution.py
@@ -40,17 +40,33 @@
     return lax.broadcasted_iota(jnp.int32, shape, dim)
 
 
-def inverse(lower, size):
+def inverses(lowers, size):
     row, col = iota((size, size), 0), iota((size, size), 1)
     level = row ^ col
-    inv = jnp.where(row == col, 1.0, jnp.where((level == 1), -lower, 0.0))
-    step = 2
+
+    def part(low, high):
+        return [jnp.where((level >= low) & (level < high), lower, 0.0) for lower in lowers]
+
+    edges = part(1, 4)
+    starts = [jnp.where(row == col, 1.0, -edge) for edge in edges]
+    edges = [split(edge) for edge in edges]
+    squares = [split(mm(edge, edge)) for edge in edges]
+    invs = [start + mm(square, split(start)) for start, square in zip(starts, squares)]
+    step = 4
     while step < size:
-        part = jnp.where((level >= step) & (level < 2 * step), lower, 0.0)
-        inv_pair = split(inv)
-        inv = inv - mm(inv_pair, split(mm(split(part), inv_pair)))
-        step *= 2
-    return inv
+        pairs = [split(inv) for inv in invs]
+        if 4 * step <= size:
+            edges = [split(mm(pair, split(edge))) for pair, edge in zip(pairs, part(step, 4 * step))]
+            starts = [mm(edge, pair) for edge, pair in zip(edges, pairs)]
+            squares = [mm(edge, edge) for edge in edges]
+            starts = [inv - start for inv, start in zip(invs, starts)]
+            invs = [start + mm(split(square), split(start)) for start, square in zip(starts, squares)]
+            step *= 4
+        else:
+            edges = [split(mm(split(edge), pair)) for pair, edge in zip(pairs, part(step, 2 * step))]
+            invs = [inv - mm(pair, edge) for inv, pair, edge in zip(invs, pairs, edges)]
+            step *= 2
+    return invs
 
 
 def places_root(index):
@@ -69,8 +85,7 @@
     row, col = iota((T, T), 0), iota((T, T), 1)
     lower = jnp.where(row > col, 2.0 * gram, 0.0)
     half = T // 2
-    first = inverse(lower[:half, :half], half)
-    second = inverse(lower[half:, half:], half)
+    first, second = inverses([lower[:half, :half], lower[half:, half:]], half)
     corner = -mm(split(second), split(mm(split(lower[half:, :half]), split(first))))
     inv_ref[:half, :half] = first
     inv_ref[:half, half:] = jnp.zeros((half, half), F32)
@@ -94,20 +109,21 @@
     root = places_root(index_ref[0])
     key = k_ref[...]
     keys, invs, keys_t = split(key), split(inv_ref[...]), split(key.T)
+    queries = [qs_ref[r, :] for r in rows]
+    scores = [causal_scores(query, keys, root) for query in queries]
     w = 2.0 * mm(invs, keys)
+    x0 = mm(invs, exact(jnp.concatenate([vs_ref[r, :] for r in rows], axis=1).astype(BF16)))
     w_ref[...] = w
-    ws = split(w)
+    x_ref[...] = x0
+    ws, x0s = split(w), split(x0)
+    mixed = [mm(split(score), ws) for score in scores]
     eye = jnp.where(iota((D, D), 0) == iota((D, D), 1), 1.0, 0.0)
     send_ref[:, :D] = eye - mm(keys_t, ws)
-    value = jnp.concatenate([vs_ref[r, :] for r in rows], axis=1).astype(BF16)
-    x0 = mm(invs, exact(value))
-    x_ref[...] = x0
-    send_ref[:, D : 3 * D] = mm(keys_t, split(x0))
-    for head in range(2):
-        query = qs_ref[rows[head], :]
-        grad = exact(ds_ref[rows[head], :].astype(BF16))
-        qhat = query * root - mm(split(causal_scores(query, keys, root)), ws)
-        send_ref[:, (3 + head) * D : (4 + head) * D] = mm(split(qhat.T), grad)
+    send_ref[:, D : 3 * D] = mm(keys_t, x0s)
+    qhats = [split((query * root - mix).T) for query, mix in zip(queries, mixed)]
+    grads = [exact(ds_ref[r, :].astype(BF16)) for r in rows]
+    back = [mm(qhat, grad) for qhat, grad in zip(qhats, grads)]
+    send_ref[:, 3 * D :] = jnp.concatenate(back, axis=1)
 
 
 def side_kernel(index_ref, sent_ref, k_ref, inv_ref, q_ref, d_ref, m_ref, z_ref, qs_ref, ds_ref):
@@ -214,14 +230,16 @@
     z = z0_ref[...] + mm(split(m_ref[...]), adjoints)
     z_ref[...] = z
     zs = split(z)
-    edge = jnp.where(row > col, mm(zs, xs, (1, 1)), 0.0)
-    gk = mm(xs, adjoints, (1, 1)) - 2.0 * mm(zs, states, (1, 1)) - 2.0 * mm(split(edge + edge.T), keys)
-    for head in range(2):
-        part = slice(head * D, (head + 1) * D)
-        query = exact(qs_ref[rows[head], :].astype(BF16))
-        grad = exact(ds_ref[rows[head], :].astype(BF16))
-        mix = jnp.where(row >= col, mm(grad, tuple(s[:, part] for s in xs), (1, 1)), 0.0) * root
-        gk = gk + mm(split(mix.T), query)
+    parts = [slice(head * D, (head + 1) * D) for head in range(2)]
+    queries = [exact(qs_ref[r, :].astype(BF16)) for r in rows]
+    grads = [exact(ds_ref[r, :].astype(BF16)) for r in rows]
+    edge = mm(zs, xs, (1, 1))
+    mixed = [mm(grad, tuple(s[:, part] for s in xs), (1, 1)) for grad, part in zip(grads, parts)]
+    gk = mm(xs, adjoints, (1, 1)) - 2.0 * mm(zs, states, (1, 1))
+    edge = jnp.where(row > col, edge, 0.0)
+    mixed = [split((jnp.where(row >= col, mix, 0.0) * root).T) for mix in mixed]
+    last = [mm(mix, query) for mix, query in zip(mixed, queries)]
+    gk = gk - 2.0 * mm(split(edge + edge.T), keys) + last[0] + last[1]
     gk_ref[...] = gk
 
 

time: 91.7 us -> 88.6 us (0.966)
  Pallas kernels: 14.1 us -> 10.9 us
    pallas_call x13, Pallas kernels: 14.1 us -> 10.9 us  [call(): pl.pallas_call(kernel, out_shape=[jax.ShapeDtypeStruct(*s) for s in shape...]
where the time goes in v6:
time: 88.6 us; the launch traced here: 88.3 us
  blocking collectives  55.7 us (63%)
  starting transfers between devices  12.4 us (14%)
  Pallas kernels  10.9 us (12%)
  waiting for transfers between devices  7.72 us (9%)
    all_gather x4, blocking collectives, exchange(): return lax.all_gather(x, 'seq', axis_index_groups=groups)  40.8 us
    all_to_all x1, blocking collectives, shards(): pieces = lax.all_to_all(gk.reshape(peers, T // peers, D), 'head', 0, 0)  14.8 us
    pallas_call x13, Pallas kernels, call(): pl.pallas_call(kernel, out_shape=[jax.ShapeDtypeStruct(*s) for s in shape...  10.9 us
    ppermute x3, starting transfers between devices, hop(): lax.ppermute(x, 'seq', up + [(PARTS - 1 - a, PARTS - 1 - b) for a, b in up])  8.85 us
    all_to_all x1, waiting for transfers between devices, shards(): total = lax.all_to_all(totals, 'head', 0, 0).reshape(T, D)  5.83 us
    all_to_all x1, starting transfers between devices, shards(): total = lax.all_to_all(totals, 'head', 0, 0).reshape(T, D)  3.51 us
    ppermute x3, waiting for transfers between devices, hop(): lax.ppermute(x, 'seq', up + [(PARTS - 1 - a, PARTS - 1 - b) for a, b in up])  1.89 us
  transfers between devices with their start and end apart: 4, of which 2 were waited for; matrix products, arithmetic and copies ran while one was open for 0% of the time, Pallas kernels for 4%

profile of v6, /device:TPU:32, one launch (start us, length us, event | category | flops | bytes accessed | tf_op | source)
XLA Modules:
  0.0 88.3 jit_solution(14575504542291530632)
XLA Ops:
  0.6 0.0 copy-start.3
  0.6 0.8 copy-done.3
  1.5 0.0 copy-start
  1.5 0.0 copy-start.1
  1.5 0.0 copy-start.2
  1.5 2.3 %shard_map.75 = (f32[256,128]{1,0:T(8,128)S(1)}, f32[256,128]{1,0:T(8,128)S(1)}, f32[256,256]{1,0:T(8,128)S(1)}) custom-call(bf16[256,128]{1,0:T(8,128)(2,1)S(1)} %copy-done.3), custom_call_target="tpu_custom_call" | custom-call | flops 4000000000 | bytes 4000000 | tf_op jit(solution)/shard_map/pallas_call | solution.py:284
  3.8 0.0 copy-done
  3.8 0.0 copy-done.1
  3.8 0.0 copy-done.2
  3.8 1.1 %shard_map.76 = (f32[128,640]{1,0:T(8,128)S(1)}, f32[256,128]{1,0:T(8,128)S(1)}, f32[256,256]{1,0:T(8,128)S(1)}) custom-call(s32[1]{0:T(128)} %bitcast.index_ref, f32[256,128]{1,0:T(8,128)S(1)} %get-tuple-element.21.k_ref, f32[256,256]{1,0:T(8,128)S(1)} %get-tuple-element.22.inv_ref, bf16[512,128]{1,0:T(8,128)(2,1)S(1)} %bitcast.21, ...), custom_call_target="tpu_custom_call" | custom-call | tf_op jit(solution)/shard_map/pallas_call | solution.py:284
  4.9 2.3 %all-gather = f32[256,640]{1,0:T(8,128)S(1)} all-gather(f32[128,640]{1,0:T(8,128)S(1)} %get-tuple-element.23), channel_id=2, replica_groups={{0,16},{32,48},{64,80},{96,112},{128,144},{160,176},{192,208},{224,240}..., dimensions={0}, use_global_device_ids=true | all-gather | bytes 983040 | tf_op jit(solution)/shard_map/all_gather | solution.py:297
  7.2 0.3 shard_map.77
  7.5 11.3 %all-gather.1 = f32[256,384]{1,0:T(8,128)S(1)} all-gather(f32[128,384]{1,0:T(8,128)S(1)} %shard_map.77), channel_id=3, replica_groups={{0,32},{16,48},{64,96},{80,112},{128,160},{144,176},{192,224},{208,240}..., dimensions={0}, use_global_device_ids=true | all-gather | bytes 589824 | tf_op jit(solution)/shard_map/all_gather | solution.py:297
  18.8 0.2 shard_map.78
  19.1 6.7 %all-gather.2 = f32[256,256]{1,0:T(8,128)S(1)} all-gather(f32[128,256]{1,0:T(8,128)S(1)} %shard_map.78), channel_id=4, replica_groups={{0,64},{16,80},{32,96},{48,112},{128,192},{144,208},{160,224},{176,240}..., dimensions={0}, use_global_device_ids=true | all-gather | bytes 393216 | tf_op jit(solution)/shard_map/all_gather | solution.py:297
  25.8 0.2 shard_map.79
  26.0 7.5 %collective-permute-start = (f32[128,128]{1,0:T(8,128)S(1)}, f32[128,128]{1,0:T(8,128)S(1)}, u32[]{:S(2)}, u32[]{:S(2)}) collective-permute-start(f32[128,128]{1,0:T(8,128)S(1)} %get-tuple-element.24.sent_ref), channel_id=1, source_target_pairs={{0,128},{32,160},{64,192},{96,224},{496,368},{464,336},{432,304},{... | collective-permute-start | bytes 196616 | tf_op jit(solution)/shard_map/ppermute | solution.py:311
  33.5 1.9 %collective-permute-done.got_ref.first_ref = f32[128,128]{1,0:T(8,128)S(1)} collective-permute-done((f32[128,128]{1,0:T(8,128)S(1)}, f32[128,128]{1,0:T(8,128)S(1)}, u32[]{:S(2)}, u32[]{:S(2)}) %collective-permute-start) | collective-permute-done | bytes 65568 | tf_op jit(solution)/shard_map/ppermute | solution.py:311
  35.4 0.2 shard_map.80
  35.5 0.7 collective-permute-start.1
  36.2 0.0 collective-permute-done.1.got_ref.second_ref
  36.2 0.2 shard_map.81
  36.4 0.7 collective-permute-start.2
  37.1 1.3 %shard_map.83 = (f32[256,128]{1,0:T(8,128)S(1)}, f32[256,256]{1,0:T(8,128)S(1)}) custom-call(s32[1]{0:T(128)} %bitcast.index_ref, f32[128,128]{1,0:T(8,128)S(1)} %get-tuple-element.24.sent_ref, f32[256,128]{1,0:T(8,128)S(1)} %get-tuple-element.21.k_ref, f32[256,256]{1,0:T(8,128)S(1)} %get-tuple-element.22.inv_ref, bf16[512,128]{1,0:T(8,128)(2,1)S(1)} %bitcast.22, ...), custom_call_target="tpu_custom_call" | custom-call | flops 500000000 | bytes 1000000 | tf_op jit(solution)/shard_map/pallas_call | solution.py:284
  38.4 0.0 collective-permute-done.2.third_ref
  38.4 0.4 shard_map.82
  38.8 20.5 %all-gather.3 = f32[512,256]{1,0:T(8,128)S(1)} all-gather(f32[128,256]{1,0:T(8,128)S(1)} %shard_map.82), channel_id=5, replica_groups={{0,16,32,48},{64,80,96,112},{128,144,160,176},{192,208,224,240},{256,27..., dimensions={0}, use_global_device_ids=true | all-gather | bytes 655360 | tf_op jit(solution)/shard_map/all_gather | solution.py:297
  59.3 1.3 %shard_map.84 = (f32[256,128]{1,0:T(8,128)S(1)}, f32[128,256]{1,0:T(8,128)S(1)}, f32[256,256]{1,0:T(8,128)S(1)}, f32[256,256]{1,0:T(8,128)S(1)}) custom-call(s32[1]{0:T(128)} %bitcast.index_ref, f32[2,128,640]{2,1,0:T(8,128)S(1)} %bitcast.14, f32[4,128,256]{2,1,0:T(8,128)S(1)} %bitcast.19, bf16[512,128]{1,0:T(8,128)(2,1)S(1)} %bitcast.23, ...), custom_call_target="tpu_custom_call" | custom-call | tf_op jit(solution)/shard_map/pallas_call | solution.py:284
  60.6 14.8 %all_to_all.10.got_ref = f32[16,16,128]{2,1,0:T(8,128)S(1)} all-to-all(f32[16,16,128]{2,1,0:T(8,128)S(1)} %bitcast.29), channel_id=1, replica_groups=mesh['seq'=32,'head'=16] {'head'}, dimensions={0} | all-to-all | bytes 262144 | tf_op jit(solution)/shard_map/all_to_all | solution.py:356
  75.4 0.7 shard_map.86
  76.1 3.5 %all-to-all-start.1 = ((f32[16,16,128]{2,1,0:T(8,128)}), f32[16,16,128]{2,1,0:T(8,128)S(1)}, u32[]{:S(2)}, u32[]{:S(2)}) async-start(f32[16,16,128]{2,1,0:T(8,128)} %shard_map.86), calls=%async_computation.1 | async-start | bytes 262144 | tf_op jit(solution)/shard_map/all_to_all | solution.py:365
  79.6 2.1 %shard_map.85 = (bf16[512,128]{1,0:T(8,128)(2,1)}, bf16[512,128]{1,0:T(8,128)(2,1)}, bf16[512,128]{1,0:T(8,128)(2,1)}) custom-call(s32[1]{0:T(128)} %bitcast.index_ref, bf16[512,128]{1,0:T(8,128)(2,1)S(1)} %bitcast.24, bf16[512,128]{1,0:T(8,128)(2,1)S(1)} %bitcast.28, f32[256,128]{1,0:T(8,128)S(1)} %get-tuple-element.21.k_ref, ...), custom_call_target="tpu_custom_call" | custom-call | flops 4000000000 | bytes 4000000 | tf_op jit(solution)/shard_map/pallas_call | solution.py:284
  81.7 5.8 %all-to-all-done.1 = f32[16,16,128]{2,1,0:T(8,128)S(1)} async-done(((f32[16,16,128]{2,1,0:T(8,128)}), f32[16,16,128]{2,1,0:T(8,128)S(1)}, u32[]{:S(2)}, u32[]{:S(2)}) %all-to-all-start.1) | async-done | bytes 131104 | tf_op jit(solution)/shard_map/all_to_all | solution.py:365
  87.6 0.7 shard_map.87
Async XLA Ops:
  0.6 0.8 copy-start.3
  1.5 2.3 %copy-start = (bf16[256,2,128]{2,1,0:T(2,128)(2,1)S(1)}, bf16[256,2,128]{2,1,0:T(2,128)(2,1)}, u32[]{:S(2)}) copy-start(bf16[256,2,128]{2,1,0:T(2,128)(2,1)} %param.4) | copy-start | bytes 393220
  1.5 2.3 %copy-start.1 = (bf16[256,2,128]{2,1,0:T(2,128)(2,1)S(1)}, bf16[256,2,128]{2,1,0:T(2,128)(2,1)}, u32[]{:S(2)}) copy-start(bf16[256,2,128]{2,1,0:T(2,128)(2,1)} %param.7) | copy-start | bytes 393220
  1.5 2.3 %copy-start.2 = (bf16[256,2,128]{2,1,0:T(2,128)(2,1)S(1)}, bf16[256,2,128]{2,1,0:T(2,128)(2,1)}, u32[]{:S(2)}) copy-start(bf16[256,2,128]{2,1,0:T(2,128)(2,1)} %param.6) | copy-start | bytes 393220
  26.0 9.4 %collective-permute-start = (f32[128,128]{1,0:T(8,128)S(1)}, f32[128,128]{1,0:T(8,128)S(1)}, u32[]{:S(2)}, u32[]{:S(2)}) collective-permute-start(f32[128,128]{1,0:T(8,128)S(1)} %get-tuple-element.24.sent_ref), channel_id=1, source_target_pairs={{0,128},{32,160},{64,192},{96,224},{496,368},{464,336},{432,304},{... | collective-permute-start | bytes 196616 | tf_op jit(solution)/shard_map/ppermute | solution.py:311
  35.5 0.7 collective-permute-start.1
  36.4 2.0 %collective-permute-start.2 = (f32[128,128]{1,0:T(8,128)S(1)}, f32[128,128]{1,0:T(8,128)S(1)}, u32[]{:S(2)}, u32[]{:S(2)}) collective-permute-start(f32[128,128]{1,0:T(8,128)S(1)} %shard_map.81), channel_id=1, source_target_pairs={{256,384},{288,416},{320,448},{352,480},{240,112},{208,80},{176,48... | collective-permute-start | bytes 196616 | tf_op jit(solution)/shard_map/ppermute | solution.py:311
  76.1 11.5 %all-to-all-start.1 = ((f32[16,16,128]{2,1,0:T(8,128)}), f32[16,16,128]{2,1,0:T(8,128)S(1)}, u32[]{:S(2)}, u32[]{:S(2)}) async-start(f32[16,16,128]{2,1,0:T(8,128)} %shard_map.86), calls=%async_computation.1 | async-start | bytes 262144 | tf_op jit(solution)/shard_map/all_to_all | solution.py:365

commit v7 on v6

--- a/solution.py
+++ b/solution.py
@@ -149,8 +149,8 @@
     return jnp.where(index_ref[0] % 2 == 1, size - 1 - place, place)
 
 
-def pair_kernel(index_ref, got_ref, send_ref):
-    down = index_ref[0] % 2 == 1
+def pair_kernel(index_ref, got_ref, own_ref, send_ref):
+    down, right = index_ref[0] % 2 == 1, (index_ref[0] // 2) % 2 == 1
 
     def ranges(i):
         return jnp.concatenate(
@@ -161,17 +161,18 @@
             axis=1,
         )
 
-    send_ref[...] = then(ranges(0), ranges(1))
-
-
-def chip_kernel(index_ref, got_ref, send_ref):
+    chip = then(ranges(0), ranges(1))
+    left, rest = chip[:, : 2 * D], jnp.concatenate([chip[:, :D], chip[:, 2 * D :]], axis=1)
+    own_ref[...] = jnp.where(right, rest, left)
+    send_ref[...] = jnp.where(right, left, rest)
+
+
+def chip_kernel(index_ref, own_ref, got_ref, first_ref, send_ref):
     down, right = index_ref[0] % 2 == 1, (index_ref[0] // 2) % 2 == 1
-    first, second = [halved(jnp.where(down, got_ref[1 - i], got_ref[i]), right) for i in range(2)]
-    send_ref[...] = then(first, second)
-
-
-def halved(x, right):
-    return jnp.concatenate([x[:, :D], jnp.where(right, x[:, 2 * D :], x[:, D : 2 * D])], axis=1)
+    own, other = own_ref[...], jnp.where(right, got_ref[0], got_ref[1])
+    first = jnp.where(right == down, own, other)
+    first_ref[...] = first
+    send_ref[...] = then(first, jnp.where(right == down, other, own))
 
 
 def block_kernel(index_ref, got_ref, send_ref, block_ref):
@@ -186,8 +187,8 @@
     send_ref[...] = block_ref[:, D:] + mm(split(block_ref[:, :D]), split(got_ref[...]))
 
 
-def top_kernel(index_ref, first_ref, second_ref, third_ref, units_ref, chips_ref, send_ref):
-    down, right = index_ref[0] % 2 == 1, (index_ref[0] // 2) % 2 == 1
+def top_kernel(index_ref, first_ref, second_ref, third_ref, units_ref, chip_ref, send_ref):
+    down = index_ref[0] % 2 == 1
     place = along(index_ref, 4, 8)
     got = jnp.where(
         place == 1, first_ref[...], jnp.where(place == 2, second_ref[...], jnp.where(place == 3, third_ref[...], 0.0))
@@ -196,8 +197,7 @@
     later = unit[:, D:] + mm(split(unit[:, :D]), split(got))
     got = jnp.where(along(index_ref, 2, 4) == 1, later, got)
     send_ref[:, :D] = got
-    chip = halved(jnp.where(down, chips_ref[1], chips_ref[0]), right)
-    send_ref[:, D:] = chip[:, D:] + mm(split(chip[:, :D]), split(got))
+    send_ref[:, D:] = chip_ref[:, D:] + mm(split(chip_ref[:, :D]), split(got))
 
 
 def after_kernel(index_ref, pair_ref, got_ref, q_ref, d_ref, k_ref, w_ref, m_ref, x0_ref, z0_ref,
@@ -327,9 +327,8 @@
         scratch=[wide] * 3,
     )
     pair = exchange(send, near(0, 1))
-    send = call(pair_kernel, ((D, 3 * D), F32), index, pair)
-    chips = exchange(send, near(0, 2))
-    send = call(chip_kernel, ((D, 2 * D), F32), index, chips)
+    own, send = call(pair_kernel, [((D, 2 * D), F32)] * 2, index, pair)
+    chip, send = call(chip_kernel, [((D, 2 * D), F32)] * 2, index, own, exchange(send, near(0, 2)))
     units = exchange(send, near(0, 4))
     send, block = call(block_kernel, [((D, D), F32), ((D, 2 * D), F32)], index, units)
     first = hop(send, 0)
@@ -344,7 +343,7 @@
     second = hop(send, 1)
     send = call(hop_kernel, ((D, D), F32), second, block, scalars=0)
     third = hop(send, 2)
-    send = call(top_kernel, ((D, 2 * D), F32), index, first, second, third, units, chips)
+    send = call(top_kernel, ((D, 2 * D), F32), index, first, second, third, units, chip)
     got = exchange(send, near(0, 1, 2, 3))
     gk, state, x, z = call(
         after_kernel,

time: 88.6 us -> 87.2 us (0.984)
  blocking collectives: 55.7 us -> 54.2 us
    all_gather x4, blocking collectives: 40.8 us -> 39.5 us  [exchange(): return lax.all_gather(x, 'seq', axis_index_groups=groups)]
where the time goes in v7:
time: 87.2 us; the launch traced here: 86.9 us
  blocking collectives  54.2 us (62%)
  starting transfers between devices  12.4 us (14%)
  Pallas kernels  10.9 us (12%)
  waiting for transfers between devices  7.72 us (9%)
    all_gather x4, blocking collectives, exchange(): return lax.all_gather(x, 'seq', axis_index_groups=groups)  39.5 us
    all_to_all x1, blocking collectives, shards(): pieces = lax.all_to_all(gk.reshape(peers, T // peers, D), 'head', 0, 0)  14.8 us
    pallas_call x13, Pallas kernels, call(): pl.pallas_call(kernel, out_shape=[jax.ShapeDtypeStruct(*s) for s in shape...  10.9 us
    ppermute x3, starting transfers between devices, hop(): lax.ppermute(x, 'seq', up + [(PARTS - 1 - a, PARTS - 1 - b) for a, b in up])  8.84 us
    all_to_all x1, waiting for transfers between devices, shards(): total = lax.all_to_all(totals, 'head', 0, 0).reshape(T, D)  5.83 us
    all_to_all x1, starting transfers between devices, shards(): total = lax.all_to_all(totals, 'head', 0, 0).reshape(T, D)  3.51 us
    ppermute x3, waiting for transfers between devices, hop(): lax.ppermute(x, 'seq', up + [(PARTS - 1 - a, PARTS - 1 - b) for a, b in up])  1.89 us
  transfers between devices with their start and end apart: 4, of which 2 were waited for; matrix products, arithmetic and copies ran while one was open for 0% of the time, Pallas kernels for 4%

profile of v7, /device:TPU:32, one launch (start us, length us, event | category | flops | bytes accessed | tf_op | source)
XLA Modules:
  0.0 86.9 jit_solution(11405360791577370914)
XLA Ops:
  0.6 0.0 copy-start.3
  0.6 0.8 copy-done.3
  1.5 0.0 copy-start
  1.5 0.0 copy-start.1
  1.5 0.0 copy-start.2
  1.5 2.3 %shard_map.75 = (f32[256,128]{1,0:T(8,128)S(1)}, f32[256,128]{1,0:T(8,128)S(1)}, f32[256,256]{1,0:T(8,128)S(1)}) custom-call(bf16[256,128]{1,0:T(8,128)(2,1)S(1)} %copy-done.3), custom_call_target="tpu_custom_call" | custom-call | flops 4000000000 | bytes 4000000 | tf_op jit(solution)/shard_map/pallas_call | solution.py:284
  3.8 0.0 copy-done
  3.8 0.0 copy-done.1
  3.8 0.0 copy-done.2
  3.8 1.1 %shard_map.76 = (f32[128,640]{1,0:T(8,128)S(1)}, f32[256,128]{1,0:T(8,128)S(1)}, f32[256,256]{1,0:T(8,128)S(1)}) custom-call(s32[1]{0:T(128)} %bitcast.index_ref, f32[256,128]{1,0:T(8,128)S(1)} %get-tuple-element.25.k_ref, f32[256,256]{1,0:T(8,128)S(1)} %get-tuple-element.26.inv_ref, bf16[512,128]{1,0:T(8,128)(2,1)S(1)} %bitcast.20, ...), custom_call_target="tpu_custom_call" | custom-call | tf_op jit(solution)/shard_map/pallas_call | solution.py:284
  4.9 2.3 %all-gather = f32[256,640]{1,0:T(8,128)S(1)} all-gather(f32[128,640]{1,0:T(8,128)S(1)} %get-tuple-element.27), channel_id=2, replica_groups={{0,16},{32,48},{64,80},{96,112},{128,144},{160,176},{192,208},{224,240}..., dimensions={0}, use_global_device_ids=true | all-gather | bytes 983040 | tf_op jit(solution)/shard_map/all_gather | solution.py:297
  7.2 0.3 shard_map.77
  7.5 9.9 %all-gather.1 = f32[256,256]{1,0:T(8,128)S(1)} all-gather(f32[128,256]{1,0:T(8,128)S(1)} %get-tuple-element.29), channel_id=3, replica_groups={{0,32},{16,48},{64,96},{80,112},{128,160},{144,176},{192,224},{208,240}..., dimensions={0}, use_global_device_ids=true | all-gather | bytes 393216 | tf_op jit(solution)/shard_map/all_gather | solution.py:297
  17.4 0.2 shard_map.78
  17.6 6.7 %all-gather.2 = f32[256,256]{1,0:T(8,128)S(1)} all-gather(f32[128,256]{1,0:T(8,128)S(1)} %get-tuple-element.30), channel_id=4, replica_groups={{0,64},{16,80},{32,96},{48,112},{128,192},{144,208},{160,224},{176,240}..., dimensions={0}, use_global_device_ids=true | all-gather | bytes 393216 | tf_op jit(solution)/shard_map/all_gather | solution.py:297
  24.4 0.2 shard_map.79
  24.6 7.5 %collective-permute-start = (f32[128,128]{1,0:T(8,128)S(1)}, f32[128,128]{1,0:T(8,128)S(1)}, u32[]{:S(2)}, u32[]{:S(2)}) collective-permute-start(f32[128,128]{1,0:T(8,128)S(1)} %get-tuple-element.31.sent_ref), channel_id=1, source_target_pairs={{0,128},{32,160},{64,192},{96,224},{496,368},{464,336},{432,304},{... | collective-permute-start | bytes 196616 | tf_op jit(solution)/shard_map/ppermute | solution.py:311
  32.1 1.9 %collective-permute-done.got_ref.first_ref = f32[128,128]{1,0:T(8,128)S(1)} collective-permute-done((f32[128,128]{1,0:T(8,128)S(1)}, f32[128,128]{1,0:T(8,128)S(1)}, u32[]{:S(2)}, u32[]{:S(2)}) %collective-permute-start) | collective-permute-done | bytes 65568 | tf_op jit(solution)/shard_map/ppermute | solution.py:311
  34.0 0.2 shard_map.80
  34.1 0.7 collective-permute-start.1
  34.8 0.0 collective-permute-done.1.got_ref.second_ref
  34.8 0.2 shard_map.81
  35.0 0.7 collective-permute-start.2
  35.7 1.3 %shard_map.83 = (f32[256,128]{1,0:T(8,128)S(1)}, f32[256,256]{1,0:T(8,128)S(1)}) custom-call(s32[1]{0:T(128)} %bitcast.index_ref, f32[128,128]{1,0:T(8,128)S(1)} %get-tuple-element.31.sent_ref, f32[256,128]{1,0:T(8,128)S(1)} %get-tuple-element.25.k_ref, f32[256,256]{1,0:T(8,128)S(1)} %get-tuple-element.26.inv_ref, bf16[512,128]{1,0:T(8,128)(2,1)S(1)} %bitcast.21, ...), custom_call_target="tpu_custom_call" | custom-call | flops 500000000 | bytes 1000000 | tf_op jit(solution)/shard_map/pallas_call | solution.py:284
  37.0 0.0 collective-permute-done.2.third_ref
  37.0 0.4 shard_map.82
  37.4 20.5 %all-gather.3 = f32[512,256]{1,0:T(8,128)S(1)} all-gather(f32[128,256]{1,0:T(8,128)S(1)} %shard_map.82), channel_id=5, replica_groups={{0,16,32,48},{64,80,96,112},{128,144,160,176},{192,208,224,240},{256,27..., dimensions={0}, use_global_device_ids=true | all-gather | bytes 655360 | tf_op jit(solution)/shard_map/all_gather | solution.py:297
  57.9 1.3 %shard_map.84 = (f32[256,128]{1,0:T(8,128)S(1)}, f32[128,256]{1,0:T(8,128)S(1)}, f32[256,256]{1,0:T(8,128)S(1)}, f32[256,256]{1,0:T(8,128)S(1)}) custom-call(s32[1]{0:T(128)} %bitcast.index_ref, f32[2,128,640]{2,1,0:T(8,128)S(1)} %bitcast.14, f32[4,128,256]{2,1,0:T(8,128)S(1)} %bitcast.17, bf16[512,128]{1,0:T(8,128)(2,1)S(1)} %bitcast.22, ...), custom_call_target="tpu_custom_call" | custom-call | tf_op jit(solution)/shard_map/pallas_call | solution.py:284
  59.2 14.8 %all_to_all.10.got_ref = f32[16,16,128]{2,1,0:T(8,128)S(1)} all-to-all(f32[16,16,128]{2,1,0:T(8,128)S(1)} %bitcast.28), channel_id=1, replica_groups=mesh['seq'=32,'head'=16] {'head'}, dimensions={0} | all-to-all | bytes 262144 | tf_op jit(solution)/shard_map/all_to_all | solution.py:355
  74.0 0.7 shard_map.86
  74.7 3.5 %all-to-all-start.1 = ((f32[16,16,128]{2,1,0:T(8,128)}), f32[16,16,128]{2,1,0:T(8,128)S(1)}, u32[]{:S(2)}, u32[]{:S(2)}) async-start(f32[16,16,128]{2,1,0:T(8,128)} %shard_map.86), calls=%async_computation.1 | async-start | bytes 262144 | tf_op jit(solution)/shard_map/all_to_all | solution.py:364
  78.2 2.1 %shard_map.85 = (bf16[512,128]{1,0:T(8,128)(2,1)}, bf16[512,128]{1,0:T(8,128)(2,1)}, bf16[512,128]{1,0:T(8,128)(2,1)}) custom-call(s32[1]{0:T(128)} %bitcast.index_ref, bf16[512,128]{1,0:T(8,128)(2,1)S(1)} %bitcast.23, bf16[512,128]{1,0:T(8,128)(2,1)S(1)} %bitcast.27, f32[256,128]{1,0:T(8,128)S(1)} %get-tuple-element.25.k_ref, ...), custom_call_target="tpu_custom_call" | custom-call | flops 4000000000 | bytes 4000000 | tf_op jit(solution)/shard_map/pallas_call | solution.py:284
  80.3 5.8 %all-to-all-done.1 = f32[16,16,128]{2,1,0:T(8,128)S(1)} async-done(((f32[16,16,128]{2,1,0:T(8,128)}), f32[16,16,128]{2,1,0:T(8,128)S(1)}, u32[]{:S(2)}, u32[]{:S(2)}) %all-to-all-start.1) | async-done | bytes 131104 | tf_op jit(solution)/shard_map/all_to_all | solution.py:364
  86.1 0.7 shard_map.87
Async XLA Ops:
  0.6 0.8 copy-start.3
  1.5 2.3 %copy-start = (bf16[256,2,128]{2,1,0:T(2,128)(2,1)S(1)}, bf16[256,2,128]{2,1,0:T(2,128)(2,1)}, u32[]{:S(2)}) copy-start(bf16[256,2,128]{2,1,0:T(2,128)(2,1)} %param.4) | copy-start | bytes 393220
  1.5 2.3 %copy-start.1 = (bf16[256,2,128]{2,1,0:T(2,128)(2,1)S(1)}, bf16[256,2,128]{2,1,0:T(2,128)(2,1)}, u32[]{:S(2)}) copy-start(bf16[256,2,128]{2,1,0:T(2,128)(2,1)} %param.7) | copy-start | bytes 393220
  1.5 2.3 %copy-start.2 = (bf16[256,2,128]{2,1,0:T(2,128)(2,1)S(1)}, bf16[256,2,128]{2,1,0:T(2,128)(2,1)}, u32[]{:S(2)}) copy-start(bf16[256,2,128]{2,1,0:T(2,128)(2,1)} %param.6) | copy-start | bytes 393220
  24.6 9.4 %collective-permute-start = (f32[128,128]{1,0:T(8,128)S(1)}, f32[128,128]{1,0:T(8,128)S(1)}, u32[]{:S(2)}, u32[]{:S(2)}) collective-permute-start(f32[128,128]{1,0:T(8,128)S(1)} %get-tuple-element.31.sent_ref), channel_id=1, source_target_pairs={{0,128},{32,160},{64,192},{96,224},{496,368},{464,336},{432,304},{... | collective-permute-start | bytes 196616 | tf_op jit(solution)/shard_map/ppermute | solution.py:311
  34.1 0.7 collective-permute-start.1
  35.0 2.0 %collective-permute-start.2 = (f32[128,128]{1,0:T(8,128)S(1)}, f32[128,128]{1,0:T(8,128)S(1)}, u32[]{:S(2)}, u32[]{:S(2)}) collective-permute-start(f32[128,128]{1,0:T(8,128)S(1)} %shard_map.81), channel_id=1, source_target_pairs={{256,384},{288,416},{320,448},{352,480},{240,112},{208,80},{176,48... | collective-permute-start | bytes 196616 | tf_op jit(solution)/shard_map/ppermute | solution.py:311
  74.7 11.5 %all-to-all-start.1 = ((f32[16,16,128]{2,1,0:T(8,128)}), f32[16,16,128]{2,1,0:T(8,128)S(1)}, u32[]{:S(2)}, u32[]{:S(2)}) async-start(f32[16,16,128]{2,1,0:T(8,128)} %shard_map.86), calls=%async_computation.1 | async-start | bytes 262144 | tf_op jit(solution)/shard_map/all_to_all | solution.py:364

commit v8 on v7

--- a/solution.py
+++ b/solution.py
@@ -70,7 +70,7 @@
 
 
 def places_root(index):
-    places = (index * T + iota((T, 1), 0) + 1).astype(F32)
+    places = (index % PARTS * T + iota((T, 1), 0) + 1).astype(F32)
     return 1.0 / jnp.sqrt(places)
 
 
@@ -221,7 +221,7 @@
     adjoint = jnp.where(upper, adjoint, step + pair_ref[1, :, 3 * D :])
     s_ref[...] = state
     states, adjoints = split(state), split(adjoint)
-    root = places_root(index_ref[0])
+    across = 1.0 / jnp.sqrt((index_ref[0] % PARTS * T + iota((1, T), 1) + 1).astype(F32))
     keys = split(k_ref[...])
     row, col = iota((T, T), 0), iota((T, T), 1)
     x = x0_ref[...] - mm(split(w_ref[...]), states)
@@ -234,10 +234,10 @@
     queries = [exact(qs_ref[r, :].astype(BF16)) for r in rows]
     grads = [exact(ds_ref[r, :].astype(BF16)) for r in rows]
     edge = mm(zs, xs, (1, 1))
-    mixed = [mm(grad, tuple(s[:, part] for s in xs), (1, 1)) for grad, part in zip(grads, parts)]
+    mixed = [mm(tuple(s[:, part] for s in xs), grad, (1, 1)) for grad, part in zip(grads, parts)]
     gk = mm(xs, adjoints, (1, 1)) - 2.0 * mm(zs, states, (1, 1))
     edge = jnp.where(row > col, edge, 0.0)
-    mixed = [split((jnp.where(row >= col, mix, 0.0) * root).T) for mix in mixed]
+    mixed = [split(jnp.where(col >= row, mix, 0.0) * across) for mix in mixed]
     last = [mm(mix, query) for mix, query in zip(mixed, queries)]
     gk = gk - 2.0 * mm(split(edge + edge.T), keys) + last[0] + last[1]
     gk_ref[...] = gk
@@ -267,14 +267,16 @@
     gv_ref[...] = zs_ref[...].astype(BF16)
 
 
-def sum_kernel(got_ref, out_ref):
-    out_ref[...] = jnp.broadcast_to(jnp.sum(got_ref[...], axis=0, keepdims=True), out_ref.shape)
-
-
-def key_kernel(got_ref, k_ref, norm_ref, out_ref):
-    total, key = got_ref[...], k_ref[...]
-    along = jnp.sum(total * key, axis=1, keepdims=True)
-    out_ref[...] = ((total - key * along) * norm_ref[...]).astype(BF16)
+def sum_kernel(index_ref, got_ref, k_ref, norm_ref, out_ref):
+    count = got_ref.shape[1]
+    rows = pl.ds(pl.multiple_of((index_ref[0] // PARTS) * count, count), count)
+    total, key = jnp.sum(got_ref[...], axis=0), k_ref[rows, :]
+    total = (total - key * jnp.sum(total * key, axis=1, keepdims=True)) * norm_ref[rows, :]
+    out_ref[...] = jnp.broadcast_to(total[None], out_ref.shape)
+
+
+def key_kernel(got_ref, out_ref):
+    out_ref[...] = got_ref[...].astype(BF16)
 
 
 def call(kernel, outs, *operands, scratch=(), scalars=1, cost=None):
@@ -312,7 +314,7 @@
 
 
 def shards(queries, raw_keys, values, cotangent):
-    index = lax.axis_index("seq").astype(jnp.int32).reshape(1)
+    index = (lax.axis_index("seq") + PARTS * lax.axis_index("head")).astype(jnp.int32).reshape(1)
     q = queries.reshape(2 * T, D)
     v = values.reshape(2 * T, D)
     d = cotangent.reshape(2 * T, D)
@@ -360,9 +362,9 @@
         scratch=[wide] * 5,
         cost=LONG,
     )
-    totals = call(sum_kernel, ((peers, T // peers, D), F32), pieces, scalars=0)
+    totals = call(sum_kernel, ((peers, T // peers, D), F32), index, pieces, key, norm)
     total = lax.all_to_all(totals, "head", 0, 0).reshape(T, D)
-    gkey = call(key_kernel, ((T, D), BF16), total, key, norm, scalars=0)
+    gkey = call(key_kernel, ((T, D), BF16), total, scalars=0)
     shape = queries.shape
     return out.reshape(shape), gq.reshape(shape), gkey, gv.reshape(shape)
 

time: 87.2 us -> 87.2 us (level)
  no operation moved by 1% of the time
where the time goes in v8:
time: 87.2 us; the launch traced here: 86.9 us
  blocking collectives  54.3 us (62%)
  starting transfers between devices  12.3 us (14%)
  Pallas kernels  10.9 us (12%)
  waiting for transfers between devices  7.72 us (9%)
    all_gather x4, blocking collectives, exchange(): return lax.all_gather(x, 'seq', axis_index_groups=groups)  39.4 us
    all_to_all x1, blocking collectives, shards(): pieces = lax.all_to_all(gk.reshape(peers, T // peers, D), 'head', 0, 0)  14.8 us
    pallas_call x13, Pallas kernels, call(): pl.pallas_call(kernel, out_shape=[jax.ShapeDtypeStruct(*s) for s in shape...  10.9 us
    ppermute x3, starting transfers between devices, hop(): lax.ppermute(x, 'seq', up + [(PARTS - 1 - a, PARTS - 1 - b) for a, b in up])  8.84 us
    all_to_all x1, waiting for transfers between devices, shards(): total = lax.all_to_all(totals, 'head', 0, 0).reshape(T, D)  5.83 us
    all_to_all x1, starting transfers between devices, shards(): total = lax.all_to_all(totals, 'head', 0, 0).reshape(T, D)  3.51 us
    ppermute x3, waiting for transfers between devices, hop(): lax.ppermute(x, 'seq', up + [(PARTS - 1 - a, PARTS - 1 - b) for a, b in up])  1.89 us
  transfers between devices with their start and end apart: 4, of which 2 were waited for; matrix products, arithmetic and copies ran while one was open for 0% of the time, Pallas kernels for 4%

profile of v8, /device:TPU:32, one launch (start us, length us, event | category | flops | bytes accessed | tf_op | source)
XLA Modules:
  0.0 86.9 jit_solution(10197959454605814915)
XLA Ops:
  0.6 0.0 copy-start.3
  0.6 0.8 copy-done.3
  1.5 0.0 copy-start
  1.5 0.0 copy-start.1
  1.5 0.0 copy-start.2
  1.5 2.3 %shard_map.75 = (f32[256,128]{1,0:T(8,128)S(1)}, f32[256,128]{1,0:T(8,128)S(1)}, f32[256,256]{1,0:T(8,128)S(1)}) custom-call(bf16[256,128]{1,0:T(8,128)(2,1)S(1)} %copy-done.3), custom_call_target="tpu_custom_call" | custom-call | flops 4000000000 | bytes 4000000 | tf_op jit(solution)/shard_map/pallas_call | solution.py:286
  3.8 0.0 copy-done
  3.8 0.0 copy-done.1
  3.8 0.0 copy-done.2
  3.8 1.1 %shard_map.76 = (f32[128,640]{1,0:T(8,128)S(1)}, f32[256,128]{1,0:T(8,128)S(1)}, f32[256,256]{1,0:T(8,128)S(1)}) custom-call(s32[1]{0:T(128)} %bitcast.index_ref, f32[256,128]{1,0:T(8,128)S(1)} %get-tuple-element.25.k_ref, f32[256,256]{1,0:T(8,128)S(1)} %get-tuple-element.26.inv_ref, bf16[512,128]{1,0:T(8,128)(2,1)S(1)} %bitcast.19, ...), custom_call_target="tpu_custom_call" | custom-call | tf_op jit(solution)/shard_map/pallas_call | solution.py:286
  4.9 2.3 %all-gather = f32[256,640]{1,0:T(8,128)S(1)} all-gather(f32[128,640]{1,0:T(8,128)S(1)} %get-tuple-element.27), channel_id=2, replica_groups={{0,16},{32,48},{64,80},{96,112},{128,144},{160,176},{192,208},{224,240}..., dimensions={0}, use_global_device_ids=true | all-gather | bytes 983040 | tf_op jit(solution)/shard_map/all_gather | solution.py:299
  7.2 0.3 shard_map.77
  7.5 9.9 %all-gather.1 = f32[256,256]{1,0:T(8,128)S(1)} all-gather(f32[128,256]{1,0:T(8,128)S(1)} %get-tuple-element.29), channel_id=3, replica_groups={{0,32},{16,48},{64,96},{80,112},{128,160},{144,176},{192,224},{208,240}..., dimensions={0}, use_global_device_ids=true | all-gather | bytes 393216 | tf_op jit(solution)/shard_map/all_gather | solution.py:299
  17.4 0.2 shard_map.78
  17.6 6.7 %all-gather.2 = f32[256,256]{1,0:T(8,128)S(1)} all-gather(f32[128,256]{1,0:T(8,128)S(1)} %get-tuple-element.30), channel_id=4, replica_groups={{0,64},{16,80},{32,96},{48,112},{128,192},{144,208},{160,224},{176,240}..., dimensions={0}, use_global_device_ids=true | all-gather | bytes 393216 | tf_op jit(solution)/shard_map/all_gather | solution.py:299
  24.4 0.2 shard_map.79
  24.6 7.5 %collective-permute-start = (f32[128,128]{1,0:T(8,128)S(1)}, f32[128,128]{1,0:T(8,128)S(1)}, u32[]{:S(2)}, u32[]{:S(2)}) collective-permute-start(f32[128,128]{1,0:T(8,128)S(1)} %get-tuple-element.31.sent_ref), channel_id=1, source_target_pairs={{0,128},{32,160},{64,192},{96,224},{496,368},{464,336},{432,304},{... | collective-permute-start | bytes 196616 | tf_op jit(solution)/shard_map/ppermute | solution.py:313
  32.1 1.9 %collective-permute-done.got_ref.first_ref = f32[128,128]{1,0:T(8,128)S(1)} collective-permute-done((f32[128,128]{1,0:T(8,128)S(1)}, f32[128,128]{1,0:T(8,128)S(1)}, u32[]{:S(2)}, u32[]{:S(2)}) %collective-permute-start) | collective-permute-done | bytes 65568 | tf_op jit(solution)/shard_map/ppermute | solution.py:313
  34.0 0.2 shard_map.80
  34.1 0.7 collective-permute-start.1
  34.8 0.0 collective-permute-done.1.got_ref.second_ref
  34.8 0.2 shard_map.81
  35.0 0.7 collective-permute-start.2
  35.7 1.3 %shard_map.83 = (f32[256,128]{1,0:T(8,128)S(1)}, f32[256,256]{1,0:T(8,128)S(1)}) custom-call(s32[1]{0:T(128)} %bitcast.index_ref, f32[128,128]{1,0:T(8,128)S(1)} %get-tuple-element.31.sent_ref, f32[256,128]{1,0:T(8,128)S(1)} %get-tuple-element.25.k_ref, f32[256,256]{1,0:T(8,128)S(1)} %get-tuple-element.26.inv_ref, bf16[512,128]{1,0:T(8,128)(2,1)S(1)} %bitcast.20, ...), custom_call_target="tpu_custom_call" | custom-call | flops 500000000 | bytes 1000000 | tf_op jit(solution)/shard_map/pallas_call | solution.py:286
  37.0 0.0 collective-permute-done.2.third_ref
  37.0 0.4 shard_map.82
  37.4 20.5 %all-gather.3 = f32[512,256]{1,0:T(8,128)S(1)} all-gather(f32[128,256]{1,0:T(8,128)S(1)} %shard_map.82), channel_id=5, replica_groups={{0,16,32,48},{64,80,96,112},{128,144,160,176},{192,208,224,240},{256,27..., dimensions={0}, use_global_device_ids=true | all-gather | bytes 655360 | tf_op jit(solution)/shard_map/all_gather | solution.py:299
  57.9 1.3 %shard_map.84 = (f32[256,128]{1,0:T(8,128)S(1)}, f32[128,256]{1,0:T(8,128)S(1)}, f32[256,256]{1,0:T(8,128)S(1)}, f32[256,256]{1,0:T(8,128)S(1)}) custom-call(s32[1]{0:T(128)} %bitcast.index_ref, f32[2,128,640]{2,1,0:T(8,128)S(1)} %bitcast.14, f32[4,128,256]{2,1,0:T(8,128)S(1)} %bitcast.17, bf16[512,128]{1,0:T(8,128)(2,1)S(1)} %bitcast.21, ...), custom_call_target="tpu_custom_call" | custom-call | tf_op jit(solution)/shard_map/pallas_call | solution.py:286
  59.2 14.8 %all_to_all.10.got_ref = f32[16,16,128]{2,1,0:T(8,128)S(1)} all-to-all(f32[16,16,128]{2,1,0:T(8,128)S(1)} %bitcast.28), channel_id=1, replica_groups=mesh['seq'=32,'head'=16] {'head'}, dimensions={0} | all-to-all | bytes 262144 | tf_op jit(solution)/shard_map/all_to_all | solution.py:357
  74.0 0.8 shard_map.86
  74.8 3.5 %all-to-all-start.1 = ((f32[16,16,128]{2,1,0:T(8,128)}), f32[16,16,128]{2,1,0:T(8,128)S(1)}, u32[]{:S(2)}, u32[]{:S(2)}) async-start(f32[16,16,128]{2,1,0:T(8,128)} %shard_map.86), calls=%async_computation.1 | async-start | bytes 262144 | tf_op jit(solution)/shard_map/all_to_all | solution.py:366
  78.3 2.1 %shard_map.85 = (bf16[512,128]{1,0:T(8,128)(2,1)}, bf16[512,128]{1,0:T(8,128)(2,1)}, bf16[512,128]{1,0:T(8,128)(2,1)}) custom-call(s32[1]{0:T(128)} %bitcast.index_ref, bf16[512,128]{1,0:T(8,128)(2,1)S(1)} %bitcast.22, bf16[512,128]{1,0:T(8,128)(2,1)S(1)} %bitcast.26, f32[256,128]{1,0:T(8,128)S(1)} %get-tuple-element.25.k_ref, ...), custom_call_target="tpu_custom_call" | custom-call | flops 4000000000 | bytes 4000000 | tf_op jit(solution)/shard_map/pallas_call | solution.py:286
  80.4 5.8 %all-to-all-done.1 = f32[16,16,128]{2,1,0:T(8,128)S(1)} async-done(((f32[16,16,128]{2,1,0:T(8,128)}), f32[16,16,128]{2,1,0:T(8,128)S(1)}, u32[]{:S(2)}, u32[]{:S(2)}) %all-to-all-start.1) | async-done | bytes 131104 | tf_op jit(solution)/shard_map/all_to_all | solution.py:366
  86.2 0.6 shard_map.87
Async XLA Ops:
  0.6 0.8 copy-start.3
  1.5 2.3 %copy-start = (bf16[256,2,128]{2,1,0:T(2,128)(2,1)S(1)}, bf16[256,2,128]{2,1,0:T(2,128)(2,1)}, u32[]{:S(2)}) copy-start(bf16[256,2,128]{2,1,0:T(2,128)(2,1)} %param.4) | copy-start | bytes 393220
  1.5 2.3 %copy-start.1 = (bf16[256,2,128]{2,1,0:T(2,128)(2,1)S(1)}, bf16[256,2,128]{2,1,0:T(2,128)(2,1)}, u32[]{:S(2)}) copy-start(bf16[256,2,128]{2,1,0:T(2,128)(2,1)} %param.7) | copy-start | bytes 393220
  1.5 2.3 %copy-start.2 = (bf16[256,2,128]{2,1,0:T(2,128)(2,1)S(1)}, bf16[256,2,128]{2,1,0:T(2,128)(2,1)}, u32[]{:S(2)}) copy-start(bf16[256,2,128]{2,1,0:T(2,128)(2,1)} %param.6) | copy-start | bytes 393220
  24.6 9.4 %collective-permute-start = (f32[128,128]{1,0:T(8,128)S(1)}, f32[128,128]{1,0:T(8,128)S(1)}, u32[]{:S(2)}, u32[]{:S(2)}) collective-permute-start(f32[128,128]{1,0:T(8,128)S(1)} %get-tuple-element.31.sent_ref), channel_id=1, source_target_pairs={{0,128},{32,160},{64,192},{96,224},{496,368},{464,336},{432,304},{... | collective-permute-start | bytes 196616 | tf_op jit(solution)/shard_map/ppermute | solution.py:313
  34.1 0.7 collective-permute-start.1
  35.0 2.0 %collective-permute-start.2 = (f32[128,128]{1,0:T(8,128)S(1)}, f32[128,128]{1,0:T(8,128)S(1)}, u32[]{:S(2)}, u32[]{:S(2)}) collective-permute-start(f32[128,128]{1,0:T(8,128)S(1)} %shard_map.81), channel_id=1, source_target_pairs={{256,384},{288,416},{320,448},{352,480},{240,112},{208,80},{176,48... | collective-permute-start | bytes 196616 | tf_op jit(solution)/shard_map/ppermute | solution.py:313
  74.8 11.5 %all-to-all-start.1 = ((f32[16,16,128]{2,1,0:T(8,128)}), f32[16,16,128]{2,1,0:T(8,128)S(1)}, u32[]{:S(2)}, u32[]{:S(2)}) async-start(f32[16,16,128]{2,1,0:T(8,128)} %shard_map.86), calls=%async_computation.1 | async-start | bytes 262144 | tf_op jit(solution)/shard_map/all_to_all | solution.py:366

commit v9 on v8

--- a/solution.py
+++ b/solution.py
@@ -110,8 +110,8 @@
     key = k_ref[...]
     keys, invs, keys_t = split(key), split(inv_ref[...]), split(key.T)
     queries = [qs_ref[r, :] for r in rows]
+    w = 2.0 * mm(invs, keys)
     scores = [causal_scores(query, keys, root) for query in queries]
-    w = 2.0 * mm(invs, keys)
     x0 = mm(invs, exact(jnp.concatenate([vs_ref[r, :] for r in rows], axis=1).astype(BF16)))
     w_ref[...] = w
     x_ref[...] = x0

time: 87.2 us -> 87 us (level)
  no operation moved by 1% of the time
where the time goes in v9:
time: 87 us; the launch traced here: 86.7 us
  blocking collectives  54.3 us (62%)
  starting transfers between devices  12.3 us (14%)
  Pallas kernels  10.7 us (12%)
  waiting for transfers between devices  7.71 us (9%)
    all_gather x4, blocking collectives, exchange(): return lax.all_gather(x, 'seq', axis_index_groups=groups)  39.5 us
    all_to_all x1, blocking collectives, shards(): pieces = lax.all_to_all(gk.reshape(peers, T // peers, D), 'head', 0, 0)  14.8 us
    pallas_call x13, Pallas kernels, call(): pl.pallas_call(kernel, out_shape=[jax.ShapeDtypeStruct(*s) for s in shape...  10.7 us
    ppermute x3, starting transfers between devices, hop(): lax.ppermute(x, 'seq', up + [(PARTS - 1 - a, PARTS - 1 - b) for a, b in up])  8.83 us
    all_to_all x1, waiting for transfers between devices, shards(): total = lax.all_to_all(totals, 'head', 0, 0).reshape(T, D)  5.82 us
    all_to_all x1, starting transfers between devices, shards(): total = lax.all_to_all(totals, 'head', 0, 0).reshape(T, D)  3.51 us
    ppermute x3, waiting for transfers between devices, hop(): lax.ppermute(x, 'seq', up + [(PARTS - 1 - a, PARTS - 1 - b) for a, b in up])  1.89 us
  transfers between devices with their start and end apart: 4, of which 2 were waited for; matrix products, arithmetic and copies ran while one was open for 0% of the time, Pallas kernels for 4%

profile of v9, /device:TPU:32, one launch (start us, length us, event | category | flops | bytes accessed | tf_op | source)
XLA Modules:
  0.0 86.7 jit_solution(12344247050152846133)
XLA Ops:
  0.6 0.0 copy-start.3
  0.6 0.8 copy-done.3
  1.5 0.0 copy-start
  1.5 0.0 copy-start.1
  1.5 0.0 copy-start.2
  1.5 2.3 %shard_map.75 = (f32[256,128]{1,0:T(8,128)S(1)}, f32[256,128]{1,0:T(8,128)S(1)}, f32[256,256]{1,0:T(8,128)S(1)}) custom-call(bf16[256,128]{1,0:T(8,128)(2,1)S(1)} %copy-done.3), custom_call_target="tpu_custom_call" | custom-call | flops 4000000000 | bytes 4000000 | tf_op jit(solution)/shard_map/pallas_call | solution.py:286
  3.8 0.0 copy-done
  3.8 0.0 copy-done.1
  3.8 0.0 copy-done.2
  3.8 0.9 %shard_map.76 = (f32[128,640]{1,0:T(8,128)S(1)}, f32[256,128]{1,0:T(8,128)S(1)}, f32[256,256]{1,0:T(8,128)S(1)}) custom-call(s32[1]{0:T(128)} %bitcast.index_ref, f32[256,128]{1,0:T(8,128)S(1)} %get-tuple-element.25.k_ref, f32[256,256]{1,0:T(8,128)S(1)} %get-tuple-element.26.inv_ref, bf16[512,128]{1,0:T(8,128)(2,1)S(1)} %bitcast.19, ...), custom_call_target="tpu_custom_call" | custom-call | tf_op jit(solution)/shard_map/pallas_call | solution.py:286
  4.8 2.3 %all-gather = f32[256,640]{1,0:T(8,128)S(1)} all-gather(f32[128,640]{1,0:T(8,128)S(1)} %get-tuple-element.27), channel_id=2, replica_groups={{0,16},{32,48},{64,80},{96,112},{128,144},{160,176},{192,208},{224,240}..., dimensions={0}, use_global_device_ids=true | all-gather | bytes 983040 | tf_op jit(solution)/shard_map/all_gather | solution.py:299
  7.0 0.3 shard_map.77
  7.3 9.9 %all-gather.1 = f32[256,256]{1,0:T(8,128)S(1)} all-gather(f32[128,256]{1,0:T(8,128)S(1)} %get-tuple-element.29), channel_id=3, replica_groups={{0,32},{16,48},{64,96},{80,112},{128,160},{144,176},{192,224},{208,240}..., dimensions={0}, use_global_device_ids=true | all-gather | bytes 393216 | tf_op jit(solution)/shard_map/all_gather | solution.py:299
  17.3 0.2 shard_map.78
  17.5 6.7 %all-gather.2 = f32[256,256]{1,0:T(8,128)S(1)} all-gather(f32[128,256]{1,0:T(8,128)S(1)} %get-tuple-element.30), channel_id=4, replica_groups={{0,64},{16,80},{32,96},{48,112},{128,192},{144,208},{160,224},{176,240}..., dimensions={0}, use_global_device_ids=true | all-gather | bytes 393216 | tf_op jit(solution)/shard_map/all_gather | solution.py:299
  24.2 0.2 shard_map.79
  24.4 7.5 %collective-permute-start = (f32[128,128]{1,0:T(8,128)S(1)}, f32[128,128]{1,0:T(8,128)S(1)}, u32[]{:S(2)}, u32[]{:S(2)}) collective-permute-start(f32[128,128]{1,0:T(8,128)S(1)} %get-tuple-element.31.sent_ref), channel_id=1, source_target_pairs={{0,128},{32,160},{64,192},{96,224},{496,368},{464,336},{432,304},{... | collective-permute-start | bytes 196616 | tf_op jit(solution)/shard_map/ppermute | solution.py:313
  31.9 1.9 %collective-permute-done.got_ref.first_ref = f32[128,128]{1,0:T(8,128)S(1)} collective-permute-done((f32[128,128]{1,0:T(8,128)S(1)}, f32[128,128]{1,0:T(8,128)S(1)}, u32[]{:S(2)}, u32[]{:S(2)}) %collective-permute-start) | collective-permute-done | bytes 65568 | tf_op jit(solution)/shard_map/ppermute | solution.py:313
  33.8 0.2 shard_map.80
  34.0 0.7 collective-permute-start.1
  34.6 0.0 collective-permute-done.1.got_ref.second_ref
  34.6 0.2 shard_map.81
  34.8 0.7 collective-permute-start.2
  35.5 1.3 %shard_map.83 = (f32[256,128]{1,0:T(8,128)S(1)}, f32[256,256]{1,0:T(8,128)S(1)}) custom-call(s32[1]{0:T(128)} %bitcast.index_ref, f32[128,128]{1,0:T(8,128)S(1)} %get-tuple-element.31.sent_ref, f32[256,128]{1,0:T(8,128)S(1)} %get-tuple-element.25.k_ref, f32[256,256]{1,0:T(8,128)S(1)} %get-tuple-element.26.inv_ref, bf16[512,128]{1,0:T(8,128)(2,1)S(1)} %bitcast.20, ...), custom_call_target="tpu_custom_call" | custom-call | flops 500000000 | bytes 1000000 | tf_op jit(solution)/shard_map/pallas_call | solution.py:286
  36.8 0.0 collective-permute-done.2.third_ref
  36.8 0.4 shard_map.82
  37.2 20.5 %all-gather.3 = f32[512,256]{1,0:T(8,128)S(1)} all-gather(f32[128,256]{1,0:T(8,128)S(1)} %shard_map.82), channel_id=5, replica_groups={{0,16,32,48},{64,80,96,112},{128,144,160,176},{192,208,224,240},{256,27..., dimensions={0}, use_global_device_ids=true | all-gather | bytes 655360 | tf_op jit(solution)/shard_map/all_gather | solution.py:299
  57.7 1.3 %shard_map.84 = (f32[256,128]{1,0:T(8,128)S(1)}, f32[128,256]{1,0:T(8,128)S(1)}, f32[256,256]{1,0:T(8,128)S(1)}, f32[256,256]{1,0:T(8,128)S(1)}) custom-call(s32[1]{0:T(128)} %bitcast.index_ref, f32[2,128,640]{2,1,0:T(8,128)S(1)} %bitcast.14, f32[4,128,256]{2,1,0:T(8,128)S(1)} %bitcast.17, bf16[512,128]{1,0:T(8,128)(2,1)S(1)} %bitcast.21, ...), custom_call_target="tpu_custom_call" | custom-call | tf_op jit(solution)/shard_map/pallas_call | solution.py:286
  59.0 14.8 %all_to_all.10.got_ref = f32[16,16,128]{2,1,0:T(8,128)S(1)} all-to-all(f32[16,16,128]{2,1,0:T(8,128)S(1)} %bitcast.28), channel_id=1, replica_groups=mesh['seq'=32,'head'=16] {'head'}, dimensions={0} | all-to-all | bytes 262144 | tf_op jit(solution)/shard_map/all_to_all | solution.py:357
  73.8 0.8 shard_map.86
  74.6 3.5 %all-to-all-start.1 = ((f32[16,16,128]{2,1,0:T(8,128)}), f32[16,16,128]{2,1,0:T(8,128)S(1)}, u32[]{:S(2)}, u32[]{:S(2)}) async-start(f32[16,16,128]{2,1,0:T(8,128)} %shard_map.86), calls=%async_computation.1 | async-start | bytes 262144 | tf_op jit(solution)/shard_map/all_to_all | solution.py:366
  78.1 2.1 %shard_map.85 = (bf16[512,128]{1,0:T(8,128)(2,1)}, bf16[512,128]{1,0:T(8,128)(2,1)}, bf16[512,128]{1,0:T(8,128)(2,1)}) custom-call(s32[1]{0:T(128)} %bitcast.index_ref, bf16[512,128]{1,0:T(8,128)(2,1)S(1)} %bitcast.22, bf16[512,128]{1,0:T(8,128)(2,1)S(1)} %bitcast.26, f32[256,128]{1,0:T(8,128)S(1)} %get-tuple-element.25.k_ref, ...), custom_call_target="tpu_custom_call" | custom-call | flops 4000000000 | bytes 4000000 | tf_op jit(solution)/shard_map/pallas_call | solution.py:286
  80.2 5.8 %all-to-all-done.1 = f32[16,16,128]{2,1,0:T(8,128)S(1)} async-done(((f32[16,16,128]{2,1,0:T(8,128)}), f32[16,16,128]{2,1,0:T(8,128)S(1)}, u32[]{:S(2)}, u32[]{:S(2)}) %all-to-all-start.1) | async-done | bytes 131104 | tf_op jit(solution)/shard_map/all_to_all | solution.py:366
  86.1 0.6 shard_map.87
Async XLA Ops:
  0.6 0.8 copy-start.3
  1.5 2.3 %copy-start = (bf16[256,2,128]{2,1,0:T(2,128)(2,1)S(1)}, bf16[256,2,128]{2,1,0:T(2,128)(2,1)}, u32[]{:S(2)}) copy-start(bf16[256,2,128]{2,1,0:T(2,128)(2,1)} %param.4) | copy-start | bytes 393220
  1.5 2.3 %copy-start.1 = (bf16[256,2,128]{2,1,0:T(2,128)(2,1)S(1)}, bf16[256,2,128]{2,1,0:T(2,128)(2,1)}, u32[]{:S(2)}) copy-start(bf16[256,2,128]{2,1,0:T(2,128)(2,1)} %param.7) | copy-start | bytes 393220
  1.5 2.3 %copy-start.2 = (bf16[256,2,128]{2,1,0:T(2,128)(2,1)S(1)}, bf16[256,2,128]{2,1,0:T(2,128)(2,1)}, u32[]{:S(2)}) copy-start(bf16[256,2,128]{2,1,0:T(2,128)(2,1)} %param.6) | copy-start | bytes 393220
  24.4 9.4 %collective-permute-start = (f32[128,128]{1,0:T(8,128)S(1)}, f32[128,128]{1,0:T(8,128)S(1)}, u32[]{:S(2)}, u32[]{:S(2)}) collective-permute-start(f32[128,128]{1,0:T(8,128)S(1)} %get-tuple-element.31.sent_ref), channel_id=1, source_target_pairs={{0,128},{32,160},{64,192},{96,224},{496,368},{464,336},{432,304},{... | collective-permute-start | bytes 196616 | tf_op jit(solution)/shard_map/ppermute | solution.py:313
  34.0 0.7 collective-permute-start.1
  34.8 2.0 %collective-permute-start.2 = (f32[128,128]{1,0:T(8,128)S(1)}, f32[128,128]{1,0:T(8,128)S(1)}, u32[]{:S(2)}, u32[]{:S(2)}) collective-permute-start(f32[128,128]{1,0:T(8,128)S(1)} %shard_map.81), channel_id=1, source_target_pairs={{256,384},{288,416},{320,448},{352,480},{240,112},{208,80},{176,48... | collective-permute-start | bytes 196616 | tf_op jit(solution)/shard_map/ppermute | solution.py:313
  74.6 11.5 %all-to-all-start.1 = ((f32[16,16,128]{2,1,0:T(8,128)}), f32[16,16,128]{2,1,0:T(8,128)S(1)}, u32[]{:S(2)}, u32[]{:S(2)}) async-start(f32[16,16,128]{2,1,0:T(8,128)} %shard_map.86), calls=%async_computation.1 | async-start | bytes 262144 | tf_op jit(solution)/shard_map/all_to_all | solution.py:366
